TPU v7x, 128 devices: a whole 4x4x4 slice. The times are simulated.
128 devices in a mesh: gx: 8 (over z, core), gy: 16 (over y, x).
Axes of the slice: x: 4, y: 4, z: 4, core: 2. Of those that a mesh axis runs over, the one named last changes fastest.
Arguments:
- coeffs: bfloat16 [16, 128, 256, 128], P('gx', 'gy'), may hold values from -0.25 to 0.25
- permit: float32 [16, 128, 256], P('gx', 'gy'), may hold values from 0.25 to 4
- shift_diag: float32 [16, 128, 128], P('gx', 'gy'), may hold values from 0.5 to 4
- codes: int32 [16, 128, 6], P('gx', 'gy'), may hold values from 0 to 8
- counts: int32 [16, 128], P('gx', 'gy'), may hold values from 1 to 6
- weights: float32 [16, 128, 6], P('gx', 'gy'), may hold values from 0.5 to 1.5
- vectors: bfloat16 [16, 128, 128, 128], P('gx', 'gy'), may hold values from -6 to 6
Outputs:
- factor: bfloat16 [16, 128, 128, 128], P('gx', 'gy')
- applied: bfloat16 [16, 128, 128, 128], P('gx', 'gy')
All inputs are finite; a program needn't handle non-finite values.
Results may differ from a plain program's by a relative error of at most 0.0051.
Values may be sent and summed in bfloat16 or wider, within the bound.
No kernel may reach another device: no remote copies, remote signals or barrier semaphores. Data moves between devices by JAX's collectives and lax.ppermute only.
A program may use at most 64 MiB of HBM per device.

v0:
```python
import jax
import jax.numpy as jnp
from jax import lax
from jax.sharding import PartitionSpec as P


def extended(block, sides, width):
    for axis, dim in sides:
        count = lax.axis_size(axis)
        forward = [(i, i + 1) for i in range(count - 1)]
        backward = [(target, source) for source, target in forward]
        low = lax.ppermute(
            lax.slice_in_dim(block, block.shape[dim] - width, None, axis=dim), axis, forward
        )
        high = lax.ppermute(lax.slice_in_dim(block, 0, width, axis=dim), axis, backward)
        block = jnp.concatenate([low, block, high], axis=dim)
    return block


def from_behind(value, axis, by):
    length = lax.axis_size(axis)
    pairs = [(i, i + by) for i in range(length) if 0 <= i + by < length]
    return lax.ppermute(value, axis, pairs)


def local(coeffs, permit, shift_diag, codes, counts, weights, vectors):
    blocks_x = coeffs.shape[0]
    blocks_y = coeffs.shape[1]
    coupling = coeffs.shape[2]
    order = coeffs.shape[3]
    slots = codes.shape[2]
    padded = extended(coeffs, (("gx", 0), ("gy", 1)), 1)
    flattened = padded.reshape((blocks_x + 2) * (blocks_y + 2), coupling, order)
    row_index = jnp.arange(blocks_x, dtype=jnp.int32)[:, None]
    column_index = jnp.arange(blocks_y, dtype=jnp.int32)[None, :]
    active = jnp.arange(slots)[None, None, :] < counts[:, :, None]
    gram = jnp.zeros((blocks_x, blocks_y, order, order), jnp.float32)
    for slot_num in range(slots):
        slot_code = codes[:, :, slot_num]
        flat_index = (row_index + slot_code // 3) * (blocks_y + 2) + column_index + slot_code % 3
        neighbour = jnp.take(flattened, flat_index.reshape(-1), axis=0).reshape(
            blocks_x, blocks_y, coupling, order
        )
        scaled = (permit[:, :, :, None] * neighbour).astype(jnp.bfloat16)
        product = jnp.einsum(
            "xyrk,xyrl->xykl", scaled, neighbour, preferred_element_type=jnp.float32
        )
        gram = gram + jnp.where(active[:, :, slot_num, None, None], product, jnp.float32(0.0))
    system = gram + shift_diag[:, :, :, None] * jnp.eye(order, dtype=jnp.float32)
    cholesky_factor = jnp.linalg.cholesky(system)
    identity = jnp.broadcast_to(jnp.eye(order, dtype=system.dtype), system.shape)
    inverse = lax.linalg.triangular_solve(cholesky_factor, identity, left_side=True, lower=True)
    factor = inverse.astype(jnp.bfloat16)
    images = jnp.einsum("xykl,xykv->xylv", factor, vectors, preferred_element_type=jnp.float32)
    width_v = vectors.shape[3]
    weight_list = []
    for offset in range(9):
        weight_list.append(
            jnp.sum(jnp.where(active & (codes == offset), weights, jnp.float32(0.0)), axis=-1)
        )
    gathered_sum = jnp.zeros((blocks_x + 2, blocks_y + 2, order, width_v), jnp.float32)
    for offset in range(9):
        gathered_sum = gathered_sum.at[
            offset // 3 : offset // 3 + blocks_x, offset % 3 : offset % 3 + blocks_y
        ].add(weight_list[offset][:, :, None, None] * images)
    from_lower = from_behind(gathered_sum[-1], "gx", 1)
    from_upper = from_behind(gathered_sum[0].astype(jnp.bfloat16), "gx", -1).astype(jnp.float32)
    partial_value = gathered_sum[1:-1]
    partial_value = partial_value.at[0].add(from_lower)
    partial_value = partial_value.at[blocks_x - 1].add(from_upper)
    from_left = from_behind(partial_value[:, -1], "gy", 1)
    from_right = from_behind(partial_value[:, 0].astype(jnp.bfloat16), "gy", -1).astype(jnp.float32)
    central = partial_value[:, 1:-1]
    central = central.at[:, 0].add(from_left)
    central = central.at[:, blocks_y - 1].add(from_right)
    applied = central.astype(jnp.bfloat16)
    return (factor, applied)


def solution(mesh):
    placed = (
        P("gx", "gy", None, None),
        P("gx", "gy", None),
        P("gx", "gy", None),
        P("gx", "gy", None),
        P("gx", "gy"),
        P("gx", "gy", None),
        P("gx", "gy", None, None),
    )
    return jax.shard_map(
        local,
        mesh=mesh,
        in_specs=placed,
        out_specs=(P("gx", "gy", None, None), P("gx", "gy", None, None)),
        check_vma=False,
    )
```

profile of v0, /device:TPU:25, one launch (start us, length us, event | category | flops | bytes accessed | tf_op | source)
XLA Modules:
  0.0 466.1 jit_solution(227351254079101640)
XLA Ops:
  0.7 2.2 fusion.47
  2.9 4.1 collective-permute-start
  7.0 1.9 collective-permute-start.1
  22.8 3.1 collective-permute-start.2
  25.9 4.3 collective-permute-start.3
  34.7 2.0 pad_maximum_fusion
  36.8 1.8 gather_fusion
  38.6 2.4 broadcast_select_fusion.5
  40.9 2.3 copy.31
  45.0 2.4 broadcast_select_fusion.4
  47.3 2.3 copy.33
  49.6 1.9 gather_fusion.2
  51.5 2.5 broadcast_select_fusion.3
  53.9 2.3 copy.35
  56.2 1.9 gather_fusion.3
  58.1 2.5 broadcast_select_fusion.2
  60.6 2.3 copy.37
  62.8 1.8 gather_fusion.4
  64.6 2.4 broadcast_select_fusion.1
  67.0 2.3 copy.39
  69.2 1.8 gather_fusion.5
  71.0 2.5 broadcast_select_fusion
  73.5 2.4 copy.41
  86.8 188.3 %custom-call.7 = f32[2,8,128,128]{3,2,1,0:T(8,128)S(1)} custom-call(f32[2,8,128,128]{3,2,1,0:T(8,128)} %copy.45), custom_call_target="Cholesky" | custom-call | tf_op jit(solution)/shard_map/jit(cholesky)/cholesky | solution.py:50
  275.5 157.4 %custom-call.8 = f32[2,8,1,128,128]{3,4,2,1,0:T(8,128)S(1)} custom-call(f32[2,8,1,128,128]{4,3,2,1,0:T(8,128)S(1)} %select_bitcast_fusion), custom_call_target="InvertDiagBlocksLowerTriangular" | custom-call | tf_op jit(solution)/shard_map/triangular_solve | solution.py:52
  432.9 1.8 convolution_convert_fusion
  437.4 2.2 fusion.5
  441.4 5.4 %collective-permute-start.4 = (f32[10,128,128]{2,1,0:T(8,128)S(1)}, f32[10,128,128]{2,1,0:T(8,128)S(1)}, u32[]{:S(2)}, u32[]{:S(2)}) collective-permute-start(f32[10,128,128]{2,1,0:T(8,128)S(1)} %slice_bitcast_fusion), channel_id=1, source_target_pairs={{0,16},{16,32},{32,48},{48,64},{64,80},{80,96},{96,112},{1,17},{17... | collective-permute-start | bytes 1966088 | tf_op jit(solution)/shard_map/ppermute | solution.py:23
  446.8 1.9 collective-permute-start.5
  448.8 5.4 %collective-permute-done.4 = f32[10,128,128]{2,1,0:T(8,128)S(1)} collective-permute-done((f32[10,128,128]{2,1,0:T(8,128)S(1)}, f32[10,128,128]{2,1,0:T(8,128)S(1)}, u32[]{:S(2)}, u32[]{:S(2)}) %collective-permute-start.4) | collective-permute-done | bytes 655392 | tf_op jit(solution)/shard_map/ppermute | solution.py:23
  455.6 3.1 collective-permute-start.6
  458.7 5.2 %collective-permute-start.7 = (bf16[2,128,128]{2,1,0:T(8,128)(2,1)S(1)}, bf16[2,128,128]{2,1,0:T(8,128)(2,1)S(1)}, u32[]{:S(2)}, u32[]{:S(2)}) collective-permute-start(bf16[2,128,128]{2,1,0:T(8,128)(2,1)S(1)} %fusion.28), channel_id=1, source_target_pairs={{1,0},{2,1},{3,2},{4,3},{5,4},{6,5},{7,6},{8,7},{9,8},{10,9},{11,1... | collective-permute-start | bytes 196616 | tf_op jit(solution)/shard_map/ppermute | solution.py:23
  (166 shorter events, 39.2 us)
Async XLA Ops:
  0.6 434.2 %copy-start = (bf16[2,8,128,128]{3,2,1,0:T(8,128)(2,1)S(1)}, bf16[2,8,128,128]{3,2,1,0:T(8,128)(2,1)}, u32[]{:S(2)}) copy-start(bf16[2,8,128,128]{3,2,1,0:T(8,128)(2,1)} %param.41) | copy-start | bytes 1572868
  0.6 20.5 %copy-start.13 = (bf16[2,8,256,128]{3,2,1,0:T(8,128)(2,1)S(1)}, bf16[2,8,256,128]{3,2,1,0:T(8,128)(2,1)}, u32[]{:S(2)}) copy-start(bf16[2,8,256,128]{3,2,1,0:T(8,128)(2,1)} %param.35) | copy-start | bytes 3145732
  2.9 18.3 %collective-permute-start = (bf16[1,8,256,128]{3,2,1,0:T(8,128)(2,1)}, bf16[1,8,256,128]{3,2,1,0:T(8,128)(2,1)S(1)}, u32[]{:S(2)}, u32[]{:S(2)}) collective-permute-start(bf16[1,8,256,128]{3,2,1,0:T(8,128)(2,1)} %get-tuple-element.187), channel_id=1, source_target_pairs={{0,16},{16,32},{32,48},{48,64},{64,80},{80,96},{96,112},{1,17},{17... | collective-permute-start | bytes 1572872 | tf_op jit(solution)/shard_map/ppermute | solution.py:12
  7.0 14.4 %collective-permute-start.1 = (bf16[1,8,256,128]{3,2,1,0:T(8,128)(2,1)S(1)}, bf16[1,8,256,128]{3,2,1,0:T(8,128)(2,1)S(1)}, u32[]{:S(2)}, u32[]{:S(2)}) collective-permute-start(bf16[1,8,256,128]{3,2,1,0:T(8,128)(2,1)S(1)} %get-tuple-element.186), channel_id=1, source_target_pairs={{16,0},{32,16},{48,32},{64,48},{80,64},{96,80},{112,96},{17,1},{33... | collective-permute-start | bytes 1572872 | tf_op jit(solution)/shard_map/ppermute | solution.py:15
  21.2 10.6 %copy-start.18 = (pred[2,8,6]{1,0,2:T(4,128)(4,1)S(1)}, pred[2,8,6]{1,0,2:T(4,128)(4,1)}, u32[]{:S(2)}) copy-start(pred[2,8,6]{1,0,2:T(4,128)(4,1)} %iota_compare_fusion.3) | copy-start | bytes 292
  22.8 10.2 %collective-permute-start.2 = (bf16[4,1,256,128]{3,2,1,0:T(8,128)(2,1)S(1)}, bf16[4,1,256,128]{3,2,1,0:T(8,128)(2,1)S(1)}, u32[]{:S(2)}, u32[]{:S(2)}) collective-permute-start(bf16[4,1,256,128]{3,2,1,0:T(8,128)(2,1)S(1)} %get-tuple-element.184), channel_id=1, source_target_pairs={{0,1},{1,2},{2,3},{3,4},{4,5},{5,6},{6,7},{7,8},{8,9},{9,10},{10,1... | collective-permute-start | bytes 786440 | tf_op jit(solution)/shard_map/ppermute | solution.py:12
  25.9 8.8 %collective-permute-start.3 = (bf16[4,1,256,128]{3,2,1,0:T(8,128)(2,1)S(1)}, bf16[4,1,256,128]{3,2,1,0:T(8,128)(2,1)}, u32[]{:S(2)}, u32[]{:S(2)}) collective-permute-start(bf16[4,1,256,128]{3,2,1,0:T(8,128)(2,1)S(1)} %get-tuple-element.185), channel_id=1, source_target_pairs={{1,0},{2,1},{3,2},{4,3},{5,4},{6,5},{7,6},{8,7},{9,8},{10,9},{11,1... | collective-permute-start | bytes 786440 | tf_op jit(solution)/shard_map/ppermute | solution.py:15
  40.9 4.0 copy-start.32
  47.3 4.1 copy-start.31
  53.9 4.1 copy-start.30
  60.6 4.0 copy-start.29
  67.0 4.1 copy-start.28
  71.0 4.8 %copy-start.1 = (bf16[16,256,128]{2,1,0:T(8,128)(2,1)S(1)}, bf16[16,256,128]{2,1,0:T(8,128)(2,1)}, u32[]{:S(2)}) copy-start(bf16[16,256,128]{2,1,0:T(8,128)(2,1)} %broadcast_select_fusion.5) | copy-start | bytes 3145732
  71.0 4.8 %copy-start.15 = (f32[2,8,256]{2,1,0:T(8,128)S(1)}, f32[2,8,256]{2,1,0:T(8,128)}, u32[]{:S(2)}) copy-start(f32[2,8,256]{2,1,0:T(8,128)} %param.36) | copy-start | bytes 49156
  71.0 4.9 %copy-start.38 = (pred[2,8]{1,0:T(4,128)(4,1)S(1)}, pred[2,8]{1,0:T(4,128)(4,1)}, u32[]{:S(2)}) copy-start(pred[2,8]{1,0:T(4,128)(4,1)} %get-tuple-element.211) | copy-start | bytes 52
  73.5 4.2 copy-start.2
  73.5 4.2 copy-start.37
  75.9 1.8 copy-start.8
  78.2 1.8 copy-start.10
  78.2 1.8 copy-start.35
  80.4 1.7 copy-start.12
  80.4 1.7 copy-start.33
  82.1 1.8 copy-start.17
  83.9 191.2 %copy-start.16 = (pred[128,128]{1,0:T(8,128)(4,1)S(1)}, pred[128,128]{1,0:T(8,128)(4,1)}, u32[]{:S(2)}) copy-start(pred[128,128]{1,0:T(8,128)(4,1)} %iota_compare_fusion.1) | copy-start | bytes 49156
  86.8 348.0 %copy-start.27 = (f32[2,8]{1,0:T(2,128)S(1)}, f32[2,8]{1,0:T(2,128)}, u32[]{:S(2)}) copy-start(f32[2,8]{1,0:T(2,128)} %get-tuple-element.170) | copy-start | bytes 196
  435.2 2.2 copy-start.25
  435.8 3.8 copy-start.24
  437.3 2.5 copy-start.23
  441.4 12.9 %collective-permute-start.4 = (f32[10,128,128]{2,1,0:T(8,128)S(1)}, f32[10,128,128]{2,1,0:T(8,128)S(1)}, u32[]{:S(2)}, u32[]{:S(2)}) collective-permute-start(f32[10,128,128]{2,1,0:T(8,128)S(1)} %slice_bitcast_fusion), channel_id=1, source_target_pairs={{0,16},{16,32},{32,48},{48,64},{64,80},{80,96},{96,112},{1,17},{17... | collective-permute-start | bytes 1966088 | tf_op jit(solution)/shard_map/ppermute | solution.py:23
  446.8 8.4 %collective-permute-start.5 = (bf16[10,128,128]{2,1,0:T(8,128)(2,1)S(1)}, bf16[10,128,128]{2,1,0:T(8,128)(2,1)S(1)}, u32[]{:S(2)}, u32[]{:S(2)}) collective-permute-start(bf16[10,128,128]{2,1,0:T(8,128)(2,1)S(1)} %fusion.24), channel_id=1, source_target_pairs={{16,0},{32,16},{48,32},{64,48},{80,64},{96,80},{112,96},{17,1},{33... | collective-permute-start | bytes 983048 | tf_op jit(solution)/shard_map/ppermute | solution.py:23
  455.6 8.7 %collective-permute-start.6 = (f32[2,128,128]{2,1,0:T(8,128)S(1)}, f32[2,128,128]{2,1,0:T(8,128)S(1)}, u32[]{:S(2)}, u32[]{:S(2)}) collective-permute-start(f32[2,128,128]{2,1,0:T(8,128)S(1)} %slice_bitcast_fusion.1), channel_id=1, source_target_pairs={{0,1},{1,2},{2,3},{3,4},{4,5},{5,6},{6,7},{7,8},{8,9},{9,10},{10,1... | collective-permute-start | bytes 393224 | tf_op jit(solution)/shard_map/ppermute | solution.py:23
  458.7 6.5 %collective-permute-start.7 = (bf16[2,128,128]{2,1,0:T(8,128)(2,1)S(1)}, bf16[2,128,128]{2,1,0:T(8,128)(2,1)S(1)}, u32[]{:S(2)}, u32[]{:S(2)}) collective-permute-start(bf16[2,128,128]{2,1,0:T(8,128)(2,1)S(1)} %fusion.28), channel_id=1, source_target_pairs={{1,0},{2,1},{3,2},{4,3},{5,4},{6,5},{7,6},{8,7},{9,8},{10,9},{11,1... | collective-permute-start | bytes 196616 | tf_op jit(solution)/shard_map/ppermute | solution.py:23
  (15 other events, 17.1 us)
where the time goes:
time: 469 us; the launch traced here: 466 us
  other arithmetic  379 us (81%)
  local copies, waits for them, and re-layouts  40.4 us (9%)
  starting transfers between devices  29 us (6%)
  waiting for transfers between devices  9.98 us (2%)
  matrix products  6.07 us (1%)
    another operation x4, other arithmetic, local(): cholesky_factor = jnp.linalg.cholesky(system)  189 us
    another operation x3, other arithmetic, local(): lax.linalg.triangular_solve(cholesky_factor, identity, left_side=True, lo...  158 us
    ppermute x4, starting transfers between devices, from_behind(): return lax.ppermute(value, axis, pairs)  15.5 us
    select_n x6, other arithmetic, local(): jnp.take(flattened, flat_index.reshape(-1), axis=0)  14.5 us
    select_n x6, local copies, waits for them, and re-layouts, local(): jnp.take(flattened, flat_index.reshape(-1), axis=0)  13.7 us
    gather x6, local copies, waits for them, and re-layouts, local(): jnp.take(flattened, flat_index.reshape(-1), axis=0)  10.9 us
  transfers between devices with their start and end apart: 8, of which 6 were waited for; matrix products, arithmetic and copies ran while one was open for 3% of the time, Pallas kernels for 0%

commit v1 on v0

v1 whole, which is shorter than its diff:
```python
import jax
import jax.numpy as jnp
from jax import lax
from jax.experimental import pallas as pl
from jax.experimental.pallas import tpu as pltpu
from jax.sharding import PartitionSpec as P

PANEL = 8
GROUP = 4


def shift(value, by_x, by_y):
    nx, ny = lax.axis_size("gx"), lax.axis_size("gy")
    pairs = [
        (x * ny + y, (x + by_x) * ny + y + by_y)
        for x in range(nx)
        for y in range(ny)
        if 0 <= x + by_x < nx and 0 <= y + by_y < ny
    ]
    return lax.ppermute(value, ("gx", "gy"), pairs)


def lower_inverse(mat, xs, blocks, order):
    lane = lax.broadcasted_iota(jnp.int32, (PANEL, order), 1)
    sub = lax.broadcasted_iota(jnp.int32, (PANEL, order), 0)
    lane_full = lax.broadcasted_iota(jnp.int32, (order, order), 1)
    row_full = lax.broadcasted_iota(jnp.int32, (order, order), 0)

    def step(kb, carry):
        r0 = pl.multiple_of(kb * PANEL, PANEL)
        in_diag = (lane >= r0) & (lane < r0 + PANEL)
        unit = jnp.where(lane - r0 == sub, jnp.float32(1.0), jnp.float32(0.0))
        later = lane >= r0 + PANEL
        clear = (lane_full >= r0) & (lane_full < r0 + PANEL) & (row_full >= r0 + PANEL)
        for g in range(0, blocks, GROUP):
            ms = range(g, g + GROUP)
            rows = [mat[m, pl.ds(r0, PANEL), :] for m in ms]
            cols = []
            for r in rows:
                rolled = pltpu.roll(r, order - r0, axis=1)
                cols.append(
                    [jnp.broadcast_to(rolled[:, k : k + 1], (PANEL, order)) for k in range(PANEL)]
                )
            rows = [jnp.where(in_diag, unit, r) for r in rows]
            for k in range(PANEL):
                for n in range(GROUP):
                    c = cols[n]
                    inv = 1.0 / c[k][k : k + 1, :]
                    mult = jnp.where(sub > k, c[k] * inv, jnp.float32(0.0))
                    for j in range(k + 1, PANEL):
                        c[j] = c[j] - mult * c[j][k : k + 1, :]
                    rows[n] = rows[n] - mult * rows[n][k : k + 1, :]
            for n, m in enumerate(ms):
                diag = cols[n][0]
                for k in range(1, PANEL):
                    diag = jnp.where(sub == k, cols[n][k], diag)
                r = rows[n] * lax.rsqrt(diag)
                xs[m, pl.ds(r0, PANEL), :] = r
                hi = r.astype(jnp.bfloat16).astype(jnp.float32)
                rest = r - hi
                mid = rest.astype(jnp.bfloat16).astype(jnp.float32)
                low = rest - mid
                zero = jnp.float32(0.0)
                hi_l = jnp.where(later, hi, zero)
                mid_l = jnp.where(later, mid, zero)
                low_l = jnp.where(later, low, zero)
                right = jnp.concatenate([hi, mid, hi, low, hi, mid], axis=0).astype(jnp.bfloat16)
                left = jnp.concatenate([hi_l, hi_l, mid_l, hi_l, low_l, mid_l], axis=0)
                left = left.T.astype(jnp.bfloat16)
                update = jnp.dot(left, right, preferred_element_type=jnp.float32)
                mat[m] = jnp.where(clear, zero, mat[m]) - update
        return carry

    lax.fori_loop(0, order // PANEL, step, 0)


def blocks_kernel(
    codes, counts, weights, permit, diag, own, low, high, left, right, vectors,
    factor, center, to_low, to_high, to_left, to_right,
    turned, mat, xs, acc,
):
    bx, by = own.shape[0], own.shape[1]
    order = own.shape[3]
    wide = by + 2
    blocks = bx * by
    slots = codes.shape[1]
    for x in range(bx):
        for y in range(by):
            turned[(x + 1) * wide + y + 1] = own[x, y].T
    for y in range(by):
        turned[y + 1] = low[y].T
        turned[(bx + 1) * wide + y + 1] = high[y].T
    for x in range(bx + 2):
        turned[x * wide] = left[x].T
        turned[x * wide + by + 1] = right[x].T

    row_full = lax.broadcasted_iota(jnp.int32, (order, order), 0)
    lane_full = lax.broadcasted_iota(jnp.int32, (order, order), 1)

    def target(i, s):
        code = codes[i, s]
        return (i // by + code // 3) * wide + i % by + code % 3

    def gram(i, carry):
        total = jnp.zeros((order, order), jnp.float32)
        scale = permit[pl.ds(i, 1), :]
        for s in range(slots):
            block = turned[target(i, s)]
            on = jnp.where(s < counts[0, i], jnp.float32(1.0), jnp.float32(0.0))
            scaled = ((scale * on) * block.astype(jnp.float32)).astype(jnp.bfloat16)
            total = total + lax.dot_general(
                scaled, block, (((1,), (1,)), ((), ())), preferred_element_type=jnp.float32
            )
        total = (total + total.T) * jnp.float32(0.5)
        mat[i] = total + jnp.where(row_full == lane_full, diag[pl.ds(i, 1), :], jnp.float32(0.0))
        return carry

    lax.fori_loop(0, blocks, gram, 0)
    lower_inverse(mat, xs, blocks, order)
    acc[...] = jnp.zeros(acc.shape, acc.dtype)

    def apply(i, carry):
        f = jnp.where(lane_full <= row_full, xs[i], jnp.float32(0.0))
        factor[i] = f.astype(jnp.bfloat16)
        image = jnp.dot(f.T.astype(jnp.bfloat16), vectors[i], preferred_element_type=jnp.float32)

        def add(s, c):
            n = target(i, s)
            acc[n] = acc[n] + weights[i, s] * image
            return c

        return lax.fori_loop(0, counts[0, i], add, carry)

    lax.fori_loop(0, blocks, apply, 0)
    for x in range(bx):
        center[x] = acc[pl.ds((x + 1) * wide + 1, by)]
    to_low[...] = acc[pl.ds(1, by)].astype(jnp.bfloat16)
    to_high[...] = acc[pl.ds((bx + 1) * wide + 1, by)].astype(jnp.bfloat16)
    for x in range(bx + 2):
        to_left[x] = acc[x * wide].astype(jnp.bfloat16)
        to_right[x] = acc[x * wide + by + 1].astype(jnp.bfloat16)


def add_kernel(center, low, high, left, right, c00, c02, c20, c22, out):
    bx, by = center.shape[0], center.shape[1]
    f32 = jnp.float32
    for x in range(bx):
        for y in range(by):
            v = center[x, y]
            if x == 0:
                v = v + low[y].astype(f32)
            if x == bx - 1:
                v = v + high[y].astype(f32)
            if y == 0:
                v = v + left[x].astype(f32)
            if y == by - 1:
                v = v + right[x].astype(f32)
            if x == 0 and y == 0:
                v = v + c00[...].astype(f32)
            if x == 0 and y == by - 1:
                v = v + c02[...].astype(f32)
            if x == bx - 1 and y == 0:
                v = v + c20[...].astype(f32)
            if x == bx - 1 and y == by - 1:
                v = v + c22[...].astype(f32)
            out[x, y] = v.astype(out.dtype)


def local_blocks(codes, counts, weights, permit, diag, own, low, high, left, right, vectors):
    bx, by, coupling, order = own.shape
    width = vectors.shape[3]
    blocks = bx * by
    slots = codes.shape[2]
    padded = (bx + 2) * (by + 2)
    smem = pl.BlockSpec(memory_space=pltpu.SMEM)
    vmem = pl.BlockSpec(memory_space=pltpu.VMEM)
    bf16, f32 = jnp.bfloat16, jnp.float32
    return pl.pallas_call(
        blocks_kernel,
        out_shape=(
            jax.ShapeDtypeStruct((blocks, order, order), bf16),
            jax.ShapeDtypeStruct((bx, by, order, width), f32),
            jax.ShapeDtypeStruct((by, order, width), bf16),
            jax.ShapeDtypeStruct((by, order, width), bf16),
            jax.ShapeDtypeStruct((bx + 2, order, width), bf16),
            jax.ShapeDtypeStruct((bx + 2, order, width), bf16),
        ),
        in_specs=[smem] * 3 + [vmem] * 8,
        out_specs=(vmem,) * 6,
        scratch_shapes=[
            pltpu.VMEM((padded, order, coupling), bf16),
            pltpu.VMEM((blocks, order, order), f32),
            pltpu.VMEM((blocks, order, order), f32),
            pltpu.VMEM((padded, order, width), f32),
        ],
        compiler_params=pltpu.CompilerParams(vmem_limit_bytes=40 * 1024 * 1024),
        name="blocks",
    )(
        codes.reshape(blocks, slots), counts.reshape(1, blocks), weights.reshape(blocks, slots),
        permit.reshape(blocks, coupling), diag.reshape(blocks, order),
        own, low, high, left, right, vectors.reshape(blocks, order, width),
    )


def local(coeffs, permit, shift_diag, codes, counts, weights, vectors):
    bx, by, coupling, order = coeffs.shape
    low = shift(coeffs[bx - 1], 1, 0)
    high = shift(coeffs[0], -1, 0)
    left_send = jnp.concatenate([low[None, by - 1], coeffs[:, by - 1], high[None, by - 1]], axis=0)
    right_send = jnp.concatenate([low[None, 0], coeffs[:, 0], high[None, 0]], axis=0)
    left = shift(left_send, 0, 1)
    right = shift(right_send, 0, -1)
    factor, center, to_low, to_high, to_left, to_right = local_blocks(
        codes, counts, weights, permit, shift_diag, coeffs, low, high, left, right, vectors
    )
    from_low = shift(to_high, 1, 0)
    from_high = shift(to_low, -1, 0)
    from_left = shift(to_right[1 : bx + 1], 0, 1)
    from_right = shift(to_left[1 : bx + 1], 0, -1)
    c00 = shift(to_right[bx + 1], 1, 1)
    c02 = shift(to_left[bx + 1], 1, -1)
    c20 = shift(to_right[0], -1, 1)
    c22 = shift(to_left[0], -1, -1)
    vmem = pl.BlockSpec(memory_space=pltpu.VMEM)
    applied = pl.pallas_call(
        add_kernel,
        out_shape=jax.ShapeDtypeStruct(center.shape, jnp.bfloat16),
        in_specs=[vmem] * 9,
        out_specs=vmem,
        compiler_params=pltpu.CompilerParams(vmem_limit_bytes=16 * 1024 * 1024),
        name="collect",
    )(center, from_low, from_high, from_left, from_right, c00, c02, c20, c22)
    return factor.reshape(bx, by, order, order), applied


def solution(mesh):
    placed = (
        P("gx", "gy", None, None),
        P("gx", "gy", None),
        P("gx", "gy", None),
        P("gx", "gy", None),
        P("gx", "gy"),
        P("gx", "gy", None),
        P("gx", "gy", None, None),
    )
    return jax.shard_map(
        local,
        mesh=mesh,
        in_specs=placed,
        out_specs=(P("gx", "gy", None, None), P("gx", "gy", None, None)),
        check_vma=False,
    )
```

time: 469 us -> 109 us (0.23)
  other arithmetic: 379 us -> 0.77 us
  Pallas kernels: 0 us -> 48.8 us
  local copies, waits for them, and re-layouts: 40.4 us -> 1.71 us
  starting transfers between devices: 29 us -> 44.6 us
  matrix products: 6.07 us -> 0 us
    another operation x9 -> x0, other arithmetic: 348 us -> none  [the longest x4 189 us: local(): cholesky_factor = jnp.linalg.cholesky(system)]
    pallas_call x0 -> x2, Pallas kernels: none -> 48.8 us  [the longest x1 47.8 us: local_blocks(): pl.pallas_call(blocks_kernel, out_shape=(jax.ShapeDtypeStruct((blocks, or...]
    ppermute x8 -> x12, starting transfers between devices: 29 us -> 44.6 us  [shift(): return lax.ppermute(value, ('gx', 'gy'), pairs)]
    select_n x6 -> x0, other arithmetic: 14.5 us -> none  [local(): jnp.take(flattened, flat_index.reshape(-1), axis=0)]
    select_n x6 -> x0, local copies, waits for them, and re-layouts: 13.7 us -> none  [local(): jnp.take(flattened, flat_index.reshape(-1), axis=0)]
    gather x6 -> x0, local copies, waits for them, and re-layouts: 10.9 us -> none  [local(): jnp.take(flattened, flat_index.reshape(-1), axis=0)]
    unnamed x82 -> x14, local copies, waits for them, and re-layouts: 5.87 us -> 0.04 us
    scatter-add x12 -> x0, other arithmetic: 5.17 us -> none  [the longest x8 4.91 us: local(): gathered_sum = gathered_sum.at[offset // 3:offset // 3 + blocks_x, offset...]
  transfers between devices with their start and end apart: 8 -> 12, of which waited for: 6 -> 5; matrix products, arithmetic and copies ran while one was open for 3% -> 1% of each run, Pallas kernels for 0% -> 0%
where the time goes in v1:
time: 109 us; the launch traced here: 107 us
  Pallas kernels  48.8 us (45%)
  starting transfers between devices  44.6 us (41%)
  waiting for transfers between devices  10.4 us (10%)
  local copies, waits for them, and re-layouts  1.71 us (2%)
    pallas_call x1, Pallas kernels, local_blocks(): pl.pallas_call(blocks_kernel, out_shape=(jax.ShapeDtypeStruct((blocks, or...  47.8 us
    ppermute x12, starting transfers between devices, shift(): return lax.ppermute(value, ('gx', 'gy'), pairs)  44.6 us
    ppermute x12, waiting for transfers between devices, shift(): return lax.ppermute(value, ('gx', 'gy'), pairs)  10.4 us
  transfers between devices with their start and end apart: 12, of which 5 were waited for; matrix products, arithmetic and copies ran while one was open for 1% of the time, Pallas kernels for 0%

profile of v1, /device:TPU:25, one launch (start us, length us, event | category | flops | bytes accessed | tf_op | source)
XLA Modules:
  0.0 107.2 jit_solution(13172545674554683374)
XLA Ops:
  0.6 1.4 %slice_bitcast_fusion = (bf16[8,256,128]{2,1,0:T(8,128)(2,1)S(1)}, bf16[8,256,128]{2,1,0:T(8,128)(2,1)S(1)}) fusion(bf16[2,8,256,128]{3,2,1,0:T(8,128)(2,1)} %own.1), kind=kLoop, calls=%fused_computation | loop fusion | bytes 2097152 | tf_op jit(solution)/shard_map/squeeze | solution.py:208
  2.0 2.6 %collective-permute-start.1 = (bf16[8,256,128]{2,1,0:T(8,128)(2,1)S(1)}, bf16[8,256,128]{2,1,0:T(8,128)(2,1)S(1)}, u32[]{:S(2)}, u32[]{:S(2)}) collective-permute-start(bf16[8,256,128]{2,1,0:T(8,128)(2,1)S(1)} %get-tuple-element.16), channel_id=1, source_target_pairs={{16,0},{17,1},{18,2},{19,3},{20,4},{21,5},{22,6},{23,7},{24,8},{25... | collective-permute-start | bytes 1572872 | tf_op jit(solution)/shard_map/ppermute | solution.py:20
  4.6 3.4 %collective-permute-start = (bf16[8,256,128]{2,1,0:T(8,128)(2,1)S(1)}, bf16[8,256,128]{2,1,0:T(8,128)(2,1)S(1)}, u32[]{:S(2)}, u32[]{:S(2)}) collective-permute-start(bf16[8,256,128]{2,1,0:T(8,128)(2,1)S(1)} %get-tuple-element.17), channel_id=1, source_target_pairs={{0,16},{1,17},{2,18},{3,19},{4,20},{5,21},{6,22},{7,23},{8,24},{9,... | collective-permute-start | bytes 1572872 | tf_op jit(solution)/shard_map/ppermute | solution.py:20
  8.1 4.9 %collective-permute-done.1.high = bf16[8,256,128]{2,1,0:T(8,128)(2,1)S(1)} collective-permute-done((bf16[8,256,128]{2,1,0:T(8,128)(2,1)S(1)}, bf16[8,256,128]{2,1,0:T(8,128)(2,1)S(1)}, u32[]{:S(2)}, u32[]{:S(2)}) %collective-permute-start.1) | collective-permute-done | bytes 524320 | tf_op jit(solution)/shard_map/ppermute | solution.py:20
  13.0 1.2 %collective-permute-done.low = bf16[8,256,128]{2,1,0:T(8,128)(2,1)S(1)} collective-permute-done((bf16[8,256,128]{2,1,0:T(8,128)(2,1)S(1)}, bf16[8,256,128]{2,1,0:T(8,128)(2,1)S(1)}, u32[]{:S(2)}, u32[]{:S(2)}) %collective-permute-start) | collective-permute-done | bytes 524320 | tf_op jit(solution)/shard_map/ppermute | solution.py:20
  14.2 0.0 copy-start.1
  14.2 3.3 %collective-permute-start.2 = (bf16[4,256,128]{2,1,0:T(8,128)(2,1)S(1)}, bf16[4,256,128]{2,1,0:T(8,128)(2,1)S(1)}, u32[]{:S(2)}, u32[]{:S(2)}) collective-permute-start(bf16[4,256,128]{2,1,0:T(8,128)(2,1)S(1)} %pad_maximum_fusion), channel_id=1, source_target_pairs={{0,1},{1,2},{2,3},{3,4},{4,5},{5,6},{6,7},{7,8},{8,9},{9,10},{10,1... | collective-permute-start | bytes 786440 | tf_op jit(solution)/shard_map/ppermute | solution.py:20
  17.5 0.0 copy-start.6
  17.5 0.0 copy-start.4
  17.5 0.0 copy-start.5
  17.5 0.7 pad_maximum_fusion.1
  18.2 4.3 %collective-permute-start.3 = (bf16[4,256,128]{2,1,0:T(8,128)(2,1)}, bf16[4,256,128]{2,1,0:T(8,128)(2,1)S(1)}, u32[]{:S(2)}, u32[]{:S(2)}) collective-permute-start(bf16[4,256,128]{2,1,0:T(8,128)(2,1)} %pad_maximum_fusion.1), channel_id=1, source_target_pairs={{1,0},{2,1},{3,2},{4,3},{5,4},{6,5},{7,6},{8,7},{9,8},{10,9},{11,1... | collective-permute-start | bytes 786440 | tf_op jit(solution)/shard_map/ppermute | solution.py:20
  22.5 0.1 reshape.26.counts
  22.6 0.1 copy.13
  22.7 0.1 copy.14
  22.8 0.8 collective-permute-done.2.left
  23.6 2.6 %collective-permute-done.3.right = bf16[4,256,128]{2,1,0:T(8,128)(2,1)S(1)} collective-permute-done((bf16[4,256,128]{2,1,0:T(8,128)(2,1)}, bf16[4,256,128]{2,1,0:T(8,128)(2,1)S(1)}, u32[]{:S(2)}, u32[]{:S(2)}) %collective-permute-start.3) | collective-permute-done | bytes 262176 | tf_op jit(solution)/shard_map/ppermute | solution.py:20
  26.1 47.8 %blocks.1 = (bf16[16,128,128]{2,1,0:T(8,128)(2,1)}, f32[2,8,128,128]{3,2,1,0:T(8,128)S(1)}, bf16[8,128,128]{2,1,0:T(8,128)(2,1)S(1)}, bf16[8,128,128]{2,1,0:T(8,...) custom-call(s32[16,6]{1,0:T(8,128)S(1)} %bitcast.27, s32[1,16]{1,0:T(1,128)S(1)} %reshape.26.counts, ...), custom_call_target="tpu_custom_call" | custom-call | tf_op jit(solution)/shard_map/blocks/pallas_call | solution.py:178
  74.0 1.9 %collective-permute-start.10 = (bf16[128,128]{1,0:T(8,128)(2,1)S(1)}, bf16[128,128]{1,0:T(8,128)(2,1)S(1)}, u32[]{:S(2)}, u32[]{:S(2)}) collective-permute-start(bf16[128,128]{1,0:T(8,128)(2,1)S(1)} %get-tuple-element.24), channel_id=1, source_target_pairs={{16,1},{17,2},{18,3},{19,4},{20,5},{21,6},{22,7},{23,8},{24,9},{25... | collective-permute-start | bytes 98312 | tf_op jit(solution)/shard_map/ppermute | solution.py:20
  75.9 7.2 %collective-permute-start.8 = (bf16[128,128]{1,0:T(8,128)(2,1)S(1)}, bf16[128,128]{1,0:T(8,128)(2,1)S(1)}, u32[]{:S(2)}, u32[]{:S(2)}) collective-permute-start(bf16[128,128]{1,0:T(8,128)(2,1)S(1)} %get-tuple-element.25), channel_id=1, source_target_pairs={{0,17},{1,18},{2,19},{3,20},{4,21},{5,22},{6,23},{7,24},{8,25},{9,... | collective-permute-start | bytes 98312 | tf_op jit(solution)/shard_map/ppermute | solution.py:20
  83.2 3.3 %collective-permute-start.4 = (bf16[8,128,128]{2,1,0:T(8,128)(2,1)S(1)}, bf16[8,128,128]{2,1,0:T(8,128)(2,1)S(1)}, u32[]{:S(2)}, u32[]{:S(2)}) collective-permute-start(bf16[8,128,128]{2,1,0:T(8,128)(2,1)S(1)} %get-tuple-element.10), channel_id=1, source_target_pairs={{0,16},{1,17},{2,18},{3,19},{4,20},{5,21},{6,22},{7,23},{8,24},{9,... | collective-permute-start | bytes 786440 | tf_op jit(solution)/shard_map/ppermute | solution.py:20
  86.5 1.9 %collective-permute-start.5 = (bf16[8,128,128]{2,1,0:T(8,128)(2,1)S(1)}, bf16[8,128,128]{2,1,0:T(8,128)(2,1)S(1)}, u32[]{:S(2)}, u32[]{:S(2)}) collective-permute-start(bf16[8,128,128]{2,1,0:T(8,128)(2,1)S(1)} %get-tuple-element.11), channel_id=1, source_target_pairs={{16,0},{17,1},{18,2},{19,3},{20,4},{21,5},{22,6},{23,7},{24,8},{25... | collective-permute-start | bytes 786440 | tf_op jit(solution)/shard_map/ppermute | solution.py:20
  88.5 3.0 %collective-permute-start.11 = (bf16[128,128]{1,0:T(8,128)(2,1)S(1)}, bf16[128,128]{1,0:T(8,128)(2,1)S(1)}, u32[]{:S(2)}, u32[]{:S(2)}) collective-permute-start(bf16[128,128]{1,0:T(8,128)(2,1)S(1)} %get-tuple-element.22), channel_id=1, source_target_pairs={{17,0},{18,1},{19,2},{20,3},{21,4},{22,5},{23,6},{24,7},{25,8},{26... | collective-permute-start | bytes 98312 | tf_op jit(solution)/shard_map/ppermute | solution.py:20
  91.5 0.0 collective-permute-done.10.c20
  91.5 3.8 %collective-permute-start.7 = (bf16[2,128,128]{2,1,0:T(8,128)(2,1)S(1)}, bf16[2,128,128]{2,1,0:T(8,128)(2,1)S(1)}, u32[]{:S(2)}, u32[]{:S(2)}) collective-permute-start(bf16[2,128,128]{2,1,0:T(8,128)(2,1)S(1)} %slice.51), channel_id=1, source_target_pairs={{1,0},{2,1},{3,2},{4,3},{5,4},{6,5},{7,6},{8,7},{9,8},{10,9},{11,1... | collective-permute-start | bytes 196616 | tf_op jit(solution)/shard_map/ppermute | solution.py:20
  95.3 0.0 collective-permute-done.8.c00
  95.3 1.9 %collective-permute-start.6 = (bf16[2,128,128]{2,1,0:T(8,128)(2,1)S(1)}, bf16[2,128,128]{2,1,0:T(8,128)(2,1)S(1)}, u32[]{:S(2)}, u32[]{:S(2)}) collective-permute-start(bf16[2,128,128]{2,1,0:T(8,128)(2,1)S(1)} %slice.50), channel_id=1, source_target_pairs={{0,1},{1,2},{2,3},{3,4},{4,5},{5,6},{6,7},{7,8},{8,9},{9,10},{10,1... | collective-permute-start | bytes 196616 | tf_op jit(solution)/shard_map/ppermute | solution.py:20
  97.3 7.9 %collective-permute-start.9 = (bf16[128,128]{1,0:T(8,128)(2,1)S(1)}, bf16[128,128]{1,0:T(8,128)(2,1)S(1)}, u32[]{:S(2)}, u32[]{:S(2)}) collective-permute-start(bf16[128,128]{1,0:T(8,128)(2,1)S(1)} %get-tuple-element.23), channel_id=1, source_target_pairs={{1,16},{2,17},{3,18},{4,19},{5,20},{6,21},{7,22},{8,23},{9,24},{10... | collective-permute-start | bytes 98312 | tf_op jit(solution)/shard_map/ppermute | solution.py:20
  105.2 1.0 collective-permute-done.9.c02
  106.2 0.0 collective-permute-done.4.low
  106.2 0.0 collective-permute-done.5.high
  106.2 0.9 collect.1
  (21 shorter events, 0.1 us)
Async XLA Ops:
  0.6 7.4 %copy-start = (bf16[2,8,256,128]{3,2,1,0:T(8,128)(2,1)S(1)}, bf16[2,8,256,128]{3,2,1,0:T(8,128)(2,1)}, u32[]{:S(2)}) copy-start(bf16[2,8,256,128]{3,2,1,0:T(8,128)(2,1)} %own.1) | copy-start | bytes 3145732
  2.0 11.0 %collective-permute-start.1 = (bf16[8,256,128]{2,1,0:T(8,128)(2,1)S(1)}, bf16[8,256,128]{2,1,0:T(8,128)(2,1)S(1)}, u32[]{:S(2)}, u32[]{:S(2)}) collective-permute-start(bf16[8,256,128]{2,1,0:T(8,128)(2,1)S(1)} %get-tuple-element.16), channel_id=1, source_target_pairs={{16,0},{17,1},{18,2},{19,3},{20,4},{21,5},{22,6},{23,7},{24,8},{25... | collective-permute-start | bytes 1572872 | tf_op jit(solution)/shard_map/ppermute | solution.py:20
  4.6 9.6 %collective-permute-start = (bf16[8,256,128]{2,1,0:T(8,128)(2,1)S(1)}, bf16[8,256,128]{2,1,0:T(8,128)(2,1)S(1)}, u32[]{:S(2)}, u32[]{:S(2)}) collective-permute-start(bf16[8,256,128]{2,1,0:T(8,128)(2,1)S(1)} %get-tuple-element.17), channel_id=1, source_target_pairs={{0,16},{1,17},{2,18},{3,19},{4,20},{5,21},{6,22},{7,23},{8,24},{9,... | collective-permute-start | bytes 1572872 | tf_op jit(solution)/shard_map/ppermute | solution.py:20
  14.2 12.0 %copy-start.1 = (bf16[2,8,128,128]{3,2,1,0:T(8,128)(2,1)S(1)}, bf16[2,8,128,128]{3,2,1,0:T(8,128)(2,1)}, u32[]{:S(2)}) copy-start(bf16[2,8,128,128]{3,2,1,0:T(8,128)(2,1)} %param.13) | copy-start | bytes 1572868
  14.2 9.4 %collective-permute-start.2 = (bf16[4,256,128]{2,1,0:T(8,128)(2,1)S(1)}, bf16[4,256,128]{2,1,0:T(8,128)(2,1)S(1)}, u32[]{:S(2)}, u32[]{:S(2)}) collective-permute-start(bf16[4,256,128]{2,1,0:T(8,128)(2,1)S(1)} %pad_maximum_fusion), channel_id=1, source_target_pairs={{0,1},{1,2},{2,3},{3,4},{4,5},{5,6},{6,7},{7,8},{8,9},{9,10},{10,1... | collective-permute-start | bytes 786440 | tf_op jit(solution)/shard_map/ppermute | solution.py:20
  17.5 5.0 %copy-start.6 = (s32[2,8]{1,0:T(2,128)S(1)}, s32[2,8]{1,0:T(2,128)}, u32[]{:S(2)}) copy-start(s32[2,8]{1,0:T(2,128)} %param.11) | copy-start | bytes 196
  17.5 5.1 %copy-start.4 = (s32[2,8,6]{1,0,2:T(2,128)S(1)}, s32[2,8,6]{1,0,2:T(2,128)}, u32[]{:S(2)}) copy-start(s32[2,8,6]{1,0,2:T(2,128)} %param.10) | copy-start | bytes 1156
  17.5 5.2 %copy-start.5 = (f32[2,8,6]{1,0,2:T(2,128)S(1)}, f32[2,8,6]{1,0,2:T(2,128)}, u32[]{:S(2)}) copy-start(f32[2,8,6]{1,0,2:T(2,128)} %param.12) | copy-start | bytes 1156
  18.2 7.9 %collective-permute-start.3 = (bf16[4,256,128]{2,1,0:T(8,128)(2,1)}, bf16[4,256,128]{2,1,0:T(8,128)(2,1)S(1)}, u32[]{:S(2)}, u32[]{:S(2)}) collective-permute-start(bf16[4,256,128]{2,1,0:T(8,128)(2,1)} %pad_maximum_fusion.1), channel_id=1, source_target_pairs={{1,0},{2,1},{3,2},{4,3},{5,4},{6,5},{7,6},{8,7},{9,8},{10,9},{11,1... | collective-permute-start | bytes 786440 | tf_op jit(solution)/shard_map/ppermute | solution.py:20
  22.6 3.5 %copy-start.2 = (f32[2,8,256]{2,1,0:T(8,128)S(1)}, f32[2,8,256]{2,1,0:T(8,128)}, u32[]{:S(2)}) copy-start(f32[2,8,256]{2,1,0:T(8,128)} %param.8) | copy-start | bytes 49156
  22.8 3.3 %copy-start.3 = (f32[2,8,128]{2,1,0:T(8,128)S(1)}, f32[2,8,128]{2,1,0:T(8,128)}, u32[]{:S(2)}) copy-start(f32[2,8,128]{2,1,0:T(8,128)} %param.9) | copy-start | bytes 24580
  74.0 17.5 %collective-permute-start.10 = (bf16[128,128]{1,0:T(8,128)(2,1)S(1)}, bf16[128,128]{1,0:T(8,128)(2,1)S(1)}, u32[]{:S(2)}, u32[]{:S(2)}) collective-permute-start(bf16[128,128]{1,0:T(8,128)(2,1)S(1)} %get-tuple-element.24), channel_id=1, source_target_pairs={{16,1},{17,2},{18,3},{19,4},{20,5},{21,6},{22,7},{23,8},{24,9},{25... | collective-permute-start | bytes 98312 | tf_op jit(solution)/shard_map/ppermute | solution.py:20
  75.9 19.4 %collective-permute-start.8 = (bf16[128,128]{1,0:T(8,128)(2,1)S(1)}, bf16[128,128]{1,0:T(8,128)(2,1)S(1)}, u32[]{:S(2)}, u32[]{:S(2)}) collective-permute-start(bf16[128,128]{1,0:T(8,128)(2,1)S(1)} %get-tuple-element.25), channel_id=1, source_target_pairs={{0,17},{1,18},{2,19},{3,20},{4,21},{5,22},{6,23},{7,24},{8,25},{9,... | collective-permute-start | bytes 98312 | tf_op jit(solution)/shard_map/ppermute | solution.py:20
  83.2 23.1 %collective-permute-start.4 = (bf16[8,128,128]{2,1,0:T(8,128)(2,1)S(1)}, bf16[8,128,128]{2,1,0:T(8,128)(2,1)S(1)}, u32[]{:S(2)}, u32[]{:S(2)}) collective-permute-start(bf16[8,128,128]{2,1,0:T(8,128)(2,1)S(1)} %get-tuple-element.10), channel_id=1, source_target_pairs={{0,16},{1,17},{2,18},{3,19},{4,20},{5,21},{6,22},{7,23},{8,24},{9,... | collective-permute-start | bytes 786440 | tf_op jit(solution)/shard_map/ppermute | solution.py:20
  86.5 19.7 %collective-permute-start.5 = (bf16[8,128,128]{2,1,0:T(8,128)(2,1)S(1)}, bf16[8,128,128]{2,1,0:T(8,128)(2,1)S(1)}, u32[]{:S(2)}, u32[]{:S(2)}) collective-permute-start(bf16[8,128,128]{2,1,0:T(8,128)(2,1)S(1)} %get-tuple-element.11), channel_id=1, source_target_pairs={{16,0},{17,1},{18,2},{19,3},{20,4},{21,5},{22,6},{23,7},{24,8},{25... | collective-permute-start | bytes 786440 | tf_op jit(solution)/shard_map/ppermute | solution.py:20
  88.5 8.8 %collective-permute-start.11 = (bf16[128,128]{1,0:T(8,128)(2,1)S(1)}, bf16[128,128]{1,0:T(8,128)(2,1)S(1)}, u32[]{:S(2)}, u32[]{:S(2)}) collective-permute-start(bf16[128,128]{1,0:T(8,128)(2,1)S(1)} %get-tuple-element.22), channel_id=1, source_target_pairs={{17,0},{18,1},{19,2},{20,3},{21,4},{22,5},{23,6},{24,7},{25,8},{26... | collective-permute-start | bytes 98312 | tf_op jit(solution)/shard_map/ppermute | solution.py:20
  91.5 14.8 %collective-permute-start.7 = (bf16[2,128,128]{2,1,0:T(8,128)(2,1)S(1)}, bf16[2,128,128]{2,1,0:T(8,128)(2,1)S(1)}, u32[]{:S(2)}, u32[]{:S(2)}) collective-permute-start(bf16[2,128,128]{2,1,0:T(8,128)(2,1)S(1)} %slice.51), channel_id=1, source_target_pairs={{1,0},{2,1},{3,2},{4,3},{5,4},{6,5},{7,6},{8,7},{9,8},{10,9},{11,1... | collective-permute-start | bytes 196616 | tf_op jit(solution)/shard_map/ppermute | solution.py:20
  95.3 10.9 %collective-permute-start.6 = (bf16[2,128,128]{2,1,0:T(8,128)(2,1)S(1)}, bf16[2,128,128]{2,1,0:T(8,128)(2,1)S(1)}, u32[]{:S(2)}, u32[]{:S(2)}) collective-permute-start(bf16[2,128,128]{2,1,0:T(8,128)(2,1)S(1)} %slice.50), channel_id=1, source_target_pairs={{0,1},{1,2},{2,3},{3,4},{4,5},{5,6},{6,7},{7,8},{8,9},{9,10},{10,1... | collective-permute-start | bytes 196616 | tf_op jit(solution)/shard_map/ppermute | solution.py:20
  97.3 9.0 %collective-permute-start.9 = (bf16[128,128]{1,0:T(8,128)(2,1)S(1)}, bf16[128,128]{1,0:T(8,128)(2,1)S(1)}, u32[]{:S(2)}, u32[]{:S(2)}) collective-permute-start(bf16[128,128]{1,0:T(8,128)(2,1)S(1)} %get-tuple-element.23), channel_id=1, source_target_pairs={{1,16},{2,17},{3,18},{4,19},{5,20},{6,21},{7,22},{8,23},{9,24},{10... | collective-permute-start | bytes 98312 | tf_op jit(solution)/shard_map/ppermute | solution.py:20

commit v2 on v0

v2 whole, which is shorter than its diff:
```python
import jax
import jax.numpy as jnp
from jax import lax
from jax.experimental import pallas as pl
from jax.experimental.pallas import tpu as pltpu
from jax.sharding import PartitionSpec as P

PANEL = 8
BF16, F32 = jnp.bfloat16, jnp.float32
VMEM = pl.BlockSpec(memory_space=pltpu.VMEM)
SMEM = pl.BlockSpec(memory_space=pltpu.SMEM)


def call(body, outs, ins, scratch, name, mib, flops):
    return pl.pallas_call(
        body,
        out_shape=outs,
        in_specs=ins,
        out_specs=jax.tree.map(lambda _: VMEM, outs),
        scratch_shapes=scratch,
        compiler_params=pltpu.CompilerParams(vmem_limit_bytes=mib * 1024 * 1024),
        cost_estimate=pl.CostEstimate(flops=flops, bytes_accessed=4 * 1024 * 1024, transcendentals=0),
        name=name,
    )


def shift(value, axis, by):
    length = lax.axis_size(axis)
    return lax.ppermute(value, axis, [(i, i + by) for i in range(length) if 0 <= i + by < length])


def iotas(order):
    return (
        lax.broadcasted_iota(jnp.int32, (order, order), 0),
        lax.broadcasted_iota(jnp.int32, (order, order), 1),
    )


def lower_inverse(mat, xs, blocks, order):
    lane = lax.broadcasted_iota(jnp.int32, (PANEL, order), 1)
    sub = lax.broadcasted_iota(jnp.int32, (PANEL, order), 0)

    def step(kb, carry):
        r0 = pl.multiple_of(kb * PANEL, PANEL)
        in_diag = (lane >= r0) & (lane < r0 + PANEL)
        unit = jnp.where(lane - r0 == sub, F32(1.0), F32(0.0))
        rows = [mat[m, pl.ds(r0, PANEL), :] for m in range(blocks)]
        picks = [jnp.full((PANEL, order), r0 + k, jnp.int32) for k in range(PANEL)]
        cols = [[jnp.take_along_axis(r, pick, axis=1) for pick in picks] for r in rows]
        rows = [jnp.where(in_diag, unit, r) for r in rows]
        for k in range(PANEL):
            for n in range(blocks):
                c = cols[n]
                inv = 1.0 / c[k][k : k + 1, :]
                mult = jnp.where(sub > k, c[k] * inv, F32(0.0))
                for j in range(k + 1, PANEL):
                    c[j] = c[j] - mult * c[j][k : k + 1, :]
                rows[n] = rows[n] - mult * rows[n][k : k + 1, :]
        for n in range(blocks):
            diag = cols[n][0]
            for k in range(1, PANEL):
                diag = jnp.where(sub == k, cols[n][k], diag)
            rows[n] = rows[n] * lax.rsqrt(diag)
        for m in range(blocks):
            r = rows[m]
            xs[m, pl.ds(r0, PANEL), :] = r
            hi = r.astype(BF16).astype(F32)
            rest = r - hi
            mid = rest.astype(BF16).astype(F32)
            low = rest - mid
            right = jnp.concatenate([hi, mid, hi, low, hi, mid], axis=0).astype(BF16)
            left = jnp.concatenate([hi, hi, mid, hi, low, mid], axis=0).astype(BF16)
            update = lax.dot_general(
                left, right, (((0,), (0,)), ((), ())), preferred_element_type=F32
            )
            for t in range(0, order, PANEL):
                mat[m, t : t + PANEL] = (
                    jnp.where(in_diag, F32(0.0), mat[m, t : t + PANEL]) - update[t : t + PANEL]
                )
        return carry

    lax.fori_loop(0, order // PANEL, step, 0)


def gram_of(x, y, codes, counts, permit, diag, block_at):
    row, lane = iotas(diag.shape[2])
    total = jnp.zeros(row.shape, F32)
    scale = permit[x, pl.ds(y, 1), :]
    for s in range(codes.shape[2]):
        code = codes[x, y, s]
        block = block_at(code // 3, code % 3)
        on = jnp.where(s < counts[x, y], F32(1.0), F32(0.0))
        scaled = ((scale * on) * block.astype(F32)).astype(BF16)
        total = total + lax.dot_general(
            scaled, block, (((1,), (1,)), ((), ())), preferred_element_type=F32
        )
    total = (total + total.T) * F32(0.5)
    return total + jnp.where(row == lane, diag[x, pl.ds(y, 1), :], F32(0.0))


def image_of(factor, vector):
    return lax.dot_general(factor, vector, (((0,), (0,)), ((), ())), preferred_element_type=F32)


def inner_gram(codes, counts, permit, diag, own, low, high, mats, edge_turned, turned):
    bx, by = own.shape[0], own.shape[1]
    inner = by - 2
    for y in range(by):
        turned[y] = low[y].T
        turned[(bx + 1) * by + y] = high[y].T
        for x in range(bx):
            turned[(x + 1) * by + y] = own[x, y].T
    for p in range(bx + 2):
        for n, y in enumerate((0, 1, by - 2, by - 1)):
            edge_turned[p * 4 + n] = turned[p * by + y]

    def some(x, g):
        for u in range(inner // 2):
            y = g * (inner // 2) + u + 1
            mats[x * inner + y - 1] = gram_of(
                x, y, codes, counts, permit, diag,
                lambda dx, dy: turned[(x + dx) * by + y + dy - 1],
            )

    def body(h, carry):
        some(h // 2, h % 2)
        return carry

    lax.fori_loop(0, 2 * bx, body, 0)


def edge_all(
    codes, counts, weights, permit, diag, edge_turned, left, right, vectors,
    factors, part, to_left, to_right, turned, mats, xs, acc,
):
    bx, by = vectors.shape[0], vectors.shape[1]
    order = mats.shape[1]
    for p in range(bx + 2):
        turned[p * 6] = left[p].T
        turned[p * 6 + 5] = right[p].T
        for n in range(4):
            turned[p * 6 + 1 + n] = edge_turned[p * 4 + n]
    edges = [(x, side) for x in range(bx) for side in range(2)]
    for m, (x, side) in enumerate(edges):
        mats[m] = gram_of(
            x, side * (by - 1), codes, counts, permit, diag,
            lambda dx, dy: turned[(x + dx) * 6 + side * 3 + dy],
        )
    lower_inverse(mats, xs, len(edges), order)
    acc[...] = jnp.zeros(acc.shape, acc.dtype)
    row, lane = iotas(order)
    images = []
    for m, (x, side) in enumerate(edges):
        f = jnp.where(lane <= row, xs[m], F32(0.0)).astype(BF16)
        factors[m] = f
        images.append(image_of(f, vectors[x, side * (by - 1)]))
    for m, (x, side) in enumerate(edges):
        y = side * (by - 1)

        def add(s, c):
            code = codes[x, y, s]
            n = (x + code // 3) * 6 + side * 3 + code % 3
            acc[n] = acc[n] + weights[x, y, s] * images[m]
            return c

        lax.fori_loop(0, counts[x, y], add, 0)
    for p in range(bx + 2):
        to_left[p] = acc[p * 6].astype(BF16)
        to_right[p] = acc[p * 6 + 5].astype(BF16)
        for n in range(4):
            part[p * 4 + n] = acc[p * 6 + 1 + n]


def inner_all(
    codes, counts, weights, mats_in, part, edge_factors, vectors,
    factor, center, halo, mats, xs, acc,
):
    bx, by = vectors.shape[0], vectors.shape[1]
    inner = by - 2
    order = mats.shape[1]
    mats[...] = mats_in[...]
    lower_inverse(mats, xs, bx * inner, order)
    zero = jnp.zeros(acc.shape[1:], F32)
    for p in range(bx + 2):
        for y in range(2, by - 2):
            acc[p * by + y] = zero
        for n, y in enumerate((0, 1, by - 2, by - 1)):
            acc[p * by + y] = part[p * 4 + n]
    for x in range(bx):
        factor[x, 0] = edge_factors[2 * x]
        factor[x, by - 1] = edge_factors[2 * x + 1]
    row, lane = iotas(order)

    def body(h, carry):
        x = h // (inner // 2)
        images = []
        for u in range(2):
            y = (h % (inner // 2)) * 2 + u + 1
            f = jnp.where(lane <= row, xs[x * inner + y - 1], F32(0.0)).astype(BF16)
            factor[x, y] = f
            images.append(image_of(f, vectors[x, y]))
        for u in range(2):
            y = (h % (inner // 2)) * 2 + u + 1

            def add(s, c):
                code = codes[x, y, s]
                n = (x + code // 3) * by + y + code % 3 - 1
                acc[n] = acc[n] + weights[x, y, s] * images[u]
                return c

            lax.fori_loop(0, counts[x, y], add, 0)
        return carry

    lax.fori_loop(0, bx * inner // 2, body, 0)
    for y in range(by):
        halo[0, y] = acc[y]
        halo[1, y] = acc[(bx + 1) * by + y]
        for x in range(bx):
            center[x, y] = acc[(x + 1) * by + y]


def close_halo(halo, from_left, from_right, to_low, to_high):
    by = halo.shape[1]
    last = from_left.shape[0] - 1
    for out, h, p in ((to_low, 0, 0), (to_high, 1, last)):
        for y in range(by):
            v = halo[h, y]
            if y == 0:
                v = v + from_left[p].astype(F32)
            if y == by - 1:
                v = v + from_right[p].astype(F32)
            out[y] = v.astype(BF16)


def collect(center, low, high, left, right, out):
    bx, by = center.shape[0], center.shape[1]
    for x in range(bx):
        for y in range(by):
            v = center[x, y]
            if x == 0:
                v = v + low[y].astype(F32)
            if x == bx - 1:
                v = v + high[y].astype(F32)
            if y == 0:
                v = v + left[x + 1].astype(F32)
            if y == by - 1:
                v = v + right[x + 1].astype(F32)
            out[x, y] = v.astype(out.dtype)


def local(coeffs, permit, diag, codes, counts, weights, vectors):
    bx, by, coupling, order = coeffs.shape
    width = vectors.shape[3]
    rows, inner = bx + 2, by - 2
    shape = jax.ShapeDtypeStruct
    low = shift(coeffs[bx - 1], "gx", 1)
    high = shift(coeffs[0], "gx", -1)
    left_send = jnp.concatenate([low[None, by - 1], coeffs[:, by - 1], high[None, by - 1]], axis=0)
    right_send = jnp.concatenate([low[None, 0], coeffs[:, 0], high[None, 0]], axis=0)
    left = shift(left_send, "gy", 1)
    right = shift(right_send, "gy", -1)
    mats, edge_turned = call(
        inner_gram,
        (shape((bx * inner, order, order), F32), shape((rows * 4, order, coupling), BF16)),
        [SMEM] * 2 + [VMEM] * 5,
        [pltpu.VMEM((rows * by, order, coupling), BF16)],
        "inner_gram", 16, 4 * 10**9,
    )(codes, counts, permit, diag, coeffs, low, high)
    edge_factors, part, to_left, to_right = call(
        edge_all,
        (
            shape((2 * bx, order, order), BF16),
            shape((rows * 4, order, width), F32),
            shape((rows, order, width), BF16),
            shape((rows, order, width), BF16),
        ),
        [SMEM] * 3 + [VMEM] * 6,
        [
            pltpu.VMEM((rows * 6, order, coupling), BF16),
            pltpu.VMEM((2 * bx, order, order), F32),
            pltpu.VMEM((2 * bx, order, order), F32),
            pltpu.VMEM((rows * 6, order, width), F32),
        ],
        "edge_all", 16, 8 * 10**9,
    )(codes, counts, weights, permit, diag, edge_turned, left, right, vectors)
    from_left = shift(to_right, "gy", 1)
    from_right = shift(to_left, "gy", -1)
    factor, center, halo = call(
        inner_all,
        (
            shape((bx, by, order, order), BF16),
            shape((bx, by, order, width), F32),
            shape((2, by, order, width), F32),
        ),
        [SMEM] * 3 + [VMEM] * 4,
        [
            pltpu.VMEM((bx * inner, order, order), F32),
            pltpu.VMEM((bx * inner, order, order), F32),
            pltpu.VMEM((rows * by, order, width), F32),
        ],
        "inner_all", 20, 12 * 10**9,
    )(codes, counts, weights, mats, part, edge_factors, vectors)
    to_low, to_high = call(
        close_halo,
        (shape((by, order, width), BF16), shape((by, order, width), BF16)),
        [VMEM] * 3, [], "close_halo", 8, 10**8,
    )(halo, from_left, from_right)
    from_low = shift(to_high, "gx", 1)
    from_high = shift(to_low, "gx", -1)
    applied = call(
        collect, shape(center.shape, BF16), [VMEM] * 5, [], "collect", 8, 10**8,
    )(center, from_low, from_high, from_left, from_right)
    return factor, applied


def solution(mesh):
    placed = (
        P("gx", "gy", None, None),
        P("gx", "gy", None),
        P("gx", "gy", None),
        P("gx", "gy", None),
        P("gx", "gy"),
        P("gx", "gy", None),
        P("gx", "gy", None, None),
    )
    return jax.shard_map(
        local,
        mesh=mesh,
        in_specs=placed,
        out_specs=(P("gx", "gy", None, None), P("gx", "gy", None, None)),
        check_vma=False,
    )
```

time: 469 us -> 71.5 us (0.15)
  other arithmetic: 379 us -> 0.07 us
  local copies, waits for them, and re-layouts: 40.4 us -> 1.64 us
  Pallas kernels: 0 us -> 26.7 us
  matrix products: 6.07 us -> 0 us
    another operation x9 -> x0, other arithmetic: 348 us -> none  [the longest x4 189 us: local(): cholesky_factor = jnp.linalg.cholesky(system)]
    pallas_call x0 -> x5, Pallas kernels: none -> 26.7 us  [the longest x1 13.8 us: local(): call(inner_all, (shape((bx, by, order, order), BF16), shape((bx, by, orde...]
    select_n x6 -> x0, other arithmetic: 14.5 us -> none  [local(): jnp.take(flattened, flat_index.reshape(-1), axis=0)]
    select_n x6 -> x0, local copies, waits for them, and re-layouts: 13.7 us -> none  [local(): jnp.take(flattened, flat_index.reshape(-1), axis=0)]
    gather x6 -> x0, local copies, waits for them, and re-layouts: 10.9 us -> none  [local(): jnp.take(flattened, flat_index.reshape(-1), axis=0)]
    unnamed x82 -> x16, local copies, waits for them, and re-layouts: 5.87 us -> 0.21 us
    scatter-add x12 -> x0, other arithmetic: 5.17 us -> none  [the longest x8 4.91 us: local(): gathered_sum = gathered_sum.at[offset // 3:offset // 3 + blocks_x, offset...]
  transfers between devices with their start and end apart: 8 -> 8, of which waited for: 6 -> 4; matrix products, arithmetic and copies ran while one was open for 3% -> 0% of each run, Pallas kernels for 0% -> 24%
where the time goes in v2:
time: 71.5 us; the launch traced here: 71.1 us
  starting transfers between devices  30.2 us (42%)
  Pallas kernels  26.7 us (37%)
  waiting for transfers between devices  11.6 us (16%)
  local copies, waits for them, and re-layouts  1.64 us (2%)
  between operations  0.86 us (1%)
    ppermute x8, starting transfers between devices, shift(): lax.ppermute(value, axis, [(i, i + by) for i in range(length) if 0 <= i +...  30.2 us
    pallas_call x1, Pallas kernels, local(): call(inner_all, (shape((bx, by, order, order), BF16), shape((bx, by, orde...  13.8 us
    ppermute x8, waiting for transfers between devices, shift(): lax.ppermute(value, axis, [(i, i + by) for i in range(length) if 0 <= i +...  11.6 us
    pallas_call x1, Pallas kernels, local(): call(edge_all, (shape((2 * bx, order, order), BF16), shape((rows * 4, ord...  8.38 us
    pallas_call x1, Pallas kernels, local(): call(inner_gram, (shape((bx * inner, order, order), F32), shape((rows * 4...  3.59 us
  transfers between devices with their start and end apart: 8, of which 4 were waited for; matrix products, arithmetic and copies ran while one was open for 0% of the time, Pallas kernels for 24%

profile of v2, /device:TPU:25, one launch (start us, length us, event | category | flops | bytes accessed | tf_op | source)
XLA Modules:
  0.0 71.1 jit_solution(5795400788928851090)
XLA Ops:
  0.6 0.0 copy-start
  0.6 0.0 copy-start.5
  0.6 1.4 %slice_bitcast_fusion = (bf16[8,256,128]{2,1,0:T(8,128)(2,1)S(1)}, bf16[8,256,128]{2,1,0:T(8,128)(2,1)S(1)}) fusion(bf16[2,8,256,128]{3,2,1,0:T(8,128)(2,1)} %own.1), kind=kLoop, calls=%fused_computation | loop fusion | bytes 2097152 | tf_op jit(solution)/shard_map/squeeze | solution.py:257
  2.0 2.6 %collective-permute-start.1 = (bf16[8,256,128]{2,1,0:T(8,128)(2,1)S(1)}, bf16[8,256,128]{2,1,0:T(8,128)(2,1)S(1)}, u32[]{:S(2)}, u32[]{:S(2)}) collective-permute-start(bf16[8,256,128]{2,1,0:T(8,128)(2,1)S(1)} %get-tuple-element.26), channel_id=1, source_target_pairs={{16,0},{32,16},{48,32},{64,48},{80,64},{96,80},{112,96},{17,1},{33... | collective-permute-start | bytes 1572872 | tf_op jit(solution)/shard_map/ppermute | solution.py:29
  4.6 0.0 copy-start.6
  4.6 3.4 %collective-permute-start = (bf16[8,256,128]{2,1,0:T(8,128)(2,1)S(1)}, bf16[8,256,128]{2,1,0:T(8,128)(2,1)S(1)}, u32[]{:S(2)}, u32[]{:S(2)}) collective-permute-start(bf16[8,256,128]{2,1,0:T(8,128)(2,1)S(1)} %get-tuple-element.27), channel_id=1, source_target_pairs={{0,16},{16,32},{32,48},{48,64},{64,80},{80,96},{96,112},{1,17},{17... | collective-permute-start | bytes 1572872 | tf_op jit(solution)/shard_map/ppermute | solution.py:29
  8.1 0.0 copy-done.5
  8.1 0.1 copy.14.codes
  8.2 0.1 copy.15.weights
  8.3 4.7 %collective-permute-done.1.high = bf16[8,256,128]{2,1,0:T(8,128)(2,1)S(1)} collective-permute-done((bf16[8,256,128]{2,1,0:T(8,128)(2,1)S(1)}, bf16[8,256,128]{2,1,0:T(8,128)(2,1)S(1)}, u32[]{:S(2)}, u32[]{:S(2)}) %collective-permute-start.1) | collective-permute-done | bytes 524320 | tf_op jit(solution)/shard_map/ppermute | solution.py:29
  13.0 1.2 %collective-permute-done.low = bf16[8,256,128]{2,1,0:T(8,128)(2,1)S(1)} collective-permute-done((bf16[8,256,128]{2,1,0:T(8,128)(2,1)S(1)}, bf16[8,256,128]{2,1,0:T(8,128)(2,1)S(1)}, u32[]{:S(2)}, u32[]{:S(2)}) %collective-permute-start) | collective-permute-done | bytes 524320 | tf_op jit(solution)/shard_map/ppermute | solution.py:29
  14.3 3.1 %collective-permute-start.2 = (bf16[4,256,128]{2,1,0:T(8,128)(2,1)S(1)}, bf16[4,256,128]{2,1,0:T(8,128)(2,1)S(1)}, u32[]{:S(2)}, u32[]{:S(2)}) collective-permute-start(bf16[4,256,128]{2,1,0:T(8,128)(2,1)S(1)} %pad_maximum_fusion), channel_id=1, source_target_pairs={{0,1},{1,2},{2,3},{3,4},{4,5},{5,6},{6,7},{7,8},{8,9},{9,10},{10,1... | collective-permute-start | bytes 786440 | tf_op jit(solution)/shard_map/ppermute | solution.py:29
  17.4 0.0 copy-start.2
  17.4 0.0 copy-start.3
  17.4 0.0 copy-start.4
  17.5 0.0 copy-start.1
  17.5 4.4 %collective-permute-start.3 = (bf16[4,256,128]{2,1,0:T(8,128)(2,1)S(1)}, bf16[4,256,128]{2,1,0:T(8,128)(2,1)S(1)}, u32[]{:S(2)}, u32[]{:S(2)}) collective-permute-start(bf16[4,256,128]{2,1,0:T(8,128)(2,1)S(1)} %pad_maximum_fusion.1), channel_id=1, source_target_pairs={{1,0},{2,1},{3,2},{4,3},{5,4},{6,5},{7,6},{8,7},{9,8},{10,9},{11,1... | collective-permute-start | bytes 786440 | tf_op jit(solution)/shard_map/ppermute | solution.py:29
  21.9 3.6 %inner_gram.1 = (f32[12,128,128]{2,1,0:T(8,128)S(1)}, bf16[16,128,256]{2,1,0:T(8,128)(2,1)S(1)}) custom-call(s32[2,8,6]{2,1,0:T(8,128)S(1)} %copy.14.codes, s32[2,8]{1,0:T(2,128)S(1)} %copy-done.4, f32[2,8,256]{2,1,0:T(8,128)S(1)} %copy-done.2, f32[2,8,128]{2,1,0:T(8,128)S(1)} %copy-done.3, bf16[2,8,256,128]{3,2,1,0:T(8,128)(2,1)S(1)} %copy-done, ...), custom_call_target="tpu_custom_call" | custom-call | flops 4000000000 | bytes 4194304 | tf_op jit(solution)/shard_map/inner_gram/pallas_call | solution.py:262
  25.5 0.0 collective-permute-done.2.left
  25.5 0.0 collective-permute-done.3.right
  25.5 8.4 %edge_all.1 = (bf16[4,128,128]{2,1,0:T(8,128)(2,1)S(1)}, f32[16,128,128]{2,1,0:T(8,128)S(1)}, bf16[4,128,128]{2,1,0:T(8,128)(2,1)S(1)}, bf16[4,128,128]{2,1,0:T(8,128)(2,1)S(1)}) custom-call(s32[2,8,6]{2,1,0:T(8,128)S(1)} %copy.14.codes, s32[2,8]{1,0:T(2,128)S(1)} %copy-done.4, f32[2,8,6]{2,1,0:T(8,128)S(1)} %copy.15.weights, f32[2,8,256]{2,1,0:T(8,128)S(1)} %copy-done.2, ...), custom_call_target="tpu_custom_call" | custom-call | flops 8000000000 | bytes 4194304 | tf_op jit(solution)/shard_map/edge_all/pallas_call | solution.py:269
  33.9 2.4 %collective-permute-start.4 = (bf16[4,128,128]{2,1,0:T(8,128)(2,1)S(1)}, bf16[4,128,128]{2,1,0:T(8,128)(2,1)S(1)}, u32[]{:S(2)}, u32[]{:S(2)}) collective-permute-start(bf16[4,128,128]{2,1,0:T(8,128)(2,1)S(1)} %get-tuple-element.20), channel_id=1, source_target_pairs={{0,1},{1,2},{2,3},{3,4},{4,5},{5,6},{6,7},{7,8},{8,9},{9,10},{10,1... | collective-permute-start | bytes 393224 | tf_op jit(solution)/shard_map/ppermute | solution.py:29
  36.3 5.3 %collective-permute-start.5 = (bf16[4,128,128]{2,1,0:T(8,128)(2,1)S(1)}, bf16[4,128,128]{2,1,0:T(8,128)(2,1)S(1)}, u32[]{:S(2)}, u32[]{:S(2)}) collective-permute-start(bf16[4,128,128]{2,1,0:T(8,128)(2,1)S(1)} %get-tuple-element.21), channel_id=1, source_target_pairs={{1,0},{2,1},{3,2},{4,3},{5,4},{6,5},{7,6},{8,7},{9,8},{10,9},{11,1... | collective-permute-start | bytes 393224 | tf_op jit(solution)/shard_map/ppermute | solution.py:29
  41.6 13.8 %inner_all.1 = (bf16[2,8,128,128]{3,2,1,0:T(8,128)(2,1)}, f32[2,8,128,128]{3,2,1,0:T(8,128)S(1)}, f32[2,8,128,128]{3,2,1,0:T(8,128)S(1)}) custom-call(s32[2,8,6]{2,1,0:T(8,128)S(1)} %copy.14.codes, s32[2,8]{1,0:T(2,128)S(1)} %copy-done.4, f32[2,8,6]{2,1,0:T(8,128)S(1)} %copy.15.weights, f32[12,128,128]{2,1,0:T(8,128)S(1)} %get-tuple-element.13.mats_in, ...), custom_call_target="tpu_custom_call" | custom-call | flops 12000000000 | bytes 4194304 | tf_op jit(solution)/shard_map/inner_all/pallas_call | solution.py:288
  55.4 0.0 collective-permute-done.4.from_left.left
  55.4 0.0 collective-permute-done.5.from_right.right
  55.4 0.1 close_halo.1
  55.5 7.0 %collective-permute-start.6 = (bf16[8,128,128]{2,1,0:T(8,128)(2,1)S(1)}, bf16[8,128,128]{2,1,0:T(8,128)(2,1)S(1)}, u32[]{:S(2)}, u32[]{:S(2)}) collective-permute-start(bf16[8,128,128]{2,1,0:T(8,128)(2,1)S(1)} %get-tuple-element.22), channel_id=1, source_target_pairs={{0,16},{16,32},{32,48},{48,64},{64,80},{80,96},{96,112},{1,17},{17... | collective-permute-start | bytes 786440 | tf_op jit(solution)/shard_map/ppermute | solution.py:29
  62.5 1.9 %collective-permute-start.7 = (bf16[8,128,128]{2,1,0:T(8,128)(2,1)S(1)}, bf16[8,128,128]{2,1,0:T(8,128)(2,1)S(1)}, u32[]{:S(2)}, u32[]{:S(2)}) collective-permute-start(bf16[8,128,128]{2,1,0:T(8,128)(2,1)S(1)} %get-tuple-element.23), channel_id=1, source_target_pairs={{16,0},{32,16},{48,32},{64,48},{80,64},{96,80},{112,96},{17,1},{33... | collective-permute-start | bytes 786440 | tf_op jit(solution)/shard_map/ppermute | solution.py:29
  64.5 1.4 %collective-permute-done.6.low = bf16[8,128,128]{2,1,0:T(8,128)(2,1)S(1)} collective-permute-done((bf16[8,128,128]{2,1,0:T(8,128)(2,1)S(1)}, bf16[8,128,128]{2,1,0:T(8,128)(2,1)S(1)}, u32[]{:S(2)}, u32[]{:S(2)}) %collective-permute-start.6) | collective-permute-done | bytes 262176 | tf_op jit(solution)/shard_map/ppermute | solution.py:29
  65.8 4.4 %collective-permute-done.7.high = bf16[8,128,128]{2,1,0:T(8,128)(2,1)S(1)} collective-permute-done((bf16[8,128,128]{2,1,0:T(8,128)(2,1)S(1)}, bf16[8,128,128]{2,1,0:T(8,128)(2,1)S(1)}, u32[]{:S(2)}, u32[]{:S(2)}) %collective-permute-start.7) | collective-permute-done | bytes 262176 | tf_op jit(solution)/shard_map/ppermute | solution.py:29
  70.2 0.9 %collect.1 = bf16[2,8,128,128]{3,2,1,0:T(8,128)(2,1)} custom-call(f32[2,8,128,128]{3,2,1,0:T(8,128)S(1)} %get-tuple-element.18.center, bf16[8,128,128]{2,1,0:T(8,128)(2,1)S(1)} %collective-permute-done.6.low, bf16[8,128,128]{2,1,0:T(8,128)(2,1)S(1)} %collective-permute-done.7.high, bf16[4,128,128]{2,1,0:T(8,128)(2,1)S(1)} %collective-permute-done.4.from_left.left, ...), custom_call_target="tpu_custom_call" | custom-call | flops 100000000 | bytes 4194304 | tf_op jit(solution)/shard_map/collect/pallas_call | solution.py:310
  (11 shorter events, 0.1 us)
Async XLA Ops:
  0.6 7.7 %copy-start = (bf16[2,8,256,128]{3,2,1,0:T(8,128)(2,1)S(1)}, bf16[2,8,256,128]{3,2,1,0:T(8,128)(2,1)}, u32[]{:S(2)}) copy-start(bf16[2,8,256,128]{3,2,1,0:T(8,128)(2,1)} %own.1) | copy-start | bytes 3145732
  0.6 7.5 %copy-start.5 = (s32[2,8,6]{1,0,2:T(2,128)S(1)}, s32[2,8,6]{1,0,2:T(2,128)}, u32[]{:S(2)}) copy-start(s32[2,8,6]{1,0,2:T(2,128)} %param.10) | copy-start | bytes 1156
  2.0 11.0 %collective-permute-start.1 = (bf16[8,256,128]{2,1,0:T(8,128)(2,1)S(1)}, bf16[8,256,128]{2,1,0:T(8,128)(2,1)S(1)}, u32[]{:S(2)}, u32[]{:S(2)}) collective-permute-start(bf16[8,256,128]{2,1,0:T(8,128)(2,1)S(1)} %get-tuple-element.26), channel_id=1, source_target_pairs={{16,0},{32,16},{48,32},{64,48},{80,64},{96,80},{112,96},{17,1},{33... | collective-permute-start | bytes 1572872 | tf_op jit(solution)/shard_map/ppermute | solution.py:29
  4.6 3.6 %copy-start.6 = (f32[2,8,6]{1,0,2:T(2,128)S(1)}, f32[2,8,6]{1,0,2:T(2,128)}, u32[]{:S(2)}) copy-start(f32[2,8,6]{1,0,2:T(2,128)} %param.12) | copy-start | bytes 1156
  4.6 9.6 %collective-permute-start = (bf16[8,256,128]{2,1,0:T(8,128)(2,1)S(1)}, bf16[8,256,128]{2,1,0:T(8,128)(2,1)S(1)}, u32[]{:S(2)}, u32[]{:S(2)}) collective-permute-start(bf16[8,256,128]{2,1,0:T(8,128)(2,1)S(1)} %get-tuple-element.27), channel_id=1, source_target_pairs={{0,16},{16,32},{32,48},{48,64},{64,80},{80,96},{96,112},{1,17},{17... | collective-permute-start | bytes 1572872 | tf_op jit(solution)/shard_map/ppermute | solution.py:29
  14.3 11.3 %collective-permute-start.2 = (bf16[4,256,128]{2,1,0:T(8,128)(2,1)S(1)}, bf16[4,256,128]{2,1,0:T(8,128)(2,1)S(1)}, u32[]{:S(2)}, u32[]{:S(2)}) collective-permute-start(bf16[4,256,128]{2,1,0:T(8,128)(2,1)S(1)} %pad_maximum_fusion), channel_id=1, source_target_pairs={{0,1},{1,2},{2,3},{3,4},{4,5},{5,6},{6,7},{7,8},{8,9},{9,10},{10,1... | collective-permute-start | bytes 786440 | tf_op jit(solution)/shard_map/ppermute | solution.py:29
  17.4 4.5 %copy-start.2 = (f32[2,8,256]{2,1,0:T(8,128)S(1)}, f32[2,8,256]{2,1,0:T(8,128)}, u32[]{:S(2)}) copy-start(f32[2,8,256]{2,1,0:T(8,128)} %permit.3) | copy-start | bytes 49156
  17.4 4.5 %copy-start.3 = (f32[2,8,128]{2,1,0:T(8,128)S(1)}, f32[2,8,128]{2,1,0:T(8,128)}, u32[]{:S(2)}) copy-start(f32[2,8,128]{2,1,0:T(8,128)} %diag.3) | copy-start | bytes 24580
  17.4 4.5 %copy-start.4 = (s32[2,8]{1,0:T(2,128)S(1)}, s32[2,8]{1,0:T(2,128)}, u32[]{:S(2)}) copy-start(s32[2,8]{1,0:T(2,128)} %counts.5) | copy-start | bytes 196
  17.5 8.1 %copy-start.1 = (bf16[2,8,128,128]{3,2,1,0:T(8,128)(2,1)S(1)}, bf16[2,8,128,128]{3,2,1,0:T(8,128)(2,1)}, u32[]{:S(2)}) copy-start(bf16[2,8,128,128]{3,2,1,0:T(8,128)(2,1)} %vectors.3) | copy-start | bytes 1572868
  17.5 8.1 %collective-permute-start.3 = (bf16[4,256,128]{2,1,0:T(8,128)(2,1)S(1)}, bf16[4,256,128]{2,1,0:T(8,128)(2,1)S(1)}, u32[]{:S(2)}, u32[]{:S(2)}) collective-permute-start(bf16[4,256,128]{2,1,0:T(8,128)(2,1)S(1)} %pad_maximum_fusion.1), channel_id=1, source_target_pairs={{1,0},{2,1},{3,2},{4,3},{5,4},{6,5},{7,6},{8,7},{9,8},{10,9},{11,1... | collective-permute-start | bytes 786440 | tf_op jit(solution)/shard_map/ppermute | solution.py:29
  33.9 21.5 %collective-permute-start.4 = (bf16[4,128,128]{2,1,0:T(8,128)(2,1)S(1)}, bf16[4,128,128]{2,1,0:T(8,128)(2,1)S(1)}, u32[]{:S(2)}, u32[]{:S(2)}) collective-permute-start(bf16[4,128,128]{2,1,0:T(8,128)(2,1)S(1)} %get-tuple-element.20), channel_id=1, source_target_pairs={{0,1},{1,2},{2,3},{3,4},{4,5},{5,6},{6,7},{7,8},{8,9},{9,10},{10,1... | collective-permute-start | bytes 393224 | tf_op jit(solution)/shard_map/ppermute | solution.py:29
  36.3 19.1 %collective-permute-start.5 = (bf16[4,128,128]{2,1,0:T(8,128)(2,1)S(1)}, bf16[4,128,128]{2,1,0:T(8,128)(2,1)S(1)}, u32[]{:S(2)}, u32[]{:S(2)}) collective-permute-start(bf16[4,128,128]{2,1,0:T(8,128)(2,1)S(1)} %get-tuple-element.21), channel_id=1, source_target_pairs={{1,0},{2,1},{3,2},{4,3},{5,4},{6,5},{7,6},{8,7},{9,8},{10,9},{11,1... | collective-permute-start | bytes 393224 | tf_op jit(solution)/shard_map/ppermute | solution.py:29
  55.5 10.3 %collective-permute-start.6 = (bf16[8,128,128]{2,1,0:T(8,128)(2,1)S(1)}, bf16[8,128,128]{2,1,0:T(8,128)(2,1)S(1)}, u32[]{:S(2)}, u32[]{:S(2)}) collective-permute-start(bf16[8,128,128]{2,1,0:T(8,128)(2,1)S(1)} %get-tuple-element.22), channel_id=1, source_target_pairs={{0,16},{16,32},{32,48},{48,64},{64,80},{80,96},{96,112},{1,17},{17... | collective-permute-start | bytes 786440 | tf_op jit(solution)/shard_map/ppermute | solution.py:29
  62.5 7.7 %collective-permute-start.7 = (bf16[8,128,128]{2,1,0:T(8,128)(2,1)S(1)}, bf16[8,128,128]{2,1,0:T(8,128)(2,1)S(1)}, u32[]{:S(2)}, u32[]{:S(2)}) collective-permute-start(bf16[8,128,128]{2,1,0:T(8,128)(2,1)S(1)} %get-tuple-element.23), channel_id=1, source_target_pairs={{16,0},{32,16},{48,32},{64,48},{80,64},{96,80},{112,96},{17,1},{33... | collective-permute-start | bytes 786440 | tf_op jit(solution)/shard_map/ppermute | solution.py:29

commit v3 on v2

--- a/solution.py
+++ b/solution.py
@@ -24,9 +24,15 @@
     )
 
 
-def shift(value, axis, by):
-    length = lax.axis_size(axis)
-    return lax.ppermute(value, axis, [(i, i + by) for i in range(length) if 0 <= i + by < length])
+def swap(value, axis, first):
+    pairs = []
+    for i in range(first, lax.axis_size(axis) - 1, 2):
+        pairs += [(i, i + 1), (i + 1, i)]
+    return lax.ppermute(value, axis, pairs)
+
+
+def parity(axis):
+    return lax.rem(lax.axis_index(axis), 2)
 
 
 def iotas(order):
@@ -102,12 +108,13 @@
     return lax.dot_general(factor, vector, (((0,), (0,)), ((), ())), preferred_element_type=F32)
 
 
-def inner_gram(codes, counts, permit, diag, own, low, high, mats, edge_turned, turned):
+def inner_gram(codes, counts, permit, diag, own, odd, even, mats, edge_turned, turned):
     bx, by = own.shape[0], own.shape[1]
     inner = by - 2
+    px = parity("gx")
     for y in range(by):
-        turned[y] = low[y].T
-        turned[(bx + 1) * by + y] = high[y].T
+        turned[px * (bx + 1) * by + y] = odd[y].T
+        turned[(1 - px) * (bx + 1) * by + y] = even[y].T
         for x in range(bx):
             turned[(x + 1) * by + y] = own[x, y].T
     for p in range(bx + 2):
@@ -130,14 +137,16 @@
 
 
 def edge_all(
-    codes, counts, weights, permit, diag, edge_turned, left, right, vectors,
-    factors, part, to_left, to_right, turned, mats, xs, acc,
+    codes, counts, weights, permit, diag, edge_turned, odd, even, vectors,
+    factors, part, to_odd, to_even, turned, mats, xs, acc,
 ):
     bx, by = vectors.shape[0], vectors.shape[1]
     order = mats.shape[1]
+    px, py = parity("gx"), parity("gy")
     for p in range(bx + 2):
-        turned[p * 6] = left[p].T
-        turned[p * 6 + 5] = right[p].T
+        row = px * (bx + 1) if p == 0 else (1 - px) * (bx + 1) if p == bx + 1 else p
+        turned[row * 6 + 5 * py] = odd[p].T
+        turned[row * 6 + 5 * (1 - py)] = even[p].T
         for n in range(4):
             turned[p * 6 + 1 + n] = edge_turned[p * 4 + n]
     edges = [(x, side) for x in range(bx) for side in range(2)]
@@ -165,8 +174,8 @@
 
         lax.fori_loop(0, counts[x, y], add, 0)
     for p in range(bx + 2):
-        to_left[p] = acc[p * 6].astype(BF16)
-        to_right[p] = acc[p * 6 + 5].astype(BF16)
+        to_odd[p] = acc[p * 6 + 5 * py].astype(BF16)
+        to_even[p] = acc[p * 6 + 5 * (1 - py)].astype(BF16)
         for n in range(4):
             part[p * 4 + n] = acc[p * 6 + 1 + n]
 
@@ -219,33 +228,26 @@
             center[x, y] = acc[(x + 1) * by + y]
 
 
-def close_halo(halo, from_left, from_right, to_low, to_high):
+def close_halo(halo, odd, even, to_odd, to_even):
     by = halo.shape[1]
-    last = from_left.shape[0] - 1
-    for out, h, p in ((to_low, 0, 0), (to_high, 1, last)):
-        for y in range(by):
-            v = halo[h, y]
-            if y == 0:
-                v = v + from_left[p].astype(F32)
-            if y == by - 1:
-                v = v + from_right[p].astype(F32)
-            out[y] = v.astype(BF16)
-
-
-def collect(center, low, high, left, right, out):
+    last = odd.shape[0] - 1
+    px, py = parity("gx"), parity("gy")
+    for out, h in ((to_odd, px), (to_even, 1 - px)):
+        for y in range(1, by - 1):
+            out[y] = halo[h, y].astype(BF16)
+        for terms, y in ((odd, (by - 1) * py), (even, (by - 1) * (1 - py))):
+            out[y] = (halo[h, y] + terms[h * last].astype(F32)).astype(BF16)
+
+
+def collect(center, odd_x, even_x, odd_y, even_y, out):
     bx, by = center.shape[0], center.shape[1]
-    for x in range(bx):
-        for y in range(by):
-            v = center[x, y]
-            if x == 0:
-                v = v + low[y].astype(F32)
-            if x == bx - 1:
-                v = v + high[y].astype(F32)
-            if y == 0:
-                v = v + left[x + 1].astype(F32)
-            if y == by - 1:
-                v = v + right[x + 1].astype(F32)
-            out[x, y] = v.astype(out.dtype)
+    px, py = parity("gx"), parity("gy")
+    for terms, x in ((odd_x, (bx - 1) * px), (even_x, (bx - 1) * (1 - px))):
+        for y in range(1, by - 1):
+            out[x, y] = (center[x, y] + terms[y].astype(F32)).astype(BF16)
+        for more, y in ((odd_y, (by - 1) * py), (even_y, (by - 1) * (1 - py))):
+            v = center[x, y] + terms[y].astype(F32) + more[x + 1].astype(F32)
+            out[x, y] = v.astype(BF16)
 
 
 def local(coeffs, permit, diag, codes, counts, weights, vectors):
@@ -253,20 +255,24 @@
     width = vectors.shape[3]
     rows, inner = bx + 2, by - 2
     shape = jax.ShapeDtypeStruct
-    low = shift(coeffs[bx - 1], "gx", 1)
-    high = shift(coeffs[0], "gx", -1)
-    left_send = jnp.concatenate([low[None, by - 1], coeffs[:, by - 1], high[None, by - 1]], axis=0)
-    right_send = jnp.concatenate([low[None, 0], coeffs[:, 0], high[None, 0]], axis=0)
-    left = shift(left_send, "gy", 1)
-    right = shift(right_send, "gy", -1)
+    px, py = parity("gx"), parity("gy")
+    pick = lax.dynamic_index_in_dim
+
+    def column(y):
+        return jnp.concatenate([pick(odd_x, y, 0), pick(coeffs, y, 1, False), pick(even_x, y, 0)])
+
+    odd_x = swap(pick(coeffs, (bx - 1) * px, 0, False), "gx", 1)
+    even_x = swap(pick(coeffs, (bx - 1) * (1 - px), 0, False), "gx", 0)
+    odd_y = swap(column((by - 1) * py), "gy", 1)
+    even_y = swap(column((by - 1) * (1 - py)), "gy", 0)
     mats, edge_turned = call(
         inner_gram,
         (shape((bx * inner, order, order), F32), shape((rows * 4, order, coupling), BF16)),
         [SMEM] * 2 + [VMEM] * 5,
         [pltpu.VMEM((rows * by, order, coupling), BF16)],
         "inner_gram", 16, 4 * 10**9,
-    )(codes, counts, permit, diag, coeffs, low, high)
-    edge_factors, part, to_left, to_right = call(
+    )(codes, counts, permit, diag, coeffs, odd_x, even_x)
+    edge_factors, part, to_odd, to_even = call(
         edge_all,
         (
             shape((2 * bx, order, order), BF16),
@@ -282,9 +288,9 @@
             pltpu.VMEM((rows * 6, order, width), F32),
         ],
         "edge_all", 16, 8 * 10**9,
-    )(codes, counts, weights, permit, diag, edge_turned, left, right, vectors)
-    from_left = shift(to_right, "gy", 1)
-    from_right = shift(to_left, "gy", -1)
+    )(codes, counts, weights, permit, diag, edge_turned, odd_y, even_y, vectors)
+    from_odd_y = swap(to_odd, "gy", 1)
+    from_even_y = swap(to_even, "gy", 0)
     factor, center, halo = call(
         inner_all,
         (
@@ -300,16 +306,16 @@
         ],
         "inner_all", 20, 12 * 10**9,
     )(codes, counts, weights, mats, part, edge_factors, vectors)
-    to_low, to_high = call(
+    to_odd, to_even = call(
         close_halo,
         (shape((by, order, width), BF16), shape((by, order, width), BF16)),
         [VMEM] * 3, [], "close_halo", 8, 10**8,
-    )(halo, from_left, from_right)
-    from_low = shift(to_high, "gx", 1)
-    from_high = shift(to_low, "gx", -1)
+    )(halo, from_odd_y, from_even_y)
+    from_odd_x = swap(to_odd, "gx", 1)
+    from_even_x = swap(to_even, "gx", 0)
     applied = call(
         collect, shape(center.shape, BF16), [VMEM] * 5, [], "collect", 8, 10**8,
-    )(center, from_low, from_high, from_left, from_right)
+    )(center, from_odd_x, from_even_x, from_odd_y, from_even_y)
     return factor, applied
 
 

time: 71.5 us -> 62.9 us (0.88); the launches traced: 71.1 us -> 61.6 us
  starting transfers between devices: 30.2 us -> 19.7 us
  local copies, waits for them, and re-layouts: 1.64 us -> 3.45 us
  waiting for transfers between devices: 11.6 us -> 10.8 us
    ppermute x8, starting transfers between devices: 30.2 us -> 19.7 us  [swap(): return lax.ppermute(value, axis, pairs)]
    unnamed x16, local copies, waits for them, and re-layouts: 0.21 us -> 2.02 us
    ppermute x8, waiting for transfers between devices: 11.6 us -> 10.8 us  [swap(): return lax.ppermute(value, axis, pairs)]
  transfers between devices with their start and end apart: 8 -> 8, of which waited for: 4 -> 4; matrix products, arithmetic and copies ran while one was open for 0% -> 0% of each run, Pallas kernels for 24% -> 28%
where the time goes in v3:
time: 62.9 us; the launch traced here: 61.6 us
  Pallas kernels  26.8 us (43%)
  starting transfers between devices  19.7 us (31%)
  waiting for transfers between devices  10.8 us (17%)
  local copies, waits for them, and re-layouts  3.45 us (5%)
  between operations  0.83 us (1%)
    ppermute x8, starting transfers between devices, swap(): return lax.ppermute(value, axis, pairs)  19.7 us
    pallas_call x1, Pallas kernels, local(): call(inner_all, (shape((bx, by, order, order), BF16), shape((bx, by, orde...  13.6 us
    ppermute x8, waiting for transfers between devices, swap(): return lax.ppermute(value, axis, pairs)  10.8 us
    pallas_call x1, Pallas kernels, local(): call(edge_all, (shape((2 * bx, order, order), BF16), shape((rows * 4, ord...  8.57 us
    pallas_call x1, Pallas kernels, local(): call(inner_gram, (shape((bx * inner, order, order), F32), shape((rows * 4...  3.6 us
    unnamed x16, local copies, waits for them, and re-layouts  2.02 us
    squeeze x1, local copies, waits for them, and re-layouts, local(): even_x = swap(pick(coeffs, (bx - 1) * (1 - px), 0, False), 'gx', 0)  1.38 us
  transfers between devices with their start and end apart: 8, of which 4 were waited for; matrix products, arithmetic and copies ran while one was open for 0% of the time, Pallas kernels for 28%

profile of v3, /device:TPU:25, one launch (start us, length us, event | category | flops | bytes accessed | tf_op | source)
XLA Modules:
  0.0 61.6 jit_solution(9482634968277933025)
XLA Ops:
  0.6 1.4 %dynamic-slice_bitcast_fusion = (bf16[8,256,128]{2,1,0:T(8,128)(2,1)S(1)}, bf16[8,256,128]{2,1,0:T(8,128)(2,1)S(1)}) fusion(bf16[2,8,256,128]{3,2,1,0:T(8,128)(2,1)} %own.1, s32[]{:T(128)S(6)} %select_n.20, s32[]{:T(128)S(6)} %select_n.19), kind=kLoop, calls=%fused_computation | loop fusion | bytes 2097160 | tf_op jit(solution)/shard_map/jit(dynamic_index_in_dim)/squeeze | solution.py:265
  2.0 0.8 %collective-permute-start.1 = (bf16[8,256,128]{2,1,0:T(8,128)(2,1)S(1)}, bf16[8,256,128]{2,1,0:T(8,128)(2,1)S(1)}, u32[]{:S(2)}, u32[]{:S(2)}) collective-permute-start(bf16[8,256,128]{2,1,0:T(8,128)(2,1)S(1)} %get-tuple-element.26), channel_id=1, source_target_pairs={{0,16},{16,0},{32,48},{48,32},{64,80},{80,64},{96,112},{112,96},{1... | collective-permute-start | bytes 1572872 | tf_op jit(solution)/shard_map/ppermute | solution.py:31
  2.8 3.4 %collective-permute-start = (bf16[8,256,128]{2,1,0:T(8,128)(2,1)S(1)}, bf16[8,256,128]{2,1,0:T(8,128)(2,1)S(1)}, u32[]{:S(2)}, u32[]{:S(2)}) collective-permute-start(bf16[8,256,128]{2,1,0:T(8,128)(2,1)S(1)} %get-tuple-element.27), channel_id=1, source_target_pairs={{16,32},{32,16},{48,64},{64,48},{80,96},{96,80},{17,33},{33,17},{4... | collective-permute-start | bytes 1572872 | tf_op jit(solution)/shard_map/ppermute | solution.py:31
  6.3 0.0 copy-start.5
  6.3 0.7 %copy-done.5 = s32[2,8,6]{1,0,2:T(2,128)S(1)} copy-done((s32[2,8,6]{1,0,2:T(2,128)S(1)}, s32[2,8,6]{1,0,2:T(2,128)}, u32[]{:S(2)}) %copy-start.5) | copy-done | bytes 408
  7.0 0.1 copy.12.codes
  7.0 0.6 copy-done.6
  7.6 0.1 copy.13.weights
  7.8 0.0 collective-permute-done.1.even
  7.8 5.8 %collective-permute-done.odd = bf16[8,256,128]{2,1,0:T(8,128)(2,1)S(1)} collective-permute-done((bf16[8,256,128]{2,1,0:T(8,128)(2,1)S(1)}, bf16[8,256,128]{2,1,0:T(8,128)(2,1)S(1)}, u32[]{:S(2)}, u32[]{:S(2)}) %collective-permute-start) | collective-permute-done | bytes 524320 | tf_op jit(solution)/shard_map/ppermute | solution.py:31
  13.6 4.6 %collective-permute-start.2 = (bf16[4,256,128]{2,1,0:T(8,128)(2,1)S(1)}, bf16[4,256,128]{2,1,0:T(8,128)(2,1)S(1)}, u32[]{:S(2)}, u32[]{:S(2)}) collective-permute-start(bf16[4,256,128]{2,1,0:T(8,128)(2,1)S(1)} %pad_maximum_fusion), channel_id=1, source_target_pairs={{1,2},{2,1},{3,4},{4,3},{5,6},{6,5},{7,8},{8,7},{9,10},{10,9},{11,... | collective-permute-start | bytes 786440 | tf_op jit(solution)/shard_map/ppermute | solution.py:31
  18.2 0.0 copy-start.2
  18.2 0.0 copy-start.3
  18.2 0.0 copy-start.4
  18.3 0.0 copy-start.1
  18.3 0.1 collective-permute-start.3
  18.4 0.5 copy-done.2
  18.9 3.6 %inner_gram.1 = (f32[12,128,128]{2,1,0:T(8,128)S(1)}, bf16[16,128,256]{2,1,0:T(8,128)(2,1)S(1)}) custom-call(s32[2,8,6]{2,1,0:T(8,128)S(1)} %copy.12.codes, s32[2,8]{1,0:T(2,128)S(1)} %copy-done.4, f32[2,8,256]{2,1,0:T(8,128)S(1)} %copy-done.2, f32[2,8,128]{2,1,0:T(8,128)S(1)} %copy-done.3, bf16[2,8,256,128]{3,2,1,0:T(8,128)(2,1)S(1)} %copy-done, ...), custom_call_target="tpu_custom_call" | custom-call | flops 4000000000 | bytes 4194304 | tf_op jit(solution)/shard_map/inner_gram/pallas_call | solution.py:268
  22.5 0.3 collective-permute-done.2.odd
  22.9 0.7 %collective-permute-done.3.even = bf16[4,256,128]{2,1,0:T(8,128)(2,1)S(1)} collective-permute-done((bf16[4,256,128]{2,1,0:T(8,128)(2,1)S(1)}, bf16[4,256,128]{2,1,0:T(8,128)(2,1)S(1)}, u32[]{:S(2)}, u32[]{:S(2)}) %collective-permute-start.3) | collective-permute-done | bytes 262176 | tf_op jit(solution)/shard_map/ppermute | solution.py:31
  23.6 8.6 %edge_all.1 = (bf16[4,128,128]{2,1,0:T(8,128)(2,1)S(1)}, f32[16,128,128]{2,1,0:T(8,128)S(1)}, bf16[4,128,128]{2,1,0:T(8,128)(2,1)S(1)}, bf16[4,128,128]{2,1,0:T(8,128)(2,1)S(1)}) custom-call(s32[2,8,6]{2,1,0:T(8,128)S(1)} %copy.12.codes, s32[2,8]{1,0:T(2,128)S(1)} %copy-done.4, f32[2,8,6]{2,1,0:T(8,128)S(1)} %copy.13.weights, f32[2,8,256]{2,1,0:T(8,128)S(1)} %copy-done.2, ...), custom_call_target="tpu_custom_call" | custom-call | flops 8000000000 | bytes 4194304 | tf_op jit(solution)/shard_map/edge_all/pallas_call | solution.py:275
  32.2 3.7 %collective-permute-start.4 = (bf16[4,128,128]{2,1,0:T(8,128)(2,1)S(1)}, bf16[4,128,128]{2,1,0:T(8,128)(2,1)S(1)}, u32[]{:S(2)}, u32[]{:S(2)}) collective-permute-start(bf16[4,128,128]{2,1,0:T(8,128)(2,1)S(1)} %get-tuple-element.20), channel_id=1, source_target_pairs={{1,2},{2,1},{3,4},{4,3},{5,6},{6,5},{7,8},{8,7},{9,10},{10,9},{11,... | collective-permute-start | bytes 393224 | tf_op jit(solution)/shard_map/ppermute | solution.py:31
  35.9 0.1 collective-permute-start.5
  36.0 13.6 %inner_all.1 = (bf16[2,8,128,128]{3,2,1,0:T(8,128)(2,1)}, f32[2,8,128,128]{3,2,1,0:T(8,128)S(1)}, f32[2,8,128,128]{3,2,1,0:T(8,128)S(1)}) custom-call(s32[2,8,6]{2,1,0:T(8,128)S(1)} %copy.12.codes, s32[2,8]{1,0:T(2,128)S(1)} %copy-done.4, f32[2,8,6]{2,1,0:T(8,128)S(1)} %copy.13.weights, f32[12,128,128]{2,1,0:T(8,128)S(1)} %get-tuple-element.13.mats_in, ...), custom_call_target="tpu_custom_call" | custom-call | flops 12000000000 | bytes 4194304 | tf_op jit(solution)/shard_map/inner_all/pallas_call | solution.py:294
  49.6 0.0 collective-permute-done.4.odd.odd_y
  49.6 0.0 collective-permute-done.5.even.even_y
  49.6 0.1 close_halo.1
  49.7 7.0 %collective-permute-start.6 = (bf16[8,128,128]{2,1,0:T(8,128)(2,1)S(1)}, bf16[8,128,128]{2,1,0:T(8,128)(2,1)S(1)}, u32[]{:S(2)}, u32[]{:S(2)}) collective-permute-start(bf16[8,128,128]{2,1,0:T(8,128)(2,1)S(1)} %get-tuple-element.22), channel_id=1, source_target_pairs={{16,32},{32,16},{48,64},{64,48},{80,96},{96,80},{17,33},{33,17},{4... | collective-permute-start | bytes 786440 | tf_op jit(solution)/shard_map/ppermute | solution.py:31
  56.7 0.1 collective-permute-start.7
  56.8 3.9 %collective-permute-done.6.odd_x = bf16[8,128,128]{2,1,0:T(8,128)(2,1)S(1)} collective-permute-done((bf16[8,128,128]{2,1,0:T(8,128)(2,1)S(1)}, bf16[8,128,128]{2,1,0:T(8,128)(2,1)S(1)}, u32[]{:S(2)}, u32[]{:S(2)}) %collective-permute-start.6) | collective-permute-done | bytes 262176 | tf_op jit(solution)/shard_map/ppermute | solution.py:31
  60.7 0.0 collective-permute-done.7.even_x
  60.7 0.9 %collect.1 = bf16[2,8,128,128]{3,2,1,0:T(8,128)(2,1)} custom-call(f32[2,8,128,128]{3,2,1,0:T(8,128)S(1)} %get-tuple-element.18.center, bf16[8,128,128]{2,1,0:T(8,128)(2,1)S(1)} %collective-permute-done.6.odd_x, bf16[8,128,128]{2,1,0:T(8,128)(2,1)S(1)} %collective-permute-done.7.even_x, bf16[4,128,128]{2,1,0:T(8,128)(2,1)S(1)} %collective-permute-done.4.odd.odd_y, ...), custom_call_target="tpu_custom_call" | custom-call | flops 100000000 | bytes 4194304 | tf_op jit(solution)/shard_map/collect/pallas_call | solution.py:316
  (11 shorter events, 0.1 us)
Async XLA Ops:
  0.6 7.1 %copy-start = (bf16[2,8,256,128]{3,2,1,0:T(8,128)(2,1)S(1)}, bf16[2,8,256,128]{3,2,1,0:T(8,128)(2,1)}, u32[]{:S(2)}) copy-start(bf16[2,8,256,128]{3,2,1,0:T(8,128)(2,1)} %own.1) | copy-start | bytes 3145732
  2.0 5.7 %collective-permute-start.1 = (bf16[8,256,128]{2,1,0:T(8,128)(2,1)S(1)}, bf16[8,256,128]{2,1,0:T(8,128)(2,1)S(1)}, u32[]{:S(2)}, u32[]{:S(2)}) collective-permute-start(bf16[8,256,128]{2,1,0:T(8,128)(2,1)S(1)} %get-tuple-element.26), channel_id=1, source_target_pairs={{0,16},{16,0},{32,48},{48,32},{64,80},{80,64},{96,112},{112,96},{1... | collective-permute-start | bytes 1572872 | tf_op jit(solution)/shard_map/ppermute | solution.py:31
  2.8 10.8 %collective-permute-start = (bf16[8,256,128]{2,1,0:T(8,128)(2,1)S(1)}, bf16[8,256,128]{2,1,0:T(8,128)(2,1)S(1)}, u32[]{:S(2)}, u32[]{:S(2)}) collective-permute-start(bf16[8,256,128]{2,1,0:T(8,128)(2,1)S(1)} %get-tuple-element.27), channel_id=1, source_target_pairs={{16,32},{32,16},{48,64},{64,48},{80,96},{96,80},{17,33},{33,17},{4... | collective-permute-start | bytes 1572872 | tf_op jit(solution)/shard_map/ppermute | solution.py:31
  6.3 0.7 %copy-start.5 = (s32[2,8,6]{1,0,2:T(2,128)S(1)}, s32[2,8,6]{1,0,2:T(2,128)}, u32[]{:S(2)}) copy-start(s32[2,8,6]{1,0,2:T(2,128)} %param.10) | copy-start | bytes 1156
  6.9 0.7 %copy-start.6 = (f32[2,8,6]{1,0,2:T(2,128)S(1)}, f32[2,8,6]{1,0,2:T(2,128)}, u32[]{:S(2)}) copy-start(f32[2,8,6]{1,0,2:T(2,128)} %param.12) | copy-start | bytes 1156
  13.6 9.2 %collective-permute-start.2 = (bf16[4,256,128]{2,1,0:T(8,128)(2,1)S(1)}, bf16[4,256,128]{2,1,0:T(8,128)(2,1)S(1)}, u32[]{:S(2)}, u32[]{:S(2)}) collective-permute-start(bf16[4,256,128]{2,1,0:T(8,128)(2,1)S(1)} %pad_maximum_fusion), channel_id=1, source_target_pairs={{1,2},{2,1},{3,4},{4,3},{5,6},{6,5},{7,8},{8,7},{9,10},{10,9},{11,... | collective-permute-start | bytes 786440 | tf_op jit(solution)/shard_map/ppermute | solution.py:31
  18.2 0.7 %copy-start.2 = (f32[2,8,256]{2,1,0:T(8,128)S(1)}, f32[2,8,256]{2,1,0:T(8,128)}, u32[]{:S(2)}) copy-start(f32[2,8,256]{2,1,0:T(8,128)} %permit.3) | copy-start | bytes 49156
  18.2 0.7 %copy-start.3 = (f32[2,8,128]{2,1,0:T(8,128)S(1)}, f32[2,8,128]{2,1,0:T(8,128)}, u32[]{:S(2)}) copy-start(f32[2,8,128]{2,1,0:T(8,128)} %diag.3) | copy-start | bytes 24580
  18.2 0.7 %copy-start.4 = (s32[2,8]{1,0:T(2,128)S(1)}, s32[2,8]{1,0:T(2,128)}, u32[]{:S(2)}) copy-start(s32[2,8]{1,0:T(2,128)} %counts.5) | copy-start | bytes 196
  18.3 5.3 %copy-start.1 = (bf16[2,8,128,128]{3,2,1,0:T(8,128)(2,1)S(1)}, bf16[2,8,128,128]{3,2,1,0:T(8,128)(2,1)}, u32[]{:S(2)}) copy-start(bf16[2,8,128,128]{3,2,1,0:T(8,128)(2,1)} %vectors.3) | copy-start | bytes 1572868
  18.3 5.3 %collective-permute-start.3 = (bf16[4,256,128]{2,1,0:T(8,128)(2,1)S(1)}, bf16[4,256,128]{2,1,0:T(8,128)(2,1)S(1)}, u32[]{:S(2)}, u32[]{:S(2)}) collective-permute-start(bf16[4,256,128]{2,1,0:T(8,128)(2,1)S(1)} %pad_maximum_fusion.1), channel_id=1, source_target_pairs={{0,1},{1,0},{2,3},{3,2},{4,5},{5,4},{6,7},{7,6},{8,9},{9,8},{10,11... | collective-permute-start | bytes 786440 | tf_op jit(solution)/shard_map/ppermute | solution.py:31
  32.2 17.4 %collective-permute-start.4 = (bf16[4,128,128]{2,1,0:T(8,128)(2,1)S(1)}, bf16[4,128,128]{2,1,0:T(8,128)(2,1)S(1)}, u32[]{:S(2)}, u32[]{:S(2)}) collective-permute-start(bf16[4,128,128]{2,1,0:T(8,128)(2,1)S(1)} %get-tuple-element.20), channel_id=1, source_target_pairs={{1,2},{2,1},{3,4},{4,3},{5,6},{6,5},{7,8},{8,7},{9,10},{10,9},{11,... | collective-permute-start | bytes 393224 | tf_op jit(solution)/shard_map/ppermute | solution.py:31
  35.9 13.7 %collective-permute-start.5 = (bf16[4,128,128]{2,1,0:T(8,128)(2,1)S(1)}, bf16[4,128,128]{2,1,0:T(8,128)(2,1)S(1)}, u32[]{:S(2)}, u32[]{:S(2)}) collective-permute-start(bf16[4,128,128]{2,1,0:T(8,128)(2,1)S(1)} %get-tuple-element.21), channel_id=1, source_target_pairs={{0,1},{1,0},{2,3},{3,2},{4,5},{5,4},{6,7},{7,6},{8,9},{9,8},{10,11... | collective-permute-start | bytes 393224 | tf_op jit(solution)/shard_map/ppermute | solution.py:31
  49.7 11.0 %collective-permute-start.6 = (bf16[8,128,128]{2,1,0:T(8,128)(2,1)S(1)}, bf16[8,128,128]{2,1,0:T(8,128)(2,1)S(1)}, u32[]{:S(2)}, u32[]{:S(2)}) collective-permute-start(bf16[8,128,128]{2,1,0:T(8,128)(2,1)S(1)} %get-tuple-element.22), channel_id=1, source_target_pairs={{16,32},{32,16},{48,64},{64,48},{80,96},{96,80},{17,33},{33,17},{4... | collective-permute-start | bytes 786440 | tf_op jit(solution)/shard_map/ppermute | solution.py:31
  56.7 4.0 %collective-permute-start.7 = (bf16[8,128,128]{2,1,0:T(8,128)(2,1)S(1)}, bf16[8,128,128]{2,1,0:T(8,128)(2,1)S(1)}, u32[]{:S(2)}, u32[]{:S(2)}) collective-permute-start(bf16[8,128,128]{2,1,0:T(8,128)(2,1)S(1)} %get-tuple-element.23), channel_id=1, source_target_pairs={{0,16},{16,0},{32,48},{48,32},{64,80},{80,64},{96,112},{112,96},{1... | collective-permute-start | bytes 786440 | tf_op jit(solution)/shard_map/ppermute | solution.py:31

commit v4 on v3

--- a/solution.py
+++ b/solution.py
@@ -6,6 +6,7 @@
 from jax.sharding import PartitionSpec as P
 
 PANEL = 8
+EARLY = 4
 BF16, F32 = jnp.bfloat16, jnp.float32
 VMEM = pl.BlockSpec(memory_space=pltpu.VMEM)
 SMEM = pl.BlockSpec(memory_space=pltpu.SMEM)
@@ -42,7 +43,48 @@
     )
 
 
-def lower_inverse(mat, xs, blocks, order):
+def eliminate(cols, rows, sub):
+    for k in range(PANEL):
+        for n, c in enumerate(cols):
+            inv = 1.0 / c[k][k : k + 1, :]
+            mult = jnp.where(sub > k, c[k] * inv, F32(0.0))
+            for j in range(k + 1, PANEL):
+                c[j] = c[j] - mult * c[j][k : k + 1, :]
+            rows[n] = rows[n] - mult * rows[n][k : k + 1, :]
+    rescale(cols, rows, sub)
+
+
+def rescale(cols, rows, sub):
+    for n, c in enumerate(cols):
+        diag = c[0]
+        for k in range(1, PANEL):
+            diag = jnp.where(sub == k, c[k], diag)
+        rows[n] = rows[n] * lax.rsqrt(diag)
+
+
+def subtract(mat, m, parts, in_diag, order):
+    hi, mid, low = [], [], []
+    for r in parts:
+        h = r.astype(BF16).astype(F32)
+        rest = r - h
+        c = rest.astype(BF16).astype(F32)
+        hi.append(h)
+        mid.append(c)
+        low.append(rest - c)
+    right = jnp.concatenate(hi + mid + hi + low + hi + mid, axis=0).astype(BF16)
+    left = jnp.concatenate(hi + hi + mid + hi + low + mid, axis=0).astype(BF16)
+    update = lax.dot_general(left, right, (((0,), (0,)), ((), ())), preferred_element_type=F32)
+    for t in range(0, order, PANEL):
+        mat[m, t : t + PANEL] = (
+            jnp.where(in_diag, F32(0.0), mat[m, t : t + PANEL]) - update[t : t + PANEL]
+        )
+
+
+def spread(row, picks):
+    return [jnp.take_along_axis(row, pick, axis=1) for pick in picks]
+
+
+def lower_inverse(mat, xs, blocks, order, first, last):
     lane = lax.broadcasted_iota(jnp.int32, (PANEL, order), 1)
     sub = lax.broadcasted_iota(jnp.int32, (PANEL, order), 0)
 
@@ -50,42 +92,62 @@
         r0 = pl.multiple_of(kb * PANEL, PANEL)
         in_diag = (lane >= r0) & (lane < r0 + PANEL)
         unit = jnp.where(lane - r0 == sub, F32(1.0), F32(0.0))
+        picks = [jnp.full((PANEL, order), r0 + k, jnp.int32) for k in range(PANEL)]
         rows = [mat[m, pl.ds(r0, PANEL), :] for m in range(blocks)]
-        picks = [jnp.full((PANEL, order), r0 + k, jnp.int32) for k in range(PANEL)]
-        cols = [[jnp.take_along_axis(r, pick, axis=1) for pick in picks] for r in rows]
+        cols = [spread(r, picks) for r in rows]
         rows = [jnp.where(in_diag, unit, r) for r in rows]
+        eliminate(cols, rows, sub)
+        for m in range(blocks):
+            xs[m, pl.ds(r0, PANEL), :] = rows[m]
+            subtract(mat, m, [rows[m]], in_diag, order)
+        return carry
+
+    lax.fori_loop(first, last, step, 0)
+
+
+def lower_inverse_wide(mat, xs, blocks, order):
+    lane = lax.broadcasted_iota(jnp.int32, (PANEL, order), 1)
+    sub = lax.broadcasted_iota(jnp.int32, (PANEL, order), 0)
+
+    def step(kb, carry):
+        r0 = pl.multiple_of(kb * 2 * PANEL, 2 * PANEL)
+        r1 = pl.multiple_of(r0 + PANEL, PANEL)
+        in_top = (lane >= r0) & (lane < r1)
+        in_bot = (lane >= r1) & (lane < r1 + PANEL)
+        unit_top = jnp.where(lane - r0 == sub, F32(1.0), F32(0.0))
+        unit_bot = jnp.where(lane - r1 == sub, F32(1.0), F32(0.0))
+        picks = [jnp.full((PANEL, order), r0 + k, jnp.int32) for k in range(2 * PANEL)]
+        top = [mat[m, pl.ds(r0, PANEL), :] for m in range(blocks)]
+        bot = [mat[m, pl.ds(r1, PANEL), :] for m in range(blocks)]
+        ctop = [spread(r, picks[:PANEL]) for r in top]
+        cbot = [spread(r, picks[:PANEL]) for r in bot]
+        top = [jnp.where(in_top, unit_top, r) for r in top]
+        bot = [jnp.where(in_top, F32(0.0), r) for r in bot]
         for k in range(PANEL):
             for n in range(blocks):
-                c = cols[n]
+                c, b = ctop[n], cbot[n]
                 inv = 1.0 / c[k][k : k + 1, :]
-                mult = jnp.where(sub > k, c[k] * inv, F32(0.0))
+                m0 = jnp.where(sub > k, c[k] * inv, F32(0.0))
+                m1 = b[k] * inv
                 for j in range(k + 1, PANEL):
-                    c[j] = c[j] - mult * c[j][k : k + 1, :]
-                rows[n] = rows[n] - mult * rows[n][k : k + 1, :]
-        for n in range(blocks):
-            diag = cols[n][0]
-            for k in range(1, PANEL):
-                diag = jnp.where(sub == k, cols[n][k], diag)
-            rows[n] = rows[n] * lax.rsqrt(diag)
+                    row = c[j][k : k + 1, :]
+                    c[j] = c[j] - m0 * row
+                    b[j] = b[j] - m1 * row
+                row = top[n][k : k + 1, :]
+                top[n] = top[n] - m0 * row
+                bot[n] = bot[n] - m1 * row
+        cols = [spread(r, picks[PANEL:]) for r in bot]
+        bot = [jnp.where(in_bot, unit_bot, r) for r in bot]
+        rescale(ctop, top, sub)
+        eliminate(cols, bot, sub)
         for m in range(blocks):
-            r = rows[m]
-            xs[m, pl.ds(r0, PANEL), :] = r
-            hi = r.astype(BF16).astype(F32)
-            rest = r - hi
-            mid = rest.astype(BF16).astype(F32)
-            low = rest - mid
-            right = jnp.concatenate([hi, mid, hi, low, hi, mid], axis=0).astype(BF16)
-            left = jnp.concatenate([hi, hi, mid, hi, low, mid], axis=0).astype(BF16)
-            update = lax.dot_general(
-                left, right, (((0,), (0,)), ((), ())), preferred_element_type=F32
-            )
-            for t in range(0, order, PANEL):
-                mat[m, t : t + PANEL] = (
-                    jnp.where(in_diag, F32(0.0), mat[m, t : t + PANEL]) - update[t : t + PANEL]
-                )
+            upper = jnp.where(in_bot, F32(0.0), top[m])
+            xs[m, pl.ds(r0, PANEL), :] = upper
+            xs[m, pl.ds(r1, PANEL), :] = bot[m]
+            subtract(mat, m, [upper, bot[m]], in_top | in_bot, order)
         return carry
 
-    lax.fori_loop(0, order // PANEL, step, 0)
+    lax.fori_loop(0, order // (2 * PANEL), step, 0)
 
 
 def gram_of(x, y, codes, counts, permit, diag, block_at):
@@ -108,7 +170,7 @@
     return lax.dot_general(factor, vector, (((0,), (0,)), ((), ())), preferred_element_type=F32)
 
 
-def inner_gram(codes, counts, permit, diag, own, odd, even, mats, edge_turned, turned):
+def inner_gram(codes, counts, permit, diag, own, odd, even, mats, xs, edge_turned, turned):
     bx, by = own.shape[0], own.shape[1]
     inner = by - 2
     px = parity("gx")
@@ -134,6 +196,7 @@
         return carry
 
     lax.fori_loop(0, 2 * bx, body, 0)
+    lower_inverse(mats, xs, bx * inner, mats.shape[1], 0, EARLY)
 
 
 def edge_all(
@@ -155,7 +218,7 @@
             x, side * (by - 1), codes, counts, permit, diag,
             lambda dx, dy: turned[(x + dx) * 6 + side * 3 + dy],
         )
-    lower_inverse(mats, xs, len(edges), order)
+    lower_inverse_wide(mats, xs, len(edges), order)
     acc[...] = jnp.zeros(acc.shape, acc.dtype)
     row, lane = iotas(order)
     images = []
@@ -181,14 +244,16 @@
 
 
 def inner_all(
-    codes, counts, weights, mats_in, part, edge_factors, vectors,
+    codes, counts, weights, mats_in, xs_in, part, edge_factors, vectors,
     factor, center, halo, mats, xs, acc,
 ):
     bx, by = vectors.shape[0], vectors.shape[1]
     inner = by - 2
     order = mats.shape[1]
-    mats[...] = mats_in[...]
-    lower_inverse(mats, xs, bx * inner, order)
+    done = EARLY * PANEL
+    mats[:, done:] = mats_in[:, done:]
+    xs[:, :done] = xs_in[:, :done]
+    lower_inverse(mats, xs, bx * inner, order, EARLY, order // PANEL)
     zero = jnp.zeros(acc.shape[1:], F32)
     for p in range(bx + 2):
         for y in range(2, by - 2):
@@ -265,9 +330,13 @@
     even_x = swap(pick(coeffs, (bx - 1) * (1 - px), 0, False), "gx", 0)
     odd_y = swap(column((by - 1) * py), "gy", 1)
     even_y = swap(column((by - 1) * (1 - py)), "gy", 0)
-    mats, edge_turned = call(
+    mats, xs, edge_turned = call(
         inner_gram,
-        (shape((bx * inner, order, order), F32), shape((rows * 4, order, coupling), BF16)),
+        (
+            shape((bx * inner, order, order), F32),
+            shape((bx * inner, order, order), F32),
+            shape((rows * 4, order, coupling), BF16),
+        ),
         [SMEM] * 2 + [VMEM] * 5,
         [pltpu.VMEM((rows * by, order, coupling), BF16)],
         "inner_gram", 16, 4 * 10**9,
@@ -298,14 +367,14 @@
             shape((bx, by, order, width), F32),
             shape((2, by, order, width), F32),
         ),
-        [SMEM] * 3 + [VMEM] * 4,
+        [SMEM] * 3 + [VMEM] * 5,
         [
             pltpu.VMEM((bx * inner, order, order), F32),
             pltpu.VMEM((bx * inner, order, order), F32),
             pltpu.VMEM((rows * by, order, width), F32),
         ],
         "inner_all", 20, 12 * 10**9,
-    )(codes, counts, weights, mats, part, edge_factors, vectors)
+    )(codes, counts, weights, mats, xs, part, edge_factors, vectors)
     to_odd, to_even = call(
         close_halo,
         (shape((by, order, width), BF16), shape((by, order, width), BF16)),

time: 62.9 us -> 59.3 us (0.943)
  the two profiles are of different devices: /device:TPU:25 before, /device:TPU:59 now
where the time goes in v4:
time: 59.3 us; the launch traced here: 58.5 us
  Pallas kernels  25.4 us (43%)
  starting transfers between devices  19.2 us (32%)
  waiting for transfers between devices  10.1 us (17%)
  local copies, waits for them, and re-layouts  2.92 us (5%)
  between operations  0.82 us (1%)
    ppermute x8, starting transfers between devices, swap(): return lax.ppermute(value, axis, pairs)  19.2 us
    pallas_call x1, Pallas kernels, local(): call(inner_all, (shape((bx, by, order, order), BF16), shape((bx, by, orde...  11.2 us
    ppermute x8, waiting for transfers between devices, swap(): return lax.ppermute(value, axis, pairs)  10.1 us
    pallas_call x1, Pallas kernels, local(): call(edge_all, (shape((2 * bx, order, order), BF16), shape((rows * 4, ord...  7.25 us
    pallas_call x1, Pallas kernels, local(): call(inner_gram, (shape((bx * inner, order, order), F32), shape((bx * inn...  6 us
    unnamed x16, local copies, waits for them, and re-layouts  1.49 us
    squeeze x1, local copies, waits for them, and re-layouts, local(): even_x = swap(pick(coeffs, (bx - 1) * (1 - px), 0, False), 'gx', 0)  1.38 us
  transfers between devices with their start and end apart: 8, of which 3 were waited for; matrix products, arithmetic and copies ran while one was open for 0% of the time, Pallas kernels for 29%

profile of v4, /device:TPU:59, one launch (start us, length us, event | category | flops | bytes accessed | tf_op | source)
XLA Modules:
  0.0 58.5 jit_solution(13990067677969951919)
XLA Ops:
  0.6 1.4 %dynamic-slice_bitcast_fusion = (bf16[8,256,128]{2,1,0:T(8,128)(2,1)S(1)}, bf16[8,256,128]{2,1,0:T(8,128)(2,1)S(1)}) fusion(bf16[2,8,256,128]{3,2,1,0:T(8,128)(2,1)} %own.1, s32[]{:T(128)S(6)} %select_n.20, s32[]{:T(128)S(6)} %select_n.19), kind=kLoop, calls=%fused_computation | loop fusion | bytes 2097160 | tf_op jit(solution)/shard_map/jit(dynamic_index_in_dim)/squeeze | solution.py:330
  2.0 0.8 %collective-permute-start.1 = (bf16[8,256,128]{2,1,0:T(8,128)(2,1)S(1)}, bf16[8,256,128]{2,1,0:T(8,128)(2,1)S(1)}, u32[]{:S(2)}, u32[]{:S(2)}) collective-permute-start(bf16[8,256,128]{2,1,0:T(8,128)(2,1)S(1)} %get-tuple-element.28), channel_id=1, source_target_pairs={{0,16},{16,0},{32,48},{48,32},{64,80},{80,64},{96,112},{112,96},{1... | collective-permute-start | bytes 1572872 | tf_op jit(solution)/shard_map/ppermute | solution.py:32
  2.8 3.4 %collective-permute-start = (bf16[8,256,128]{2,1,0:T(8,128)(2,1)S(1)}, bf16[8,256,128]{2,1,0:T(8,128)(2,1)S(1)}, u32[]{:S(2)}, u32[]{:S(2)}) collective-permute-start(bf16[8,256,128]{2,1,0:T(8,128)(2,1)S(1)} %get-tuple-element.29), channel_id=1, source_target_pairs={{16,32},{32,16},{48,64},{64,48},{80,96},{96,80},{17,33},{33,17},{4... | collective-permute-start | bytes 1572872 | tf_op jit(solution)/shard_map/ppermute | solution.py:32
  6.3 0.0 copy-start.5
  6.3 0.7 %copy-done.5 = s32[2,8,6]{1,0,2:T(2,128)S(1)} copy-done((s32[2,8,6]{1,0,2:T(2,128)S(1)}, s32[2,8,6]{1,0,2:T(2,128)}, u32[]{:S(2)}) %copy-start.5) | copy-done | bytes 408
  7.0 0.1 copy.12.codes
  7.0 0.6 %copy-done.6 = f32[2,8,6]{1,0,2:T(2,128)S(1)} copy-done((f32[2,8,6]{1,0,2:T(2,128)S(1)}, f32[2,8,6]{1,0,2:T(2,128)}, u32[]{:S(2)}) %copy-start.6) | copy-done | bytes 408
  7.6 0.1 copy.13.weights
  7.8 0.0 collective-permute-done.1.even
  7.8 5.5 %collective-permute-done.odd = bf16[8,256,128]{2,1,0:T(8,128)(2,1)S(1)} collective-permute-done((bf16[8,256,128]{2,1,0:T(8,128)(2,1)S(1)}, bf16[8,256,128]{2,1,0:T(8,128)(2,1)S(1)}, u32[]{:S(2)}, u32[]{:S(2)}) %collective-permute-start) | collective-permute-done | bytes 524320 | tf_op jit(solution)/shard_map/ppermute | solution.py:32
  13.3 3.1 %collective-permute-start.2 = (bf16[4,256,128]{2,1,0:T(8,128)(2,1)S(1)}, bf16[4,256,128]{2,1,0:T(8,128)(2,1)S(1)}, u32[]{:S(2)}, u32[]{:S(2)}) collective-permute-start(bf16[4,256,128]{2,1,0:T(8,128)(2,1)S(1)} %pad_maximum_fusion), channel_id=1, source_target_pairs={{1,2},{2,1},{3,4},{4,3},{5,6},{6,5},{7,8},{8,7},{9,10},{10,9},{11,... | collective-permute-start | bytes 786440 | tf_op jit(solution)/shard_map/ppermute | solution.py:32
  16.5 0.0 copy-start.2
  16.5 0.0 copy-start.3
  16.5 0.0 copy-start.4
  16.5 0.0 copy-start.1
  16.6 1.8 %collective-permute-start.3 = (bf16[4,256,128]{2,1,0:T(8,128)(2,1)S(1)}, bf16[4,256,128]{2,1,0:T(8,128)(2,1)S(1)}, u32[]{:S(2)}, u32[]{:S(2)}) collective-permute-start(bf16[4,256,128]{2,1,0:T(8,128)(2,1)S(1)} %pad_maximum_fusion.1), channel_id=1, source_target_pairs={{0,1},{1,0},{2,3},{3,2},{4,5},{5,4},{6,7},{7,6},{8,9},{9,8},{10,11... | collective-permute-start | bytes 786440 | tf_op jit(solution)/shard_map/ppermute | solution.py:32
  18.3 0.0 copy-done.3
  18.3 6.0 %inner_gram.1 = (f32[12,128,128]{2,1,0:T(8,128)S(1)}, f32[12,128,128]{2,1,0:T(8,128)S(1)}, bf16[16,128,256]{2,1,0:T(8,128)(2,1)S(1)}) custom-call(s32[2,8,6]{2,1,0:T(8,128)S(1)} %copy.12.codes, s32[2,8]{1,0:T(2,128)S(1)} %copy-done.4, f32[2,8,256]{2,1,0:T(8,128)S(1)} %copy-done.2, f32[2,8,128]{2,1,0:T(8,128)S(1)} %copy-done.3, ...), custom_call_target="tpu_custom_call" | custom-call | flops 4000000000 | bytes 4194304 | tf_op jit(solution)/shard_map/inner_gram/pallas_call | solution.py:333
  24.4 0.0 collective-permute-done.2.odd
  24.4 0.4 collective-permute-done.3.even
  24.8 7.3 %edge_all.1 = (bf16[4,128,128]{2,1,0:T(8,128)(2,1)S(1)}, f32[16,128,128]{2,1,0:T(8,128)S(1)}, bf16[4,128,128]{2,1,0:T(8,128)(2,1)S(1)}, bf16[4,128,128]{2,1,0:T(8,128)(2,1)S(1)}) custom-call(s32[2,8,6]{2,1,0:T(8,128)S(1)} %copy.12.codes, s32[2,8]{1,0:T(2,128)S(1)} %copy-done.4, f32[2,8,6]{2,1,0:T(8,128)S(1)} %copy.13.weights, f32[2,8,256]{2,1,0:T(8,128)S(1)} %copy-done.2, ...), custom_call_target="tpu_custom_call" | custom-call | flops 8000000000 | bytes 4194304 | tf_op jit(solution)/shard_map/edge_all/pallas_call | solution.py:344
  32.0 1.9 %collective-permute-start.4 = (bf16[4,128,128]{2,1,0:T(8,128)(2,1)S(1)}, bf16[4,128,128]{2,1,0:T(8,128)(2,1)S(1)}, u32[]{:S(2)}, u32[]{:S(2)}) collective-permute-start(bf16[4,128,128]{2,1,0:T(8,128)(2,1)S(1)} %get-tuple-element.22), channel_id=1, source_target_pairs={{1,2},{2,1},{3,4},{4,3},{5,6},{6,5},{7,8},{8,7},{9,10},{10,9},{11,... | collective-permute-start | bytes 393224 | tf_op jit(solution)/shard_map/ppermute | solution.py:32
  33.9 3.5 %collective-permute-start.5 = (bf16[4,128,128]{2,1,0:T(8,128)(2,1)S(1)}, bf16[4,128,128]{2,1,0:T(8,128)(2,1)S(1)}, u32[]{:S(2)}, u32[]{:S(2)}) collective-permute-start(bf16[4,128,128]{2,1,0:T(8,128)(2,1)S(1)} %get-tuple-element.23), channel_id=1, source_target_pairs={{0,1},{1,0},{2,3},{3,2},{4,5},{5,4},{6,7},{7,6},{8,9},{9,8},{10,11... | collective-permute-start | bytes 393224 | tf_op jit(solution)/shard_map/ppermute | solution.py:32
  37.4 11.2 %inner_all.1 = (bf16[2,8,128,128]{3,2,1,0:T(8,128)(2,1)}, f32[2,8,128,128]{3,2,1,0:T(8,128)S(1)}, f32[2,8,128,128]{3,2,1,0:T(8,128)S(1)}) custom-call(s32[2,8,6]{2,1,0:T(8,128)S(1)} %copy.12.codes, s32[2,8]{1,0:T(2,128)S(1)} %copy-done.4, f32[2,8,6]{2,1,0:T(8,128)S(1)} %copy.13.weights, f32[12,128,128]{2,1,0:T(8,128)S(1)} %get-tuple-element.14.mats_in, ...), custom_call_target="tpu_custom_call" | custom-call | flops 12000000000 | bytes 4194304 | tf_op jit(solution)/shard_map/inner_all/pallas_call | solution.py:363
  48.6 0.0 collective-permute-done.4.odd.odd_y
  48.6 0.0 collective-permute-done.5.even.even_y
  48.6 0.1 close_halo.1
  48.7 4.6 %collective-permute-start.6 = (bf16[8,128,128]{2,1,0:T(8,128)(2,1)S(1)}, bf16[8,128,128]{2,1,0:T(8,128)(2,1)S(1)}, u32[]{:S(2)}, u32[]{:S(2)}) collective-permute-start(bf16[8,128,128]{2,1,0:T(8,128)(2,1)S(1)} %get-tuple-element.24), channel_id=1, source_target_pairs={{16,32},{32,16},{48,64},{64,48},{80,96},{96,80},{17,33},{33,17},{4... | collective-permute-start | bytes 786440 | tf_op jit(solution)/shard_map/ppermute | solution.py:32
  53.3 0.1 collective-permute-start.7
  53.4 4.2 %collective-permute-done.6.odd_x = bf16[8,128,128]{2,1,0:T(8,128)(2,1)S(1)} collective-permute-done((bf16[8,128,128]{2,1,0:T(8,128)(2,1)S(1)}, bf16[8,128,128]{2,1,0:T(8,128)(2,1)S(1)}, u32[]{:S(2)}, u32[]{:S(2)}) %collective-permute-start.6) | collective-permute-done | bytes 262176 | tf_op jit(solution)/shard_map/ppermute | solution.py:32
  57.6 0.0 collective-permute-done.7.even_x
  57.6 0.9 %collect.1 = bf16[2,8,128,128]{3,2,1,0:T(8,128)(2,1)} custom-call(f32[2,8,128,128]{3,2,1,0:T(8,128)S(1)} %get-tuple-element.20.center, bf16[8,128,128]{2,1,0:T(8,128)(2,1)S(1)} %collective-permute-done.6.odd_x, bf16[8,128,128]{2,1,0:T(8,128)(2,1)S(1)} %collective-permute-done.7.even_x, bf16[4,128,128]{2,1,0:T(8,128)(2,1)S(1)} %collective-permute-done.4.odd.odd_y, ...), custom_call_target="tpu_custom_call" | custom-call | flops 100000000 | bytes 4194304 | tf_op jit(solution)/shard_map/collect/pallas_call | solution.py:385
  (11 shorter events, 0.1 us)
Async XLA Ops:
  0.6 7.1 %copy-start = (bf16[2,8,256,128]{3,2,1,0:T(8,128)(2,1)S(1)}, bf16[2,8,256,128]{3,2,1,0:T(8,128)(2,1)}, u32[]{:S(2)}) copy-start(bf16[2,8,256,128]{3,2,1,0:T(8,128)(2,1)} %own.1) | copy-start | bytes 3145732
  2.0 5.7 %collective-permute-start.1 = (bf16[8,256,128]{2,1,0:T(8,128)(2,1)S(1)}, bf16[8,256,128]{2,1,0:T(8,128)(2,1)S(1)}, u32[]{:S(2)}, u32[]{:S(2)}) collective-permute-start(bf16[8,256,128]{2,1,0:T(8,128)(2,1)S(1)} %get-tuple-element.28), channel_id=1, source_target_pairs={{0,16},{16,0},{32,48},{48,32},{64,80},{80,64},{96,112},{112,96},{1... | collective-permute-start | bytes 1572872 | tf_op jit(solution)/shard_map/ppermute | solution.py:32
  2.8 10.5 %collective-permute-start = (bf16[8,256,128]{2,1,0:T(8,128)(2,1)S(1)}, bf16[8,256,128]{2,1,0:T(8,128)(2,1)S(1)}, u32[]{:S(2)}, u32[]{:S(2)}) collective-permute-start(bf16[8,256,128]{2,1,0:T(8,128)(2,1)S(1)} %get-tuple-element.29), channel_id=1, source_target_pairs={{16,32},{32,16},{48,64},{64,48},{80,96},{96,80},{17,33},{33,17},{4... | collective-permute-start | bytes 1572872 | tf_op jit(solution)/shard_map/ppermute | solution.py:32
  6.3 0.7 %copy-start.5 = (s32[2,8,6]{1,0,2:T(2,128)S(1)}, s32[2,8,6]{1,0,2:T(2,128)}, u32[]{:S(2)}) copy-start(s32[2,8,6]{1,0,2:T(2,128)} %param.10) | copy-start | bytes 1156
  6.9 0.7 %copy-start.6 = (f32[2,8,6]{1,0,2:T(2,128)S(1)}, f32[2,8,6]{1,0,2:T(2,128)}, u32[]{:S(2)}) copy-start(f32[2,8,6]{1,0,2:T(2,128)} %param.12) | copy-start | bytes 1156
  13.3 11.0 %collective-permute-start.2 = (bf16[4,256,128]{2,1,0:T(8,128)(2,1)S(1)}, bf16[4,256,128]{2,1,0:T(8,128)(2,1)S(1)}, u32[]{:S(2)}, u32[]{:S(2)}) collective-permute-start(bf16[4,256,128]{2,1,0:T(8,128)(2,1)S(1)} %pad_maximum_fusion), channel_id=1, source_target_pairs={{1,2},{2,1},{3,4},{4,3},{5,6},{6,5},{7,8},{8,7},{9,10},{10,9},{11,... | collective-permute-start | bytes 786440 | tf_op jit(solution)/shard_map/ppermute | solution.py:32
  16.5 1.9 %copy-start.2 = (f32[2,8,256]{2,1,0:T(8,128)S(1)}, f32[2,8,256]{2,1,0:T(8,128)}, u32[]{:S(2)}) copy-start(f32[2,8,256]{2,1,0:T(8,128)} %permit.3) | copy-start | bytes 49156
  16.5 1.9 %copy-start.3 = (f32[2,8,128]{2,1,0:T(8,128)S(1)}, f32[2,8,128]{2,1,0:T(8,128)}, u32[]{:S(2)}) copy-start(f32[2,8,128]{2,1,0:T(8,128)} %diag.3) | copy-start | bytes 24580
  16.5 1.9 %copy-start.4 = (s32[2,8]{1,0:T(2,128)S(1)}, s32[2,8]{1,0:T(2,128)}, u32[]{:S(2)}) copy-start(s32[2,8]{1,0:T(2,128)} %counts.5) | copy-start | bytes 196
  16.5 8.2 %copy-start.1 = (bf16[2,8,128,128]{3,2,1,0:T(8,128)(2,1)S(1)}, bf16[2,8,128,128]{3,2,1,0:T(8,128)(2,1)}, u32[]{:S(2)}) copy-start(bf16[2,8,128,128]{3,2,1,0:T(8,128)(2,1)} %vectors.3) | copy-start | bytes 1572868
  16.6 8.2 %collective-permute-start.3 = (bf16[4,256,128]{2,1,0:T(8,128)(2,1)S(1)}, bf16[4,256,128]{2,1,0:T(8,128)(2,1)S(1)}, u32[]{:S(2)}, u32[]{:S(2)}) collective-permute-start(bf16[4,256,128]{2,1,0:T(8,128)(2,1)S(1)} %pad_maximum_fusion.1), channel_id=1, source_target_pairs={{0,1},{1,0},{2,3},{3,2},{4,5},{5,4},{6,7},{7,6},{8,9},{9,8},{10,11... | collective-permute-start | bytes 786440 | tf_op jit(solution)/shard_map/ppermute | solution.py:32
  32.0 16.6 %collective-permute-start.4 = (bf16[4,128,128]{2,1,0:T(8,128)(2,1)S(1)}, bf16[4,128,128]{2,1,0:T(8,128)(2,1)S(1)}, u32[]{:S(2)}, u32[]{:S(2)}) collective-permute-start(bf16[4,128,128]{2,1,0:T(8,128)(2,1)S(1)} %get-tuple-element.22), channel_id=1, source_target_pairs={{1,2},{2,1},{3,4},{4,3},{5,6},{6,5},{7,8},{8,7},{9,10},{10,9},{11,... | collective-permute-start | bytes 393224 | tf_op jit(solution)/shard_map/ppermute | solution.py:32
  33.9 14.7 %collective-permute-start.5 = (bf16[4,128,128]{2,1,0:T(8,128)(2,1)S(1)}, bf16[4,128,128]{2,1,0:T(8,128)(2,1)S(1)}, u32[]{:S(2)}, u32[]{:S(2)}) collective-permute-start(bf16[4,128,128]{2,1,0:T(8,128)(2,1)S(1)} %get-tuple-element.23), channel_id=1, source_target_pairs={{0,1},{1,0},{2,3},{3,2},{4,5},{5,4},{6,7},{7,6},{8,9},{9,8},{10,11... | collective-permute-start | bytes 393224 | tf_op jit(solution)/shard_map/ppermute | solution.py:32
  48.7 8.9 %collective-permute-start.6 = (bf16[8,128,128]{2,1,0:T(8,128)(2,1)S(1)}, bf16[8,128,128]{2,1,0:T(8,128)(2,1)S(1)}, u32[]{:S(2)}, u32[]{:S(2)}) collective-permute-start(bf16[8,128,128]{2,1,0:T(8,128)(2,1)S(1)} %get-tuple-element.24), channel_id=1, source_target_pairs={{16,32},{32,16},{48,64},{64,48},{80,96},{96,80},{17,33},{33,17},{4... | collective-permute-start | bytes 786440 | tf_op jit(solution)/shard_map/ppermute | solution.py:32
  53.3 4.3 %collective-permute-start.7 = (bf16[8,128,128]{2,1,0:T(8,128)(2,1)S(1)}, bf16[8,128,128]{2,1,0:T(8,128)(2,1)S(1)}, u32[]{:S(2)}, u32[]{:S(2)}) collective-permute-start(bf16[8,128,128]{2,1,0:T(8,128)(2,1)S(1)} %get-tuple-element.25), channel_id=1, source_target_pairs={{0,16},{16,0},{32,48},{48,32},{64,80},{80,64},{96,112},{112,96},{1... | collective-permute-start | bytes 786440 | tf_op jit(solution)/shard_map/ppermute | solution.py:32

commit v5 on v4

--- a/solution.py
+++ b/solution.py
@@ -170,7 +170,7 @@
     return lax.dot_general(factor, vector, (((0,), (0,)), ((), ())), preferred_element_type=F32)
 
 
-def inner_gram(codes, counts, permit, diag, own, odd, even, mats, xs, edge_turned, turned):
+def inner_gram(codes, counts, permit, diag, own, odd, even, mats, xs, turned):
     bx, by = own.shape[0], own.shape[1]
     inner = by - 2
     px = parity("gx")
@@ -179,9 +179,6 @@
         turned[(1 - px) * (bx + 1) * by + y] = even[y].T
         for x in range(bx):
             turned[(x + 1) * by + y] = own[x, y].T
-    for p in range(bx + 2):
-        for n, y in enumerate((0, 1, by - 2, by - 1)):
-            edge_turned[p * 4 + n] = turned[p * by + y]
 
     def some(x, g):
         for u in range(inner // 2):
@@ -200,8 +197,8 @@
 
 
 def edge_all(
-    codes, counts, weights, permit, diag, edge_turned, odd, even, vectors,
-    factors, part, to_odd, to_even, turned, mats, xs, acc,
+    codes, counts, weights, permit, diag, inner_turned, odd, even, vectors,
+    factors, acc, to_odd, to_even, turned, mats, xs,
 ):
     bx, by = vectors.shape[0], vectors.shape[1]
     order = mats.shape[1]
@@ -210,8 +207,8 @@
         row = px * (bx + 1) if p == 0 else (1 - px) * (bx + 1) if p == bx + 1 else p
         turned[row * 6 + 5 * py] = odd[p].T
         turned[row * 6 + 5 * (1 - py)] = even[p].T
-        for n in range(4):
-            turned[p * 6 + 1 + n] = edge_turned[p * 4 + n]
+        for n, y in enumerate((0, 1, by - 2, by - 1)):
+            turned[p * 6 + 1 + n] = inner_turned[p * by + y]
     edges = [(x, side) for x in range(bx) for side in range(2)]
     for m, (x, side) in enumerate(edges):
         mats[m] = gram_of(
@@ -239,13 +236,11 @@
     for p in range(bx + 2):
         to_odd[p] = acc[p * 6 + 5 * py].astype(BF16)
         to_even[p] = acc[p * 6 + 5 * (1 - py)].astype(BF16)
-        for n in range(4):
-            part[p * 4 + n] = acc[p * 6 + 1 + n]
 
 
 def inner_all(
-    codes, counts, weights, mats_in, xs_in, part, edge_factors, vectors,
-    factor, center, halo, mats, xs, acc,
+    codes, counts, weights, mats_in, xs_in, edge_acc, edge_factors, vectors,
+    factor, acc, mats, xs,
 ):
     bx, by = vectors.shape[0], vectors.shape[1]
     inner = by - 2
@@ -259,7 +254,7 @@
         for y in range(2, by - 2):
             acc[p * by + y] = zero
         for n, y in enumerate((0, 1, by - 2, by - 1)):
-            acc[p * by + y] = part[p * 4 + n]
+            acc[p * by + y] = edge_acc[p * 6 + 1 + n]
     for x in range(bx):
         factor[x, 0] = edge_factors[2 * x]
         factor[x, by - 1] = edge_factors[2 * x + 1]
@@ -286,32 +281,29 @@
         return carry
 
     lax.fori_loop(0, bx * inner // 2, body, 0)
-    for y in range(by):
-        halo[0, y] = acc[y]
-        halo[1, y] = acc[(bx + 1) * by + y]
-        for x in range(bx):
-            center[x, y] = acc[(x + 1) * by + y]
-
-
-def close_halo(halo, odd, even, to_odd, to_even):
-    by = halo.shape[1]
+
+
+def close_halo(acc, odd, even, to_odd, to_even):
+    by = to_odd.shape[0]
     last = odd.shape[0] - 1
     px, py = parity("gx"), parity("gy")
     for out, h in ((to_odd, px), (to_even, 1 - px)):
+        row = h * last * by
         for y in range(1, by - 1):
-            out[y] = halo[h, y].astype(BF16)
+            out[y] = acc[row + y].astype(BF16)
         for terms, y in ((odd, (by - 1) * py), (even, (by - 1) * (1 - py))):
-            out[y] = (halo[h, y] + terms[h * last].astype(F32)).astype(BF16)
-
-
-def collect(center, odd_x, even_x, odd_y, even_y, out):
-    bx, by = center.shape[0], center.shape[1]
+            out[y] = (acc[row + y] + terms[h * last].astype(F32)).astype(BF16)
+
+
+def collect(acc, odd_x, even_x, odd_y, even_y, out):
+    bx, by = out.shape[0], out.shape[1]
     px, py = parity("gx"), parity("gy")
     for terms, x in ((odd_x, (bx - 1) * px), (even_x, (bx - 1) * (1 - px))):
+        row = (x + 1) * by
         for y in range(1, by - 1):
-            out[x, y] = (center[x, y] + terms[y].astype(F32)).astype(BF16)
+            out[x, y] = (acc[row + y] + terms[y].astype(F32)).astype(BF16)
         for more, y in ((odd_y, (by - 1) * py), (even_y, (by - 1) * (1 - py))):
-            v = center[x, y] + terms[y].astype(F32) + more[x + 1].astype(F32)
+            v = acc[row + y] + terms[y].astype(F32) + more[x + 1].astype(F32)
             out[x, y] = v.astype(BF16)
 
 
@@ -326,26 +318,27 @@
     def column(y):
         return jnp.concatenate([pick(odd_x, y, 0), pick(coeffs, y, 1, False), pick(even_x, y, 0)])
 
+    again = lax.optimization_barrier(coeffs)
+    even_x = swap(pick(again, (bx - 1) * (1 - px), 0, False), "gx", 0)
     odd_x = swap(pick(coeffs, (bx - 1) * px, 0, False), "gx", 1)
-    even_x = swap(pick(coeffs, (bx - 1) * (1 - px), 0, False), "gx", 0)
     odd_y = swap(column((by - 1) * py), "gy", 1)
     even_y = swap(column((by - 1) * (1 - py)), "gy", 0)
-    mats, xs, edge_turned = call(
+    mats, xs, turned = call(
         inner_gram,
         (
             shape((bx * inner, order, order), F32),
             shape((bx * inner, order, order), F32),
-            shape((rows * 4, order, coupling), BF16),
+            shape((rows * by, order, coupling), BF16),
         ),
         [SMEM] * 2 + [VMEM] * 5,
-        [pltpu.VMEM((rows * by, order, coupling), BF16)],
+        [],
         "inner_gram", 16, 4 * 10**9,
     )(codes, counts, permit, diag, coeffs, odd_x, even_x)
-    edge_factors, part, to_odd, to_even = call(
+    edge_factors, edge_acc, to_odd, to_even = call(
         edge_all,
         (
             shape((2 * bx, order, order), BF16),
-            shape((rows * 4, order, width), F32),
+            shape((rows * 6, order, width), F32),
             shape((rows, order, width), BF16),
             shape((rows, order, width), BF16),
         ),
@@ -354,37 +347,34 @@
             pltpu.VMEM((rows * 6, order, coupling), BF16),
             pltpu.VMEM((2 * bx, order, order), F32),
             pltpu.VMEM((2 * bx, order, order), F32),
-            pltpu.VMEM((rows * 6, order, width), F32),
         ],
         "edge_all", 16, 8 * 10**9,
-    )(codes, counts, weights, permit, diag, edge_turned, odd_y, even_y, vectors)
+    )(codes, counts, weights, permit, diag, turned, odd_y, even_y, vectors)
     from_odd_y = swap(to_odd, "gy", 1)
     from_even_y = swap(to_even, "gy", 0)
-    factor, center, halo = call(
+    factor, acc = call(
         inner_all,
         (
             shape((bx, by, order, order), BF16),
-            shape((bx, by, order, width), F32),
-            shape((2, by, order, width), F32),
+            shape((rows * by, order, width), F32),
         ),
         [SMEM] * 3 + [VMEM] * 5,
         [
             pltpu.VMEM((bx * inner, order, order), F32),
             pltpu.VMEM((bx * inner, order, order), F32),
-            pltpu.VMEM((rows * by, order, width), F32),
         ],
         "inner_all", 20, 12 * 10**9,
-    )(codes, counts, weights, mats, xs, part, edge_factors, vectors)
+    )(codes, counts, weights, mats, xs, edge_acc, edge_factors, vectors)
     to_odd, to_even = call(
         close_halo,
         (shape((by, order, width), BF16), shape((by, order, width), BF16)),
         [VMEM] * 3, [], "close_halo", 8, 10**8,
-    )(halo, from_odd_y, from_even_y)
+    )(acc, from_odd_y, from_even_y)
     from_odd_x = swap(to_odd, "gx", 1)
     from_even_x = swap(to_even, "gx", 0)
     applied = call(
-        collect, shape(center.shape, BF16), [VMEM] * 5, [], "collect", 8, 10**8,
-    )(center, from_odd_x, from_even_x, from_odd_y, from_even_y)
+        collect, shape((bx, by, order, width), BF16), [VMEM] * 5, [], "collect", 8, 10**8,
+    )(acc, from_odd_x, from_even_x, from_odd_y, from_even_y)
     return factor, applied
 
 

time: 59.3 us -> 58.5 us (0.987)
  the two profiles are of different devices: /device:TPU:59 before, /device:TPU:25 now
where the time goes in v5:
time: 58.5 us; the launch traced here: 57.8 us
  Pallas kernels  25.5 us (44%)
  starting transfers between devices  19.4 us (33%)
  waiting for transfers between devices  9.41 us (16%)
  local copies, waits for them, and re-layouts  2.49 us (4%)
  between operations  0.9 us (2%)
    ppermute x8, starting transfers between devices, swap(): return lax.ppermute(value, axis, pairs)  19.4 us
    pallas_call x1, Pallas kernels, local(): call(inner_all, (shape((bx, by, order, order), BF16), shape((rows * by, o...  11.4 us
    ppermute x8, waiting for transfers between devices, swap(): return lax.ppermute(value, axis, pairs)  9.41 us
    pallas_call x1, Pallas kernels, local(): call(edge_all, (shape((2 * bx, order, order), BF16), shape((rows * 6, ord...  7.14 us
    pallas_call x1, Pallas kernels, local(): call(inner_gram, (shape((bx * inner, order, order), F32), shape((bx * inn...  5.98 us
  transfers between devices with their start and end apart: 8, of which 2 were waited for; matrix products, arithmetic and copies ran while one was open for 2% of the time, Pallas kernels for 30%

profile of v5, /device:TPU:25, one launch (start us, length us, event | category | flops | bytes accessed | tf_op | source)
XLA Modules:
  0.0 57.8 jit_solution(315479501270177423)
XLA Ops:
  0.6 0.0 copy-start
  0.6 0.0 copy-start.5
  0.7 0.0 copy-start.6
  0.7 0.0 copy-start.2
  0.7 0.0 copy-start.3
  0.7 1.2 %dynamic-slice_bitcast_fusion.1 = bf16[8,256,128]{2,1,0:T(8,128)(2,1)S(1)} fusion(bf16[2,8,256,128]{3,2,1,0:T(8,128)(2,1)} %own.1, s32[]{:T(128)S(6)} %select_n.19), kind=kLoop, calls=%fused_computation.1 | loop fusion | bytes 1048580 | tf_op jit(solution)/shard_map/jit(dynamic_index_in_dim)/squeeze | solution.py:323
  1.9 4.1 %collective-permute-start = (bf16[8,256,128]{2,1,0:T(8,128)(2,1)S(1)}, bf16[8,256,128]{2,1,0:T(8,128)(2,1)S(1)}, u32[]{:S(2)}, u32[]{:S(2)}) collective-permute-start(bf16[8,256,128]{2,1,0:T(8,128)(2,1)S(1)} %dynamic-slice_bitcast_fusion.1), channel_id=1, source_target_pairs={{16,32},{32,16},{48,64},{64,48},{80,96},{96,80},{17,33},{33,17},{4... | collective-permute-start | bytes 1572872 | tf_op jit(solution)/shard_map/ppermute | solution.py:32
  6.0 1.1 %dynamic-slice_bitcast_fusion = bf16[8,256,128]{2,1,0:T(8,128)(2,1)S(1)} fusion(bf16[2,8,256,128]{3,2,1,0:T(8,128)(2,1)} %own.1, s32[]{:T(128)S(6)} %select_n.20), kind=kLoop, calls=%fused_computation | loop fusion | bytes 1048580 | tf_op jit(solution)/shard_map/jit(dynamic_index_in_dim)/squeeze | solution.py:322
  7.1 0.1 collective-permute-start.1
  7.2 0.1 copy.12.codes
  7.3 0.0 copy-done.6
  7.3 0.1 copy.13.weights
  7.4 5.4 %collective-permute-done.odd = bf16[8,256,128]{2,1,0:T(8,128)(2,1)S(1)} collective-permute-done((bf16[8,256,128]{2,1,0:T(8,128)(2,1)S(1)}, bf16[8,256,128]{2,1,0:T(8,128)(2,1)S(1)}, u32[]{:S(2)}, u32[]{:S(2)}) %collective-permute-start) | collective-permute-done | bytes 524320 | tf_op jit(solution)/shard_map/ppermute | solution.py:32
  12.8 0.0 collective-permute-done.1.even
  12.9 4.6 %collective-permute-start.2 = (bf16[4,256,128]{2,1,0:T(8,128)(2,1)S(1)}, bf16[4,256,128]{2,1,0:T(8,128)(2,1)S(1)}, u32[]{:S(2)}, u32[]{:S(2)}) collective-permute-start(bf16[4,256,128]{2,1,0:T(8,128)(2,1)S(1)} %pad_maximum_fusion), channel_id=1, source_target_pairs={{1,2},{2,1},{3,4},{4,3},{5,6},{6,5},{7,8},{8,7},{9,10},{10,9},{11,... | collective-permute-start | bytes 786440 | tf_op jit(solution)/shard_map/ppermute | solution.py:32
  17.5 0.0 copy-start.1
  17.5 0.1 collective-permute-start.3
  17.7 6.0 %inner_gram.1 = (f32[12,128,128]{2,1,0:T(8,128)S(1)}, f32[12,128,128]{2,1,0:T(8,128)S(1)}, bf16[32,128,256]{2,1,0:T(8,128)(2,1)S(1)}) custom-call(s32[2,8,6]{2,1,0:T(8,128)S(1)} %copy.12.codes, s32[2,8]{1,0:T(2,128)S(1)} %copy-done.4, f32[2,8,256]{2,1,0:T(8,128)S(1)} %copy-done.2, f32[2,8,128]{2,1,0:T(8,128)S(1)} %copy-done.3, ...), custom_call_target="tpu_custom_call" | custom-call | flops 4000000000 | bytes 4194304 | tf_op jit(solution)/shard_map/inner_gram/pallas_call | solution.py:326
  23.7 0.0 collective-permute-done.2.odd
  23.7 0.0 collective-permute-done.3.even
  23.7 7.1 %edge_all.1 = (bf16[4,128,128]{2,1,0:T(8,128)(2,1)S(1)}, f32[24,128,128]{2,1,0:T(8,128)S(1)}, bf16[4,128,128]{2,1,0:T(8,128)(2,1)S(1)}, bf16[4,128,128]{2,1,0:T(8,128)(2,1)S(1)}) custom-call(s32[2,8,6]{2,1,0:T(8,128)S(1)} %copy.12.codes, s32[2,8]{1,0:T(2,128)S(1)} %copy-done.4, f32[2,8,6]{2,1,0:T(8,128)S(1)} %copy.13.weights, f32[2,8,256]{2,1,0:T(8,128)S(1)} %copy-done.2, ...), custom_call_target="tpu_custom_call" | custom-call | flops 8000000000 | bytes 4194304 | tf_op jit(solution)/shard_map/edge_all/pallas_call | solution.py:337
  30.8 3.0 %collective-permute-start.4 = (bf16[4,128,128]{2,1,0:T(8,128)(2,1)S(1)}, bf16[4,128,128]{2,1,0:T(8,128)(2,1)S(1)}, u32[]{:S(2)}, u32[]{:S(2)}) collective-permute-start(bf16[4,128,128]{2,1,0:T(8,128)(2,1)S(1)} %get-tuple-element.20), channel_id=1, source_target_pairs={{1,2},{2,1},{3,4},{4,3},{5,6},{6,5},{7,8},{8,7},{9,10},{10,9},{11,... | collective-permute-start | bytes 393224 | tf_op jit(solution)/shard_map/ppermute | solution.py:32
  33.8 0.6 %collective-permute-start.5 = (bf16[4,128,128]{2,1,0:T(8,128)(2,1)S(1)}, bf16[4,128,128]{2,1,0:T(8,128)(2,1)S(1)}, u32[]{:S(2)}, u32[]{:S(2)}) collective-permute-start(bf16[4,128,128]{2,1,0:T(8,128)(2,1)S(1)} %get-tuple-element.21), channel_id=1, source_target_pairs={{0,1},{1,0},{2,3},{3,2},{4,5},{5,4},{6,7},{7,6},{8,9},{9,8},{10,11... | collective-permute-start | bytes 393224 | tf_op jit(solution)/shard_map/ppermute | solution.py:32
  34.4 11.4 %inner_all.1 = (bf16[2,8,128,128]{3,2,1,0:T(8,128)(2,1)}, f32[32,128,128]{2,1,0:T(8,128)S(1)}) custom-call(s32[2,8,6]{2,1,0:T(8,128)S(1)} %copy.12.codes, s32[2,8]{1,0:T(2,128)S(1)} %copy-done.4, f32[2,8,6]{2,1,0:T(8,128)S(1)} %copy.13.weights, f32[12,128,128]{2,1,0:T(8,128)S(1)} %get-tuple-element.13.mats_in, f32[12,128,128]{2,1,0:T(8,128)S(1)} %get-tuple-element.14.xs_in, ...), custom_call_target="tpu_custom_call" | custom-call | flops 12000000000 | bytes 4194304 | tf_op jit(solution)/shard_map/inner_all/pallas_call | solution.py:355
  45.8 0.0 collective-permute-done.4.odd.odd_y
  45.8 0.0 collective-permute-done.5.even.even_y
  45.8 0.1 close_halo.1
  45.9 6.9 %collective-permute-start.6 = (bf16[8,128,128]{2,1,0:T(8,128)(2,1)S(1)}, bf16[8,128,128]{2,1,0:T(8,128)(2,1)S(1)}, u32[]{:S(2)}, u32[]{:S(2)}) collective-permute-start(bf16[8,128,128]{2,1,0:T(8,128)(2,1)S(1)} %get-tuple-element.22), channel_id=1, source_target_pairs={{16,32},{32,16},{48,64},{64,48},{80,96},{96,80},{17,33},{33,17},{4... | collective-permute-start | bytes 786440 | tf_op jit(solution)/shard_map/ppermute | solution.py:32
  52.8 0.1 collective-permute-start.7
  52.9 3.9 %collective-permute-done.6.odd_x = bf16[8,128,128]{2,1,0:T(8,128)(2,1)S(1)} collective-permute-done((bf16[8,128,128]{2,1,0:T(8,128)(2,1)S(1)}, bf16[8,128,128]{2,1,0:T(8,128)(2,1)S(1)}, u32[]{:S(2)}, u32[]{:S(2)}) %collective-permute-start.6) | collective-permute-done | bytes 262176 | tf_op jit(solution)/shard_map/ppermute | solution.py:32
  56.9 0.0 collective-permute-done.7.even_x
  56.9 0.9 %collect.1 = bf16[2,8,128,128]{3,2,1,0:T(8,128)(2,1)} custom-call(f32[32,128,128]{2,1,0:T(8,128)S(1)} %get-tuple-element.19.acc, bf16[8,128,128]{2,1,0:T(8,128)(2,1)S(1)} %collective-permute-done.6.odd_x, bf16[8,128,128]{2,1,0:T(8,128)(2,1)S(1)} %collective-permute-done.7.even_x, bf16[4,128,128]{2,1,0:T(8,128)(2,1)S(1)} %collective-permute-done.4.odd.odd_y, ...), custom_call_target="tpu_custom_call" | custom-call | flops 100000000 | bytes 4194304 | tf_op jit(solution)/shard_map/collect/pallas_call | solution.py:375
  (12 shorter events, 0.1 us)
Async XLA Ops:
  0.6 6.7 %copy-start = (bf16[2,8,256,128]{3,2,1,0:T(8,128)(2,1)S(1)}, bf16[2,8,256,128]{3,2,1,0:T(8,128)(2,1)}, u32[]{:S(2)}) copy-start(bf16[2,8,256,128]{3,2,1,0:T(8,128)(2,1)} %own.1) | copy-start | bytes 3145732
  0.6 6.5 %copy-start.5 = (s32[2,8,6]{1,0,2:T(2,128)S(1)}, s32[2,8,6]{1,0,2:T(2,128)}, u32[]{:S(2)}) copy-start(s32[2,8,6]{1,0,2:T(2,128)} %param.10) | copy-start | bytes 1156
  0.7 6.6 %copy-start.6 = (f32[2,8,6]{1,0,2:T(2,128)S(1)}, f32[2,8,6]{1,0,2:T(2,128)}, u32[]{:S(2)}) copy-start(f32[2,8,6]{1,0,2:T(2,128)} %param.12) | copy-start | bytes 1156
  0.7 17.0 %copy-start.2 = (f32[2,8,256]{2,1,0:T(8,128)S(1)}, f32[2,8,256]{2,1,0:T(8,128)}, u32[]{:S(2)}) copy-start(f32[2,8,256]{2,1,0:T(8,128)} %permit.3) | copy-start | bytes 49156
  0.7 17.0 %copy-start.3 = (f32[2,8,128]{2,1,0:T(8,128)S(1)}, f32[2,8,128]{2,1,0:T(8,128)}, u32[]{:S(2)}) copy-start(f32[2,8,128]{2,1,0:T(8,128)} %diag.3) | copy-start | bytes 24580
  0.7 17.0 %copy-start.4 = (s32[2,8]{1,0:T(2,128)S(1)}, s32[2,8]{1,0:T(2,128)}, u32[]{:S(2)}) copy-start(s32[2,8]{1,0:T(2,128)} %counts.5) | copy-start | bytes 196
  1.9 11.0 %collective-permute-start = (bf16[8,256,128]{2,1,0:T(8,128)(2,1)S(1)}, bf16[8,256,128]{2,1,0:T(8,128)(2,1)S(1)}, u32[]{:S(2)}, u32[]{:S(2)}) collective-permute-start(bf16[8,256,128]{2,1,0:T(8,128)(2,1)S(1)} %dynamic-slice_bitcast_fusion.1), channel_id=1, source_target_pairs={{16,32},{32,16},{48,64},{64,48},{80,96},{96,80},{17,33},{33,17},{4... | collective-permute-start | bytes 1572872 | tf_op jit(solution)/shard_map/ppermute | solution.py:32
  7.1 5.8 %collective-permute-start.1 = (bf16[8,256,128]{2,1,0:T(8,128)(2,1)S(1)}, bf16[8,256,128]{2,1,0:T(8,128)(2,1)S(1)}, u32[]{:S(2)}, u32[]{:S(2)}) collective-permute-start(bf16[8,256,128]{2,1,0:T(8,128)(2,1)S(1)} %dynamic-slice_bitcast_fusion), channel_id=1, source_target_pairs={{0,16},{16,0},{32,48},{48,32},{64,80},{80,64},{96,112},{112,96},{1... | collective-permute-start | bytes 1572872 | tf_op jit(solution)/shard_map/ppermute | solution.py:32
  12.9 10.7 %collective-permute-start.2 = (bf16[4,256,128]{2,1,0:T(8,128)(2,1)S(1)}, bf16[4,256,128]{2,1,0:T(8,128)(2,1)S(1)}, u32[]{:S(2)}, u32[]{:S(2)}) collective-permute-start(bf16[4,256,128]{2,1,0:T(8,128)(2,1)S(1)} %pad_maximum_fusion), channel_id=1, source_target_pairs={{1,2},{2,1},{3,4},{4,3},{5,6},{6,5},{7,8},{8,7},{9,10},{10,9},{11,... | collective-permute-start | bytes 786440 | tf_op jit(solution)/shard_map/ppermute | solution.py:32
  17.5 6.1 %copy-start.1 = (bf16[2,8,128,128]{3,2,1,0:T(8,128)(2,1)S(1)}, bf16[2,8,128,128]{3,2,1,0:T(8,128)(2,1)}, u32[]{:S(2)}) copy-start(bf16[2,8,128,128]{3,2,1,0:T(8,128)(2,1)} %vectors.3) | copy-start | bytes 1572868
  17.5 6.1 %collective-permute-start.3 = (bf16[4,256,128]{2,1,0:T(8,128)(2,1)S(1)}, bf16[4,256,128]{2,1,0:T(8,128)(2,1)S(1)}, u32[]{:S(2)}, u32[]{:S(2)}) collective-permute-start(bf16[4,256,128]{2,1,0:T(8,128)(2,1)S(1)} %pad_maximum_fusion.1), channel_id=1, source_target_pairs={{0,1},{1,0},{2,3},{3,2},{4,5},{5,4},{6,7},{7,6},{8,9},{9,8},{10,11... | collective-permute-start | bytes 786440 | tf_op jit(solution)/shard_map/ppermute | solution.py:32
  30.8 15.0 %collective-permute-start.4 = (bf16[4,128,128]{2,1,0:T(8,128)(2,1)S(1)}, bf16[4,128,128]{2,1,0:T(8,128)(2,1)S(1)}, u32[]{:S(2)}, u32[]{:S(2)}) collective-permute-start(bf16[4,128,128]{2,1,0:T(8,128)(2,1)S(1)} %get-tuple-element.20), channel_id=1, source_target_pairs={{1,2},{2,1},{3,4},{4,3},{5,6},{6,5},{7,8},{8,7},{9,10},{10,9},{11,... | collective-permute-start | bytes 393224 | tf_op jit(solution)/shard_map/ppermute | solution.py:32
  33.8 12.0 %collective-permute-start.5 = (bf16[4,128,128]{2,1,0:T(8,128)(2,1)S(1)}, bf16[4,128,128]{2,1,0:T(8,128)(2,1)S(1)}, u32[]{:S(2)}, u32[]{:S(2)}) collective-permute-start(bf16[4,128,128]{2,1,0:T(8,128)(2,1)S(1)} %get-tuple-element.21), channel_id=1, source_target_pairs={{0,1},{1,0},{2,3},{3,2},{4,5},{5,4},{6,7},{7,6},{8,9},{9,8},{10,11... | collective-permute-start | bytes 393224 | tf_op jit(solution)/shard_map/ppermute | solution.py:32
  45.9 11.0 %collective-permute-start.6 = (bf16[8,128,128]{2,1,0:T(8,128)(2,1)S(1)}, bf16[8,128,128]{2,1,0:T(8,128)(2,1)S(1)}, u32[]{:S(2)}, u32[]{:S(2)}) collective-permute-start(bf16[8,128,128]{2,1,0:T(8,128)(2,1)S(1)} %get-tuple-element.22), channel_id=1, source_target_pairs={{16,32},{32,16},{48,64},{64,48},{80,96},{96,80},{17,33},{33,17},{4... | collective-permute-start | bytes 786440 | tf_op jit(solution)/shard_map/ppermute | solution.py:32
  52.8 4.0 %collective-permute-start.7 = (bf16[8,128,128]{2,1,0:T(8,128)(2,1)S(1)}, bf16[8,128,128]{2,1,0:T(8,128)(2,1)S(1)}, u32[]{:S(2)}, u32[]{:S(2)}) collective-permute-start(bf16[8,128,128]{2,1,0:T(8,128)(2,1)S(1)} %get-tuple-element.23), channel_id=1, source_target_pairs={{0,16},{16,0},{32,48},{48,32},{64,80},{80,64},{96,112},{112,96},{1... | collective-permute-start | bytes 786440 | tf_op jit(solution)/shard_map/ppermute | solution.py:32

commit v6 on v5

--- a/solution.py
+++ b/solution.py
@@ -6,7 +6,7 @@
 from jax.sharding import PartitionSpec as P
 
 PANEL = 8
-EARLY = 4
+EARLY = 6
 BF16, F32 = jnp.bfloat16, jnp.float32
 VMEM = pl.BlockSpec(memory_space=pltpu.VMEM)
 SMEM = pl.BlockSpec(memory_space=pltpu.SMEM)
@@ -170,34 +170,79 @@
     return lax.dot_general(factor, vector, (((0,), (0,)), ((), ())), preferred_element_type=F32)
 
 
-def inner_gram(codes, counts, permit, diag, own, odd, even, mats, xs, turned):
+def products(x, y, codes, counts, permit, blocks):
+    slots = range(codes.shape[2])
+    named = [jnp.where(s < counts[x, y], codes[x, y, s], -1) for s in slots]
+    scale = permit[x, pl.ds(y, 1), :]
+    total = None
+    for code, block in blocks:
+        times = F32(0.0)
+        for c in named:
+            times = times + jnp.where(c == code, F32(1.0), F32(0.0))
+        scaled = (scale * block.astype(F32)).astype(BF16)
+        term = times * lax.dot_general(
+            scaled, block, (((1,), (1,)), ((), ())), preferred_element_type=F32
+        )
+        total = term if total is None else total + term
+    return total
+
+
+def own_gram(codes, counts, permit, own, sums, turned):
     bx, by = own.shape[0], own.shape[1]
     inner = by - 2
+    for x in range(bx):
+        for y in range(by):
+            turned[x * by + y] = own[x, y].T
+
+    def body(g, carry):
+        for x in range(bx):
+            for u in range(inner // 2):
+                y = g * (inner // 2) + u + 1
+                blocks = [
+                    (3 * (r - x + 1) + dy, turned[r * by + y + dy - 1])
+                    for r in range(max(x - 1, 0), min(x + 2, bx))
+                    for dy in range(3)
+                ]
+                sums[x * inner + y - 1] = products(x, y, codes, counts, permit, blocks)
+        return carry
+
+    lax.fori_loop(0, 2, body, 0)
+
+
+def inner_gram(codes, counts, permit, diag, odd, even, sums, mats, xs, turned):
+    by = odd.shape[0]
+    inner = by - 2
+    bx = sums.shape[0] // inner
+    order = mats.shape[1]
     px = parity("gx")
     for y in range(by):
-        turned[px * (bx + 1) * by + y] = odd[y].T
-        turned[(1 - px) * (bx + 1) * by + y] = even[y].T
+        turned[px * by + y] = odd[y].T
+        turned[(1 - px) * by + y] = even[y].T
+    row, lane = iotas(order)
+
+    def body(g, carry):
         for x in range(bx):
-            turned[(x + 1) * by + y] = own[x, y].T
-
-    def some(x, g):
-        for u in range(inner // 2):
-            y = g * (inner // 2) + u + 1
-            mats[x * inner + y - 1] = gram_of(
-                x, y, codes, counts, permit, diag,
-                lambda dx, dy: turned[(x + dx) * by + y + dy - 1],
-            )
-
-    def body(h, carry):
-        some(h // 2, h % 2)
+            for u in range(inner // 2):
+                y = g * (inner // 2) + u + 1
+                blocks = []
+                if x == 0:
+                    blocks += [(dy, turned[y + dy - 1]) for dy in range(3)]
+                if x == bx - 1:
+                    blocks += [(6 + dy, turned[by + y + dy - 1]) for dy in range(3)]
+                n = x * inner + y - 1
+                total = sums[n]
+                if blocks:
+                    total = total + products(x, y, codes, counts, permit, blocks)
+                total = (total + total.T) * F32(0.5)
+                mats[n] = total + jnp.where(row == lane, diag[x, pl.ds(y, 1), :], F32(0.0))
         return carry
 
-    lax.fori_loop(0, 2 * bx, body, 0)
-    lower_inverse(mats, xs, bx * inner, mats.shape[1], 0, EARLY)
+    lax.fori_loop(0, 2, body, 0)
+    lower_inverse(mats, xs, bx * inner, order, 0, EARLY)
 
 
 def edge_all(
-    codes, counts, weights, permit, diag, inner_turned, odd, even, vectors,
+    codes, counts, weights, permit, diag, own_turned, far_turned, odd, even, vectors,
     factors, acc, to_odd, to_even, turned, mats, xs,
 ):
     bx, by = vectors.shape[0], vectors.shape[1]
@@ -208,7 +253,10 @@
         turned[row * 6 + 5 * py] = odd[p].T
         turned[row * 6 + 5 * (1 - py)] = even[p].T
         for n, y in enumerate((0, 1, by - 2, by - 1)):
-            turned[p * 6 + 1 + n] = inner_turned[p * by + y]
+            if 0 < p < bx + 1:
+                turned[p * 6 + 1 + n] = own_turned[(p - 1) * by + y]
+            else:
+                turned[p * 6 + 1 + n] = far_turned[p // (bx + 1) * by + y]
     edges = [(x, side) for x in range(bx) for side in range(2)]
     for m, (x, side) in enumerate(edges):
         mats[m] = gram_of(
@@ -323,17 +371,20 @@
     odd_x = swap(pick(coeffs, (bx - 1) * px, 0, False), "gx", 1)
     odd_y = swap(column((by - 1) * py), "gy", 1)
     even_y = swap(column((by - 1) * (1 - py)), "gy", 0)
-    mats, xs, turned = call(
+    sums, own_turned = call(
+        own_gram,
+        (shape((bx * inner, order, order), F32), shape((bx * by, order, coupling), BF16)),
+        [SMEM] * 2 + [VMEM] * 2, [], "own_gram", 12, 4 * 10**9,
+    )(codes, counts, permit, coeffs)
+    mats, xs, far_turned = call(
         inner_gram,
         (
             shape((bx * inner, order, order), F32),
             shape((bx * inner, order, order), F32),
-            shape((rows * by, order, coupling), BF16),
+            shape((2 * by, order, coupling), BF16),
         ),
-        [SMEM] * 2 + [VMEM] * 5,
-        [],
-        "inner_gram", 16, 4 * 10**9,
-    )(codes, counts, permit, diag, coeffs, odd_x, even_x)
+        [SMEM] * 2 + [VMEM] * 5, [], "inner_gram", 16, 6 * 10**9,
+    )(codes, counts, permit, diag, odd_x, even_x, sums)
     edge_factors, edge_acc, to_odd, to_even = call(
         edge_all,
         (
@@ -342,14 +393,14 @@
             shape((rows, order, width), BF16),
             shape((rows, order, width), BF16),
         ),
-        [SMEM] * 3 + [VMEM] * 6,
+        [SMEM] * 3 + [VMEM] * 7,
         [
             pltpu.VMEM((rows * 6, order, coupling), BF16),
             pltpu.VMEM((2 * bx, order, order), F32),
             pltpu.VMEM((2 * bx, order, order), F32),
         ],
         "edge_all", 16, 8 * 10**9,
-    )(codes, counts, weights, permit, diag, turned, odd_y, even_y, vectors)
+    )(codes, counts, weights, permit, diag, own_turned, far_turned, odd_y, even_y, vectors)
     from_odd_y = swap(to_odd, "gy", 1)
     from_even_y = swap(to_even, "gy", 0)
     factor, acc = call(

time: 58.5 us -> 57.1 us (0.976)
  waiting for transfers between devices: 9.41 us -> 7.36 us
  Pallas kernels: 25.5 us -> 27 us
  starting transfers between devices: 19.4 us -> 18.5 us
    pallas_call x0 -> x1, Pallas kernels: none -> 2.79 us  [local(): call(own_gram, (shape((bx * inner, order, order), F32), shape((bx * by, o...]
    ppermute x8, waiting for transfers between devices: 9.41 us -> 7.36 us  [swap(): return lax.ppermute(value, axis, pairs)]
    pallas_call x1, Pallas kernels: 11.4 us -> 10.2 us  [local(): call(inner_all, (shape((bx, by, order, order), BF16), shape((rows * by, o...]
    ppermute x8, starting transfers between devices: 19.4 us -> 18.5 us  [swap(): return lax.ppermute(value, axis, pairs)]
  transfers between devices with their start and end apart: 8 -> 8, of which waited for: 2 -> 3; matrix products, arithmetic and copies ran while one was open for 2% -> 2% of each run, Pallas kernels for 30% -> 33%
where the time goes in v6:
time: 57.1 us; the launch traced here: 56.3 us
  Pallas kernels  27 us (47%)
  starting transfers between devices  18.5 us (32%)
  waiting for transfers between devices  7.36 us (13%)
  local copies, waits for them, and re-layouts  2.5 us (4%)
  between operations  0.89 us (2%)
    ppermute x8, starting transfers between devices, swap(): return lax.ppermute(value, axis, pairs)  18.5 us
    pallas_call x1, Pallas kernels, local(): call(inner_all, (shape((bx, by, order, order), BF16), shape((rows * by, o...  10.2 us
    ppermute x8, waiting for transfers between devices, swap(): return lax.ppermute(value, axis, pairs)  7.36 us
    pallas_call x1, Pallas kernels, local(): call(edge_all, (shape((2 * bx, order, order), BF16), shape((rows * 6, ord...  7.18 us
    pallas_call x1, Pallas kernels, local(): call(inner_gram, (shape((bx * inner, order, order), F32), shape((bx * inn...  5.81 us
    pallas_call x1, Pallas kernels, local(): call(own_gram, (shape((bx * inner, order, order), F32), shape((bx * by, o...  2.79 us
    squeeze x1, local copies, waits for them, and re-layouts, local(): odd_x = swap(pick(coeffs, (bx - 1) * px, 0, False), 'gx', 1)  1.16 us
  transfers between devices with their start and end apart: 8, of which 3 were waited for; matrix products, arithmetic and copies ran while one was open for 2% of the time, Pallas kernels for 33%

profile of v6, /device:TPU:25, one launch (start us, length us, event | category | flops | bytes accessed | tf_op | source)
XLA Modules:
  0.0 56.3 jit_solution(11036672011108154375)
XLA Ops:
  0.6 0.0 copy-start
  0.6 0.0 copy-start.5
  0.7 0.0 copy-start.6
  0.7 0.0 copy-start.4
  0.7 0.0 copy-start.2
  0.7 1.2 %dynamic-slice_bitcast_fusion.1 = bf16[8,256,128]{2,1,0:T(8,128)(2,1)S(1)} fusion(bf16[2,8,256,128]{3,2,1,0:T(8,128)(2,1)} %own.1, s32[]{:T(128)S(6)} %select_n.19), kind=kLoop, calls=%fused_computation.1 | loop fusion | bytes 1048580 | tf_op jit(solution)/shard_map/jit(dynamic_index_in_dim)/squeeze | solution.py:371
  1.9 4.1 %collective-permute-start = (bf16[8,256,128]{2,1,0:T(8,128)(2,1)S(1)}, bf16[8,256,128]{2,1,0:T(8,128)(2,1)S(1)}, u32[]{:S(2)}, u32[]{:S(2)}) collective-permute-start(bf16[8,256,128]{2,1,0:T(8,128)(2,1)S(1)} %dynamic-slice_bitcast_fusion.1), channel_id=1, source_target_pairs={{16,32},{32,16},{48,64},{64,48},{80,96},{96,80},{17,33},{33,17},{4... | collective-permute-start | bytes 1572872 | tf_op jit(solution)/shard_map/ppermute | solution.py:32
  6.0 1.1 %dynamic-slice_bitcast_fusion = bf16[8,256,128]{2,1,0:T(8,128)(2,1)S(1)} fusion(bf16[2,8,256,128]{3,2,1,0:T(8,128)(2,1)} %own.1, s32[]{:T(128)S(6)} %select_n.20), kind=kLoop, calls=%fused_computation | loop fusion | bytes 1048580 | tf_op jit(solution)/shard_map/jit(dynamic_index_in_dim)/squeeze | solution.py:370
  7.1 0.1 collective-permute-start.1
  7.2 0.1 copy.13.codes
  7.3 0.1 copy.14.weights
  7.4 2.8 %own_gram.1 = (f32[12,128,128]{2,1,0:T(8,128)S(1)}, bf16[16,128,256]{2,1,0:T(8,128)(2,1)S(1)}) custom-call(s32[2,8,6]{2,1,0:T(8,128)S(1)} %copy.13.codes, s32[2,8]{1,0:T(2,128)S(1)} %copy-done.4, f32[2,8,256]{2,1,0:T(8,128)S(1)} %copy-done.2, bf16[2,8,256,128]{3,2,1,0:T(8,128)(2,1)S(1)} %copy-done), custom_call_target="tpu_custom_call" | custom-call | flops 4000000000 | bytes 4194304 | tf_op jit(solution)/shard_map/own_gram/pallas_call | solution.py:374
  10.2 2.6 %collective-permute-done.odd = bf16[8,256,128]{2,1,0:T(8,128)(2,1)S(1)} collective-permute-done((bf16[8,256,128]{2,1,0:T(8,128)(2,1)S(1)}, bf16[8,256,128]{2,1,0:T(8,128)(2,1)S(1)}, u32[]{:S(2)}, u32[]{:S(2)}) %collective-permute-start) | collective-permute-done | bytes 524320 | tf_op jit(solution)/shard_map/ppermute | solution.py:32
  12.8 0.0 collective-permute-done.1.even
  12.9 4.6 %collective-permute-start.2 = (bf16[4,256,128]{2,1,0:T(8,128)(2,1)S(1)}, bf16[4,256,128]{2,1,0:T(8,128)(2,1)S(1)}, u32[]{:S(2)}, u32[]{:S(2)}) collective-permute-start(bf16[4,256,128]{2,1,0:T(8,128)(2,1)S(1)} %pad_maximum_fusion), channel_id=1, source_target_pairs={{1,2},{2,1},{3,4},{4,3},{5,6},{6,5},{7,8},{8,7},{9,10},{10,9},{11,... | collective-permute-start | bytes 786440 | tf_op jit(solution)/shard_map/ppermute | solution.py:32
  17.5 0.1 collective-permute-start.3
  17.6 0.0 copy-start.1
  17.6 5.8 %inner_gram.1 = (f32[12,128,128]{2,1,0:T(8,128)S(1)}, f32[12,128,128]{2,1,0:T(8,128)S(1)}, bf16[16,128,256]{2,1,0:T(8,128)(2,1)S(1)}) custom-call(s32[2,8,6]{2,1,0:T(8,128)S(1)} %copy.13.codes, s32[2,8]{1,0:T(2,128)S(1)} %copy-done.4, f32[2,8,256]{2,1,0:T(8,128)S(1)} %copy-done.2, f32[2,8,128]{2,1,0:T(8,128)S(1)} %copy-done.3, ...), custom_call_target="tpu_custom_call" | custom-call | flops 6000000000 | bytes 4194304 | tf_op jit(solution)/shard_map/inner_gram/pallas_call | solution.py:379
  23.5 0.0 collective-permute-done.2.odd
  23.5 0.8 %collective-permute-done.3.even = bf16[4,256,128]{2,1,0:T(8,128)(2,1)S(1)} collective-permute-done((bf16[4,256,128]{2,1,0:T(8,128)(2,1)S(1)}, bf16[4,256,128]{2,1,0:T(8,128)(2,1)S(1)}, u32[]{:S(2)}, u32[]{:S(2)}) %collective-permute-start.3) | collective-permute-done | bytes 262176 | tf_op jit(solution)/shard_map/ppermute | solution.py:32
  24.3 7.2 %edge_all.1 = (bf16[4,128,128]{2,1,0:T(8,128)(2,1)S(1)}, f32[24,128,128]{2,1,0:T(8,128)S(1)}, bf16[4,128,128]{2,1,0:T(8,128)(2,1)S(1)}, bf16[4,128,128]{2,1,0:T(8,128)(2,1)S(1)}) custom-call(s32[2,8,6]{2,1,0:T(8,128)S(1)} %copy.13.codes, s32[2,8]{1,0:T(2,128)S(1)} %copy-done.4, f32[2,8,6]{2,1,0:T(8,128)S(1)} %copy.14.weights, f32[2,8,256]{2,1,0:T(8,128)S(1)} %copy-done.2, ...), custom_call_target="tpu_custom_call" | custom-call | flops 8000000000 | bytes 4194304 | tf_op jit(solution)/shard_map/edge_all/pallas_call | solution.py:388
  31.4 3.5 %collective-permute-start.4 = (bf16[4,128,128]{2,1,0:T(8,128)(2,1)S(1)}, bf16[4,128,128]{2,1,0:T(8,128)(2,1)S(1)}, u32[]{:S(2)}, u32[]{:S(2)}) collective-permute-start(bf16[4,128,128]{2,1,0:T(8,128)(2,1)S(1)} %get-tuple-element.24), channel_id=1, source_target_pairs={{1,2},{2,1},{3,4},{4,3},{5,6},{6,5},{7,8},{8,7},{9,10},{10,9},{11,... | collective-permute-start | bytes 393224 | tf_op jit(solution)/shard_map/ppermute | solution.py:32
  35.0 0.1 collective-permute-start.5
  35.1 10.2 %inner_all.1 = (bf16[2,8,128,128]{3,2,1,0:T(8,128)(2,1)}, f32[32,128,128]{2,1,0:T(8,128)S(1)}) custom-call(s32[2,8,6]{2,1,0:T(8,128)S(1)} %copy.13.codes, s32[2,8]{1,0:T(2,128)S(1)} %copy-done.4, f32[2,8,6]{2,1,0:T(8,128)S(1)} %copy.14.weights, f32[12,128,128]{2,1,0:T(8,128)S(1)} %get-tuple-element.16.mats_in, f32[12,128,128]{2,1,0:T(8,128)S(1)} %get-tuple-element.17.xs_in, ...), custom_call_target="tpu_custom_call" | custom-call | flops 12000000000 | bytes 4194304 | tf_op jit(solution)/shard_map/inner_all/pallas_call | solution.py:406
  45.3 0.0 collective-permute-done.4.odd.odd_y
  45.3 0.0 collective-permute-done.5.even.even_y
  45.3 0.1 close_halo.1
  45.4 6.0 %collective-permute-start.6 = (bf16[8,128,128]{2,1,0:T(8,128)(2,1)S(1)}, bf16[8,128,128]{2,1,0:T(8,128)(2,1)S(1)}, u32[]{:S(2)}, u32[]{:S(2)}) collective-permute-start(bf16[8,128,128]{2,1,0:T(8,128)(2,1)S(1)} %get-tuple-element.26), channel_id=1, source_target_pairs={{16,32},{32,16},{48,64},{64,48},{80,96},{96,80},{17,33},{33,17},{4... | collective-permute-start | bytes 786440 | tf_op jit(solution)/shard_map/ppermute | solution.py:32
  51.4 0.1 collective-permute-start.7
  51.5 3.9 %collective-permute-done.6.odd_x = bf16[8,128,128]{2,1,0:T(8,128)(2,1)S(1)} collective-permute-done((bf16[8,128,128]{2,1,0:T(8,128)(2,1)S(1)}, bf16[8,128,128]{2,1,0:T(8,128)(2,1)S(1)}, u32[]{:S(2)}, u32[]{:S(2)}) %collective-permute-start.6) | collective-permute-done | bytes 262176 | tf_op jit(solution)/shard_map/ppermute | solution.py:32
  55.4 0.0 collective-permute-done.7.even_x
  55.4 0.9 %collect.1 = bf16[2,8,128,128]{3,2,1,0:T(8,128)(2,1)} custom-call(f32[32,128,128]{2,1,0:T(8,128)S(1)} %get-tuple-element.23.acc, bf16[8,128,128]{2,1,0:T(8,128)(2,1)S(1)} %collective-permute-done.6.odd_x, bf16[8,128,128]{2,1,0:T(8,128)(2,1)S(1)} %collective-permute-done.7.even_x, bf16[4,128,128]{2,1,0:T(8,128)(2,1)S(1)} %collective-permute-done.4.odd.odd_y, ...), custom_call_target="tpu_custom_call" | custom-call | flops 100000000 | bytes 4194304 | tf_op jit(solution)/shard_map/collect/pallas_call | solution.py:426
  (13 shorter events, 0.1 us)
Async XLA Ops:
  0.6 6.5 %copy-start = (bf16[2,8,256,128]{3,2,1,0:T(8,128)(2,1)S(1)}, bf16[2,8,256,128]{3,2,1,0:T(8,128)(2,1)}, u32[]{:S(2)}) copy-start(bf16[2,8,256,128]{3,2,1,0:T(8,128)(2,1)} %own.1) | copy-start | bytes 3145732
  0.6 6.6 %copy-start.5 = (s32[2,8,6]{1,0,2:T(2,128)S(1)}, s32[2,8,6]{1,0,2:T(2,128)}, u32[]{:S(2)}) copy-start(s32[2,8,6]{1,0,2:T(2,128)} %param.10) | copy-start | bytes 1156
  0.7 6.7 %copy-start.6 = (f32[2,8,6]{1,0,2:T(2,128)S(1)}, f32[2,8,6]{1,0,2:T(2,128)}, u32[]{:S(2)}) copy-start(f32[2,8,6]{1,0,2:T(2,128)} %param.12) | copy-start | bytes 1156
  0.7 6.7 %copy-start.4 = (s32[2,8]{1,0:T(2,128)S(1)}, s32[2,8]{1,0:T(2,128)}, u32[]{:S(2)}) copy-start(s32[2,8]{1,0:T(2,128)} %counts.7) | copy-start | bytes 196
  0.7 6.7 %copy-start.2 = (f32[2,8,256]{2,1,0:T(8,128)S(1)}, f32[2,8,256]{2,1,0:T(8,128)}, u32[]{:S(2)}) copy-start(f32[2,8,256]{2,1,0:T(8,128)} %permit.5) | copy-start | bytes 49156
  1.9 11.0 %collective-permute-start = (bf16[8,256,128]{2,1,0:T(8,128)(2,1)S(1)}, bf16[8,256,128]{2,1,0:T(8,128)(2,1)S(1)}, u32[]{:S(2)}, u32[]{:S(2)}) collective-permute-start(bf16[8,256,128]{2,1,0:T(8,128)(2,1)S(1)} %dynamic-slice_bitcast_fusion.1), channel_id=1, source_target_pairs={{16,32},{32,16},{48,64},{64,48},{80,96},{96,80},{17,33},{33,17},{4... | collective-permute-start | bytes 1572872 | tf_op jit(solution)/shard_map/ppermute | solution.py:32
  7.1 5.8 %collective-permute-start.1 = (bf16[8,256,128]{2,1,0:T(8,128)(2,1)S(1)}, bf16[8,256,128]{2,1,0:T(8,128)(2,1)S(1)}, u32[]{:S(2)}, u32[]{:S(2)}) collective-permute-start(bf16[8,256,128]{2,1,0:T(8,128)(2,1)S(1)} %dynamic-slice_bitcast_fusion), channel_id=1, source_target_pairs={{0,16},{16,0},{32,48},{48,32},{64,80},{80,64},{96,112},{112,96},{1... | collective-permute-start | bytes 1572872 | tf_op jit(solution)/shard_map/ppermute | solution.py:32
  7.4 10.2 %copy-start.3 = (f32[2,8,128]{2,1,0:T(8,128)S(1)}, f32[2,8,128]{2,1,0:T(8,128)}, u32[]{:S(2)}) copy-start(f32[2,8,128]{2,1,0:T(8,128)} %diag.3) | copy-start | bytes 24580
  12.9 10.6 %collective-permute-start.2 = (bf16[4,256,128]{2,1,0:T(8,128)(2,1)S(1)}, bf16[4,256,128]{2,1,0:T(8,128)(2,1)S(1)}, u32[]{:S(2)}, u32[]{:S(2)}) collective-permute-start(bf16[4,256,128]{2,1,0:T(8,128)(2,1)S(1)} %pad_maximum_fusion), channel_id=1, source_target_pairs={{1,2},{2,1},{3,4},{4,3},{5,6},{6,5},{7,8},{8,7},{9,10},{10,9},{11,... | collective-permute-start | bytes 786440 | tf_op jit(solution)/shard_map/ppermute | solution.py:32
  17.5 6.7 %collective-permute-start.3 = (bf16[4,256,128]{2,1,0:T(8,128)(2,1)S(1)}, bf16[4,256,128]{2,1,0:T(8,128)(2,1)S(1)}, u32[]{:S(2)}, u32[]{:S(2)}) collective-permute-start(bf16[4,256,128]{2,1,0:T(8,128)(2,1)S(1)} %pad_maximum_fusion.1), channel_id=1, source_target_pairs={{0,1},{1,0},{2,3},{3,2},{4,5},{5,4},{6,7},{7,6},{8,9},{9,8},{10,11... | collective-permute-start | bytes 786440 | tf_op jit(solution)/shard_map/ppermute | solution.py:32
  17.6 6.6 %copy-start.1 = (bf16[2,8,128,128]{3,2,1,0:T(8,128)(2,1)S(1)}, bf16[2,8,128,128]{3,2,1,0:T(8,128)(2,1)}, u32[]{:S(2)}) copy-start(bf16[2,8,128,128]{3,2,1,0:T(8,128)(2,1)} %vectors.3) | copy-start | bytes 1572868
  31.4 13.9 %collective-permute-start.4 = (bf16[4,128,128]{2,1,0:T(8,128)(2,1)S(1)}, bf16[4,128,128]{2,1,0:T(8,128)(2,1)S(1)}, u32[]{:S(2)}, u32[]{:S(2)}) collective-permute-start(bf16[4,128,128]{2,1,0:T(8,128)(2,1)S(1)} %get-tuple-element.24), channel_id=1, source_target_pairs={{1,2},{2,1},{3,4},{4,3},{5,6},{6,5},{7,8},{8,7},{9,10},{10,9},{11,... | collective-permute-start | bytes 393224 | tf_op jit(solution)/shard_map/ppermute | solution.py:32
  35.0 10.3 %collective-permute-start.5 = (bf16[4,128,128]{2,1,0:T(8,128)(2,1)S(1)}, bf16[4,128,128]{2,1,0:T(8,128)(2,1)S(1)}, u32[]{:S(2)}, u32[]{:S(2)}) collective-permute-start(bf16[4,128,128]{2,1,0:T(8,128)(2,1)S(1)} %get-tuple-element.25), channel_id=1, source_target_pairs={{0,1},{1,0},{2,3},{3,2},{4,5},{5,4},{6,7},{7,6},{8,9},{9,8},{10,11... | collective-permute-start | bytes 393224 | tf_op jit(solution)/shard_map/ppermute | solution.py:32
  45.4 10.0 %collective-permute-start.6 = (bf16[8,128,128]{2,1,0:T(8,128)(2,1)S(1)}, bf16[8,128,128]{2,1,0:T(8,128)(2,1)S(1)}, u32[]{:S(2)}, u32[]{:S(2)}) collective-permute-start(bf16[8,128,128]{2,1,0:T(8,128)(2,1)S(1)} %get-tuple-element.26), channel_id=1, source_target_pairs={{16,32},{32,16},{48,64},{64,48},{80,96},{96,80},{17,33},{33,17},{4... | collective-permute-start | bytes 786440 | tf_op jit(solution)/shard_map/ppermute | solution.py:32
  51.4 4.0 %collective-permute-start.7 = (bf16[8,128,128]{2,1,0:T(8,128)(2,1)S(1)}, bf16[8,128,128]{2,1,0:T(8,128)(2,1)S(1)}, u32[]{:S(2)}, u32[]{:S(2)}) collective-permute-start(bf16[8,128,128]{2,1,0:T(8,128)(2,1)S(1)} %get-tuple-element.27), channel_id=1, source_target_pairs={{0,16},{16,0},{32,48},{48,32},{64,80},{80,64},{96,112},{112,96},{1... | collective-permute-start | bytes 786440 | tf_op jit(solution)/shard_map/ppermute | solution.py:32

commit v7 on v6

--- a/solution.py
+++ b/solution.py
@@ -6,7 +6,7 @@
 from jax.sharding import PartitionSpec as P
 
 PANEL = 8
-EARLY = 6
+EARLY = 8
 BF16, F32 = jnp.bfloat16, jnp.float32
 VMEM = pl.BlockSpec(memory_space=pltpu.VMEM)
 SMEM = pl.BlockSpec(memory_space=pltpu.SMEM)
@@ -308,16 +308,15 @@
         factor[x, by - 1] = edge_factors[2 * x + 1]
     row, lane = iotas(order)
 
-    def body(h, carry):
-        x = h // (inner // 2)
+    def body(x, carry):
         images = []
-        for u in range(2):
-            y = (h % (inner // 2)) * 2 + u + 1
+        for u in range(inner):
+            y = u + 1
             f = jnp.where(lane <= row, xs[x * inner + y - 1], F32(0.0)).astype(BF16)
             factor[x, y] = f
             images.append(image_of(f, vectors[x, y]))
-        for u in range(2):
-            y = (h % (inner // 2)) * 2 + u + 1
+        for u in range(inner):
+            y = u + 1
 
             def add(s, c):
                 code = codes[x, y, s]
@@ -328,7 +327,7 @@
             lax.fori_loop(0, counts[x, y], add, 0)
         return carry
 
-    lax.fori_loop(0, bx * inner // 2, body, 0)
+    lax.fori_loop(0, bx, body, 0)
 
 
 def close_halo(acc, odd, even, to_odd, to_even):

time: 57.1 us -> 55.3 us (0.968)
  Pallas kernels: 27 us -> 26 us
  waiting for transfers between devices: 7.36 us -> 6.58 us
    pallas_call x1, Pallas kernels: 10.2 us -> 8 us  [local(): call(inner_all, (shape((bx, by, order, order), BF16), shape((rows * by, o...]
    pallas_call x1, Pallas kernels: 5.81 us -> 7.01 us  [local(): call(inner_gram, (shape((bx * inner, order, order), F32), shape((bx * inn...]
    ppermute x8, waiting for transfers between devices: 7.36 us -> 6.58 us  [swap(): return lax.ppermute(value, axis, pairs)]
  transfers between devices with their start and end apart: 8 -> 8, of which waited for: 3 -> 2; matrix products, arithmetic and copies ran while one was open for 2% -> 2% of each run, Pallas kernels for 33% -> 33%
where the time goes in v7:
time: 55.3 us; the launch traced here: 54.6 us
  Pallas kernels  26 us (47%)
  starting transfers between devices  18.5 us (33%)
  waiting for transfers between devices  6.58 us (12%)
  local copies, waits for them, and re-layouts  2.5 us (5%)
  between operations  0.89 us (2%)
    ppermute x8, starting transfers between devices, swap(): return lax.ppermute(value, axis, pairs)  18.5 us
    pallas_call x1, Pallas kernels, local(): call(inner_all, (shape((bx, by, order, order), BF16), shape((rows * by, o...  8 us
    pallas_call x1, Pallas kernels, local(): call(edge_all, (shape((2 * bx, order, order), BF16), shape((rows * 6, ord...  7.2 us
    pallas_call x1, Pallas kernels, local(): call(inner_gram, (shape((bx * inner, order, order), F32), shape((bx * inn...  7.01 us
    ppermute x8, waiting for transfers between devices, swap(): return lax.ppermute(value, axis, pairs)  6.58 us
    pallas_call x1, Pallas kernels, local(): call(own_gram, (shape((bx * inner, order, order), F32), shape((bx * by, o...  2.79 us
    squeeze x1, local copies, waits for them, and re-layouts, local(): odd_x = swap(pick(coeffs, (bx - 1) * px, 0, False), 'gx', 1)  1.16 us
  transfers between devices with their start and end apart: 8, of which 2 were waited for; matrix products, arithmetic and copies ran while one was open for 2% of the time, Pallas kernels for 33%

profile of v7, /device:TPU:25, one launch (start us, length us, event | category | flops | bytes accessed | tf_op | source)
XLA Modules:
  0.0 54.6 jit_solution(7180831758967674298)
XLA Ops:
  0.6 0.0 copy-start
  0.6 0.0 copy-start.5
  0.7 0.0 copy-start.6
  0.7 0.0 copy-start.4
  0.7 0.0 copy-start.2
  0.7 1.2 %dynamic-slice_bitcast_fusion.1 = bf16[8,256,128]{2,1,0:T(8,128)(2,1)S(1)} fusion(bf16[2,8,256,128]{3,2,1,0:T(8,128)(2,1)} %own.1, s32[]{:T(128)S(6)} %select_n.19), kind=kLoop, calls=%fused_computation.1 | loop fusion | bytes 1048580 | tf_op jit(solution)/shard_map/jit(dynamic_index_in_dim)/squeeze | solution.py:370
  1.9 4.1 %collective-permute-start = (bf16[8,256,128]{2,1,0:T(8,128)(2,1)S(1)}, bf16[8,256,128]{2,1,0:T(8,128)(2,1)S(1)}, u32[]{:S(2)}, u32[]{:S(2)}) collective-permute-start(bf16[8,256,128]{2,1,0:T(8,128)(2,1)S(1)} %dynamic-slice_bitcast_fusion.1), channel_id=1, source_target_pairs={{16,32},{32,16},{48,64},{64,48},{80,96},{96,80},{17,33},{33,17},{4... | collective-permute-start | bytes 1572872 | tf_op jit(solution)/shard_map/ppermute | solution.py:32
  6.0 1.1 %dynamic-slice_bitcast_fusion = bf16[8,256,128]{2,1,0:T(8,128)(2,1)S(1)} fusion(bf16[2,8,256,128]{3,2,1,0:T(8,128)(2,1)} %own.1, s32[]{:T(128)S(6)} %select_n.20), kind=kLoop, calls=%fused_computation | loop fusion | bytes 1048580 | tf_op jit(solution)/shard_map/jit(dynamic_index_in_dim)/squeeze | solution.py:369
  7.1 0.1 collective-permute-start.1
  7.2 0.1 copy.13.codes
  7.3 0.1 copy.14.weights
  7.4 2.8 %own_gram.1 = (f32[12,128,128]{2,1,0:T(8,128)S(1)}, bf16[16,128,256]{2,1,0:T(8,128)(2,1)S(1)}) custom-call(s32[2,8,6]{2,1,0:T(8,128)S(1)} %copy.13.codes, s32[2,8]{1,0:T(2,128)S(1)} %copy-done.4, f32[2,8,256]{2,1,0:T(8,128)S(1)} %copy-done.2, bf16[2,8,256,128]{3,2,1,0:T(8,128)(2,1)S(1)} %copy-done), custom_call_target="tpu_custom_call" | custom-call | flops 4000000000 | bytes 4194304 | tf_op jit(solution)/shard_map/own_gram/pallas_call | solution.py:373
  10.2 2.6 %collective-permute-done.odd = bf16[8,256,128]{2,1,0:T(8,128)(2,1)S(1)} collective-permute-done((bf16[8,256,128]{2,1,0:T(8,128)(2,1)S(1)}, bf16[8,256,128]{2,1,0:T(8,128)(2,1)S(1)}, u32[]{:S(2)}, u32[]{:S(2)}) %collective-permute-start) | collective-permute-done | bytes 524320 | tf_op jit(solution)/shard_map/ppermute | solution.py:32
  12.8 0.0 collective-permute-done.1.even
  12.9 4.6 %collective-permute-start.2 = (bf16[4,256,128]{2,1,0:T(8,128)(2,1)S(1)}, bf16[4,256,128]{2,1,0:T(8,128)(2,1)S(1)}, u32[]{:S(2)}, u32[]{:S(2)}) collective-permute-start(bf16[4,256,128]{2,1,0:T(8,128)(2,1)S(1)} %pad_maximum_fusion), channel_id=1, source_target_pairs={{1,2},{2,1},{3,4},{4,3},{5,6},{6,5},{7,8},{8,7},{9,10},{10,9},{11,... | collective-permute-start | bytes 786440 | tf_op jit(solution)/shard_map/ppermute | solution.py:32
  17.5 0.1 collective-permute-start.3
  17.6 0.0 copy-start.1
  17.6 7.0 %inner_gram.1 = (f32[12,128,128]{2,1,0:T(8,128)S(1)}, f32[12,128,128]{2,1,0:T(8,128)S(1)}, bf16[16,128,256]{2,1,0:T(8,128)(2,1)S(1)}) custom-call(s32[2,8,6]{2,1,0:T(8,128)S(1)} %copy.13.codes, s32[2,8]{1,0:T(2,128)S(1)} %copy-done.4, f32[2,8,256]{2,1,0:T(8,128)S(1)} %copy-done.2, f32[2,8,128]{2,1,0:T(8,128)S(1)} %copy-done.3, ...), custom_call_target="tpu_custom_call" | custom-call | flops 6000000000 | bytes 4194304 | tf_op jit(solution)/shard_map/inner_gram/pallas_call | solution.py:378
  24.7 0.0 collective-permute-done.2.odd
  24.7 0.0 collective-permute-done.3.even
  24.7 7.2 %edge_all.1 = (bf16[4,128,128]{2,1,0:T(8,128)(2,1)S(1)}, f32[24,128,128]{2,1,0:T(8,128)S(1)}, bf16[4,128,128]{2,1,0:T(8,128)(2,1)S(1)}, bf16[4,128,128]{2,1,0:T(8,128)(2,1)S(1)}) custom-call(s32[2,8,6]{2,1,0:T(8,128)S(1)} %copy.13.codes, s32[2,8]{1,0:T(2,128)S(1)} %copy-done.4, f32[2,8,6]{2,1,0:T(8,128)S(1)} %copy.14.weights, f32[2,8,256]{2,1,0:T(8,128)S(1)} %copy-done.2, ...), custom_call_target="tpu_custom_call" | custom-call | flops 8000000000 | bytes 4194304 | tf_op jit(solution)/shard_map/edge_all/pallas_call | solution.py:387
  31.9 3.1 %collective-permute-start.4 = (bf16[4,128,128]{2,1,0:T(8,128)(2,1)S(1)}, bf16[4,128,128]{2,1,0:T(8,128)(2,1)S(1)}, u32[]{:S(2)}, u32[]{:S(2)}) collective-permute-start(bf16[4,128,128]{2,1,0:T(8,128)(2,1)S(1)} %get-tuple-element.24), channel_id=1, source_target_pairs={{1,2},{2,1},{3,4},{4,3},{5,6},{6,5},{7,8},{8,7},{9,10},{10,9},{11,... | collective-permute-start | bytes 393224 | tf_op jit(solution)/shard_map/ppermute | solution.py:32
  35.0 0.3 collective-permute-start.5
  35.3 8.0 %inner_all.1 = (bf16[2,8,128,128]{3,2,1,0:T(8,128)(2,1)}, f32[32,128,128]{2,1,0:T(8,128)S(1)}) custom-call(s32[2,8,6]{2,1,0:T(8,128)S(1)} %copy.13.codes, s32[2,8]{1,0:T(2,128)S(1)} %copy-done.4, f32[2,8,6]{2,1,0:T(8,128)S(1)} %copy.14.weights, f32[12,128,128]{2,1,0:T(8,128)S(1)} %get-tuple-element.16.mats_in, f32[12,128,128]{2,1,0:T(8,128)S(1)} %get-tuple-element.17.xs_in, ...), custom_call_target="tpu_custom_call" | custom-call | flops 12000000000 | bytes 4194304 | tf_op jit(solution)/shard_map/inner_all/pallas_call | solution.py:405
  43.3 0.0 collective-permute-done.4.odd.odd_y
  43.3 0.0 collective-permute-done.5.even.even_y
  43.3 0.1 close_halo.1
  43.4 6.2 %collective-permute-start.6 = (bf16[8,128,128]{2,1,0:T(8,128)(2,1)S(1)}, bf16[8,128,128]{2,1,0:T(8,128)(2,1)S(1)}, u32[]{:S(2)}, u32[]{:S(2)}) collective-permute-start(bf16[8,128,128]{2,1,0:T(8,128)(2,1)S(1)} %get-tuple-element.26), channel_id=1, source_target_pairs={{16,32},{32,16},{48,64},{64,48},{80,96},{96,80},{17,33},{33,17},{4... | collective-permute-start | bytes 786440 | tf_op jit(solution)/shard_map/ppermute | solution.py:32
  49.6 0.1 collective-permute-start.7
  49.7 3.9 %collective-permute-done.6.odd_x = bf16[8,128,128]{2,1,0:T(8,128)(2,1)S(1)} collective-permute-done((bf16[8,128,128]{2,1,0:T(8,128)(2,1)S(1)}, bf16[8,128,128]{2,1,0:T(8,128)(2,1)S(1)}, u32[]{:S(2)}, u32[]{:S(2)}) %collective-permute-start.6) | collective-permute-done | bytes 262176 | tf_op jit(solution)/shard_map/ppermute | solution.py:32
  53.6 0.0 collective-permute-done.7.even_x
  53.6 0.9 %collect.1 = bf16[2,8,128,128]{3,2,1,0:T(8,128)(2,1)} custom-call(f32[32,128,128]{2,1,0:T(8,128)S(1)} %get-tuple-element.23.acc, bf16[8,128,128]{2,1,0:T(8,128)(2,1)S(1)} %collective-permute-done.6.odd_x, bf16[8,128,128]{2,1,0:T(8,128)(2,1)S(1)} %collective-permute-done.7.even_x, bf16[4,128,128]{2,1,0:T(8,128)(2,1)S(1)} %collective-permute-done.4.odd.odd_y, ...), custom_call_target="tpu_custom_call" | custom-call | flops 100000000 | bytes 4194304 | tf_op jit(solution)/shard_map/collect/pallas_call | solution.py:425
  (13 shorter events, 0.1 us)
Async XLA Ops:
  0.6 6.5 %copy-start = (bf16[2,8,256,128]{3,2,1,0:T(8,128)(2,1)S(1)}, bf16[2,8,256,128]{3,2,1,0:T(8,128)(2,1)}, u32[]{:S(2)}) copy-start(bf16[2,8,256,128]{3,2,1,0:T(8,128)(2,1)} %own.1) | copy-start | bytes 3145732
  0.6 6.6 %copy-start.5 = (s32[2,8,6]{1,0,2:T(2,128)S(1)}, s32[2,8,6]{1,0,2:T(2,128)}, u32[]{:S(2)}) copy-start(s32[2,8,6]{1,0,2:T(2,128)} %param.10) | copy-start | bytes 1156
  0.7 6.7 %copy-start.6 = (f32[2,8,6]{1,0,2:T(2,128)S(1)}, f32[2,8,6]{1,0,2:T(2,128)}, u32[]{:S(2)}) copy-start(f32[2,8,6]{1,0,2:T(2,128)} %param.12) | copy-start | bytes 1156
  0.7 6.7 %copy-start.4 = (s32[2,8]{1,0:T(2,128)S(1)}, s32[2,8]{1,0:T(2,128)}, u32[]{:S(2)}) copy-start(s32[2,8]{1,0:T(2,128)} %counts.7) | copy-start | bytes 196
  0.7 6.7 %copy-start.2 = (f32[2,8,256]{2,1,0:T(8,128)S(1)}, f32[2,8,256]{2,1,0:T(8,128)}, u32[]{:S(2)}) copy-start(f32[2,8,256]{2,1,0:T(8,128)} %permit.5) | copy-start | bytes 49156
  1.9 11.0 %collective-permute-start = (bf16[8,256,128]{2,1,0:T(8,128)(2,1)S(1)}, bf16[8,256,128]{2,1,0:T(8,128)(2,1)S(1)}, u32[]{:S(2)}, u32[]{:S(2)}) collective-permute-start(bf16[8,256,128]{2,1,0:T(8,128)(2,1)S(1)} %dynamic-slice_bitcast_fusion.1), channel_id=1, source_target_pairs={{16,32},{32,16},{48,64},{64,48},{80,96},{96,80},{17,33},{33,17},{4... | collective-permute-start | bytes 1572872 | tf_op jit(solution)/shard_map/ppermute | solution.py:32
  7.1 5.8 %collective-permute-start.1 = (bf16[8,256,128]{2,1,0:T(8,128)(2,1)S(1)}, bf16[8,256,128]{2,1,0:T(8,128)(2,1)S(1)}, u32[]{:S(2)}, u32[]{:S(2)}) collective-permute-start(bf16[8,256,128]{2,1,0:T(8,128)(2,1)S(1)} %dynamic-slice_bitcast_fusion), channel_id=1, source_target_pairs={{0,16},{16,0},{32,48},{48,32},{64,80},{80,64},{96,112},{112,96},{1... | collective-permute-start | bytes 1572872 | tf_op jit(solution)/shard_map/ppermute | solution.py:32
  7.4 10.2 %copy-start.3 = (f32[2,8,128]{2,1,0:T(8,128)S(1)}, f32[2,8,128]{2,1,0:T(8,128)}, u32[]{:S(2)}) copy-start(f32[2,8,128]{2,1,0:T(8,128)} %diag.3) | copy-start | bytes 24580
  12.9 11.8 %collective-permute-start.2 = (bf16[4,256,128]{2,1,0:T(8,128)(2,1)S(1)}, bf16[4,256,128]{2,1,0:T(8,128)(2,1)S(1)}, u32[]{:S(2)}, u32[]{:S(2)}) collective-permute-start(bf16[4,256,128]{2,1,0:T(8,128)(2,1)S(1)} %pad_maximum_fusion), channel_id=1, source_target_pairs={{1,2},{2,1},{3,4},{4,3},{5,6},{6,5},{7,8},{8,7},{9,10},{10,9},{11,... | collective-permute-start | bytes 786440 | tf_op jit(solution)/shard_map/ppermute | solution.py:32
  17.5 7.1 %collective-permute-start.3 = (bf16[4,256,128]{2,1,0:T(8,128)(2,1)S(1)}, bf16[4,256,128]{2,1,0:T(8,128)(2,1)S(1)}, u32[]{:S(2)}, u32[]{:S(2)}) collective-permute-start(bf16[4,256,128]{2,1,0:T(8,128)(2,1)S(1)} %pad_maximum_fusion.1), channel_id=1, source_target_pairs={{0,1},{1,0},{2,3},{3,2},{4,5},{5,4},{6,7},{7,6},{8,9},{9,8},{10,11... | collective-permute-start | bytes 786440 | tf_op jit(solution)/shard_map/ppermute | solution.py:32
  17.6 7.1 %copy-start.1 = (bf16[2,8,128,128]{3,2,1,0:T(8,128)(2,1)S(1)}, bf16[2,8,128,128]{3,2,1,0:T(8,128)(2,1)}, u32[]{:S(2)}) copy-start(bf16[2,8,128,128]{3,2,1,0:T(8,128)(2,1)} %vectors.3) | copy-start | bytes 1572868
  31.9 11.4 %collective-permute-start.4 = (bf16[4,128,128]{2,1,0:T(8,128)(2,1)S(1)}, bf16[4,128,128]{2,1,0:T(8,128)(2,1)S(1)}, u32[]{:S(2)}, u32[]{:S(2)}) collective-permute-start(bf16[4,128,128]{2,1,0:T(8,128)(2,1)S(1)} %get-tuple-element.24), channel_id=1, source_target_pairs={{1,2},{2,1},{3,4},{4,3},{5,6},{6,5},{7,8},{8,7},{9,10},{10,9},{11,... | collective-permute-start | bytes 393224 | tf_op jit(solution)/shard_map/ppermute | solution.py:32
  35.0 8.3 %collective-permute-start.5 = (bf16[4,128,128]{2,1,0:T(8,128)(2,1)S(1)}, bf16[4,128,128]{2,1,0:T(8,128)(2,1)S(1)}, u32[]{:S(2)}, u32[]{:S(2)}) collective-permute-start(bf16[4,128,128]{2,1,0:T(8,128)(2,1)S(1)} %get-tuple-element.25), channel_id=1, source_target_pairs={{0,1},{1,0},{2,3},{3,2},{4,5},{5,4},{6,7},{7,6},{8,9},{9,8},{10,11... | collective-permute-start | bytes 393224 | tf_op jit(solution)/shard_map/ppermute | solution.py:32
  43.4 10.2 %collective-permute-start.6 = (bf16[8,128,128]{2,1,0:T(8,128)(2,1)S(1)}, bf16[8,128,128]{2,1,0:T(8,128)(2,1)S(1)}, u32[]{:S(2)}, u32[]{:S(2)}) collective-permute-start(bf16[8,128,128]{2,1,0:T(8,128)(2,1)S(1)} %get-tuple-element.26), channel_id=1, source_target_pairs={{16,32},{32,16},{48,64},{64,48},{80,96},{96,80},{17,33},{33,17},{4... | collective-permute-start | bytes 786440 | tf_op jit(solution)/shard_map/ppermute | solution.py:32
  49.6 4.0 %collective-permute-start.7 = (bf16[8,128,128]{2,1,0:T(8,128)(2,1)S(1)}, bf16[8,128,128]{2,1,0:T(8,128)(2,1)S(1)}, u32[]{:S(2)}, u32[]{:S(2)}) collective-permute-start(bf16[8,128,128]{2,1,0:T(8,128)(2,1)S(1)} %get-tuple-element.27), channel_id=1, source_target_pairs={{0,16},{16,0},{32,48},{48,32},{64,80},{80,64},{96,112},{112,96},{1... | collective-permute-start | bytes 786440 | tf_op jit(solution)/shard_map/ppermute | solution.py:32
